TPU v7x, 32 devices: a whole 2x2x4 slice. The times are simulated.
32 devices in a mesh: groups: 2 (over y), acq: 8 (over z, x), rng: 2 (over core).
Axes of the slice: x: 2, y: 2, z: 4, core: 2. Of those that a mesh axis runs over, the one named last changes fastest.
Arguments:
- slc: bfloat16 [2, 16, 64, 2048], P(None, ('groups', 'acq'), None, 'rng'), parts along dimension 1, may hold values from -32 to 32, as said below
- map_cell: int32 [16, 256], P('groups', 'rng'), parts along dimension 0, may hold values from 0 to 16383, as said below
Outputs:
- geocoded: float32 [3, 8, 2, 16384], P(None, 'groups', None, ('acq', 'rng')), parts along dimension 1
There are 2 independent parts, one for each index of `groups`. A program takes and returns all parts, laid end to end along the dimension named above; each array names one. Nothing has to cross between parts.
Inputs may be any that keep to these rules, and one draw needn't show every extreme that they name: `slc`: samples of an acquisition share a scene phase with the others, up to a per-sample phase drift. `map_cell`: A map cell is row * 128 + column on a grid of 128 rows; several radar cells may share one, and some map cells receive none. Nothing more is promised about where a radar cell lands.
All inputs are finite; a program needn't handle non-finite values.
Results may differ from a plain program's by a relative error of at most 0.0003.
Values may be sent and summed in bfloat16 or wider, within the bound.
No kernel may reach another device: no remote copies, remote signals or barrier semaphores. Data moves between devices by JAX's collectives and lax.ppermute only.
A program may use at most 128 MiB of HBM per device.

v0:
```python
import jax
import jax.numpy as jnp
from jax import lax
from jax.sharding import PartitionSpec as P

LOOK_A = 8
LOOK_R = 8
HALF_W = 4
ROUNDS = 3
MAPC = 16384


def swapped(value, axis, stride):
    mask = 2**stride
    pairs = [(source, source ^ mask) for source in range(lax.axis_size(axis))]
    return lax.ppermute(value, axis, pairs)


def padded_2(shard, sides, width):
    for axis, dim in sides:
        size, length = (lax.axis_size(axis), shard.shape[dim])
        up = [(i, (i + 1) % size) for i in range(size - 1)]
        down = [(j, i) for i, j in up]
        last = lax.slice_in_dim(shard, length - width, length, axis=dim)
        leading = lax.slice_in_dim(shard, 0, width, axis=dim)
        before = lax.ppermute(last, axis, up)
        after = lax.ppermute(leading, axis, down)
        shard = jnp.concatenate([before, shard, after], axis=dim)
    return shard


def look_sum(values_in):
    line_count, col_count = values_in.shape
    return values_in.reshape(line_count // LOOK_A, LOOK_A, col_count // LOOK_R, LOOK_R).sum(
        axis=(1, 3)
    )


def per_device(slc, map_cell):
    acq_count = lax.axis_size("acq")
    rng_count = lax.axis_size("rng")
    acq_rank = lax.axis_index("acq")
    own_block = slc[:, 0]
    line_total = own_block.shape[1]
    half_lines = line_total // 2
    half_looks = half_lines // LOOK_A
    owner_cells = MAPC // acq_count
    piece = owner_cells // rng_count
    map_bins = []
    for round_index in range(ROUNDS):
        upper_flag = acq_rank // 2**round_index % 2
        row_start = upper_flag * half_lines
        mine_rows = lax.dynamic_slice_in_dim(own_block, row_start, half_lines, 1)
        partner_all = swapped(own_block, "acq", round_index)
        their_rows = lax.dynamic_slice_in_dim(partner_all, row_start, half_lines, 1)
        mine_f = mine_rows.astype(jnp.float32)
        their_f = their_rows.astype(jnp.float32)
        sign_flip = (1 - 2 * upper_flag).astype(jnp.float32)
        real_part = mine_f[0] * their_f[0] + mine_f[1] * their_f[1]
        imag_part = (mine_f[1] * their_f[0] - mine_f[0] * their_f[1]) * sign_flip
        power_mine = look_sum(mine_f[0] * mine_f[0] + mine_f[1] * mine_f[1])
        power_their = look_sum(their_f[0] * their_f[0] + their_f[1] * their_f[1])
        inverse = 1.0 / jnp.sqrt(power_mine * power_their + 1e-06)
        gamma = jnp.stack([look_sum(real_part) * inverse, look_sum(imag_part) * inverse])
        padded = padded_2(gamma, (("rng", 2),), HALF_W)
        col_count = gamma.shape[2]
        smooth = jnp.zeros_like(gamma)
        for offset in range(-HALF_W, HALF_W + 1):
            weight = (HALF_W + 1 - abs(offset)) / float((HALF_W + 1) ** 2)
            smooth = smooth + weight * padded[:, :, HALF_W + offset : HALF_W + offset + col_count]
        gain_term = (smooth[0] * smooth[0] + smooth[1] * smooth[1] + 0.01) ** (-0.25)
        filtered = smooth * gain_term[None]
        cell_rows = lax.dynamic_slice_in_dim(
            map_cell, upper_flag * half_looks, half_looks, 0
        ).reshape(-1)
        cell_sums = jnp.zeros((2, MAPC), jnp.float32).at[:, cell_rows].add(filtered.reshape(2, -1))
        map_bins.append(cell_sums)
    stacked = jnp.stack(map_bins)[:, None]
    local_counts = jnp.zeros((MAPC,), jnp.float32).at[map_cell.reshape(-1)].add(1.0)
    shaped = stacked.reshape(ROUNDS, 1, 2, acq_count, rng_count * piece)
    count_rows = local_counts.reshape(1, 1, 1, acq_count, rng_count * piece)
    partial_sum, count_sum = (
        lax.psum_scatter(shaped, "rng", scatter_dimension=4, tiled=True),
        lax.psum_scatter(count_rows, "rng", scatter_dimension=4, tiled=True),
    )
    arrived = lax.all_to_all(partial_sum, "acq", split_axis=3, concat_axis=1, tiled=True)
    reduced = arrived.reshape(ROUNDS, acq_count, 2, piece)
    count_mine = lax.dynamic_slice_in_dim(
        count_sum.reshape(acq_count, piece), acq_rank, 1, 0
    ).reshape(piece)
    divisor = jnp.maximum(count_mine, 1.0)
    results = []
    for round_index in range(ROUNDS):
        stride = 2**round_index
        rows_now = (
            reduced[round_index].reshape(acq_count // (2 * stride), 2, stride, 2, piece).sum(axis=1)
        )
        results.append(rows_now.reshape(acq_count // 2, 2, piece) / divisor)
    return jnp.stack(results)


def solution(mesh):
    in_specs = (P(None, ("groups", "acq"), None, "rng"), P("groups", "rng"))
    out_specs = P(None, "groups", None, ("acq", "rng"))
    return jax.shard_map(
        per_device, mesh=mesh, in_specs=in_specs, out_specs=out_specs, check_vma=False
    )
```

profile of v0, /device:TPU:0, one launch (start us, length us, event | category | flops | bytes accessed | tf_op | source)
XLA Modules:
  0.0 361.2 jit_solution(14497064538894836737)
XLA Ops:
  6.5 2.9 collective-permute-start
  11.1 2.6 collective-permute-start.6
  17.2 2.5 add.339
  33.8 3.0 collective-permute-start.4
  43.8 3.0 collective-permute-start.7
  48.7 6.0 %scatter_custom_fusion = f32[2,16384]{0,1:T(8,128)} fusion(s32[512]{0:T(512)S(1)} %bitcast.191, f32[512,2]{1,0:T(8,128)S(1)} %bitcast.171, f32[]{:T(128)} %constant.75.clone.1), kind=kCustom, calls=%fused_computation.10 | custom fusion | flops 1024 | bytes 131076 | tf_op jit(solution)/shard_map/scatter-add | solution.py:76
  54.6 5.2 %copy.61 = f32[1,1,2,8,2048]{4,2,1,0,3:T(2,128)S(1)} copy(f32[1,1,2,8,2048]{2,4,3,1,0:T(8,128)} %bitcast.162) | data formatting | bytes 262144 | tf_op jit(solution)/shard_map/stack | solution.py:78
  60.2 6.0 %scatter_custom_fusion.1 = f32[2,16384]{0,1:T(8,128)} fusion(s32[512]{0:T(512)S(1)} %bitcast.193, f32[512,2]{1,0:T(8,128)S(1)} %bitcast.172, f32[]{:T(128)} %constant.75.clone.1), kind=kCustom, calls=%fused_computation.8 | custom fusion | flops 1024 | bytes 131076 | tf_op jit(solution)/shard_map/scatter-add | solution.py:76
  66.2 5.2 %copy.62 = f32[1,1,2,8,2048]{4,2,1,0,3:T(2,128)S(1)} copy(f32[1,1,2,8,2048]{2,4,3,1,0:T(8,128)} %bitcast.163) | data formatting | bytes 262144 | tf_op jit(solution)/shard_map/stack | solution.py:78
  71.8 6.0 %scatter_custom_fusion.2 = f32[2,16384]{0,1:T(8,128)} fusion(s32[512]{0:T(512)S(1)} %bitcast.192, f32[512,2]{1,0:T(8,128)S(1)} %bitcast.170, f32[]{:T(128)} %constant.75.clone.1), kind=kCustom, calls=%fused_computation.6 | custom fusion | flops 1024 | bytes 131076 | tf_op jit(solution)/shard_map/scatter-add | solution.py:76
  77.7 5.2 %copy.63 = f32[1,1,2,8,2048]{4,2,1,0,3:T(2,128)S(1)} copy(f32[1,1,2,8,2048]{2,4,3,1,0:T(8,128)} %bitcast.164) | data formatting | bytes 262144 | tf_op jit(solution)/shard_map/stack | solution.py:78
  83.2 43.0 %copy.68 = f32[3,1,2,8,2048]{2,1,0,3,4:T(1,128)} copy(f32[3,1,2,8,2048]{4,2,1,0,3:T(2,128)S(1)} %pad_maximum_fusion.1) | data formatting | bytes 786432
  126.2 91.3 %bitcast_reduce_fusion = f32[2048,8,3,2]{3,2,1,0:T(4,128)} fusion(f32[3,1,2,8,2048]{2,1,0,3,4:T(1,128)} %copy.68), kind=kLoop, calls=%fused_computation.4 | loop fusion | bytes 786432
  217.4 36.2 %reshape.470 = f32[2048,48]{1,0:T(8,128)} reshape(f32[2048,8,3,2]{3,2,1,0:T(4,128)} %bitcast_reduce_fusion) | data formatting | bytes 786432
  253.7 11.0 %reduce-scatter.7.cloned.1.call-done = f32[1024,48]{1,0:T(8,128)} async-done(((f32[2048,48]{1,0:T(8,128)}), f32[1024,48]{1,0:T(8,128)}) %reduce-scatter.7.cloned.1.call-update) | async-done | bytes 196624
  264.6 23.7 %reshape.471 = f32[1024,8,3,1,2]{4,3,2,1,0:T(1,128)} reshape(f32[1024,48]{1,0:T(8,128)} %reduce-scatter.7.cloned.1.call-done) | data formatting | bytes 393216
  288.4 27.8 %copy.69 = f32[3,1,2,8,1024]{4,2,1,0,3:T(2,128)} copy(f32[3,1,2,8,1024]{2,1,0,3,4:T(1,128)} %bitcast.161) | data formatting | bytes 393216
  316.2 5.8 %all-to-all-start = ((f32[3,1,2,8,1024]{4,2,1,0,3:T(2,128)}), f32[3,1,2,8,1024]{4,2,1,0,3:T(2,128)S(1)}, u32[]{:S(2)}, u32[]{:S(2)}) async-start(f32[3,1,2,8,1024]{4,2,1,0,3:T(2,128)} %copy.69), calls=%async_computation | async-start | bytes 393216 | tf_op jit(solution)/shard_map/all_to_all | solution.py:86
  322.0 5.9 %scatter_custom_fusion.3 = f32[16384]{0:T(1024)S(1)} fusion(s32[1024]{0:T(1024)S(1)} %bitcast.190, f32[1024]{0:T(1024)S(1)} %broadcast.205, f32[]{:T(128)} %constant.75.clone.1), kind=kCustom, calls=%fused_computation.40 | custom fusion | flops 1024 | bytes 65540 | tf_op jit(solution)/shard_map/scatter-add | solution.py:79
  328.6 9.0 %reduce-scatter.5.cloned.1.call-done = f32[1,1,1,8,1024]{4,3,2,1,0:T(8,128)} async-done(((f32[1,1,1,8,2048]{4,3,2,1,0:T(8,128)}), f32[1,1,1,8,1024]{4,3,2,1,0:T(8,128)}) %reduce-scatter.5.cloned.1.call-update) | async-done | bytes 32784 | tf_op jit(solution)/shard_map/reduce_scatter | solution.py:84
  339.2 2.0 copy.73
  343.2 2.9 bitcast_divide_fusion.2
  346.1 3.2 pad_maximum_fusion
  349.3 5.1 %copy.67 = f32[3,4,2,1024]{3,2,1,0:T(2,128)} copy(f32[3,4,2,1024]{2,3,1,0:T(8,128)} %pad_maximum_fusion) | data formatting | bytes 196608 | tf_op jit(solution)/shard_map/stack | solution.py:99
  (89 shorter events, 32.9 us)
Async XLA Ops:
  6.5 258.1 %reduce-scatter.7.cloned.1.call-start = ((), (), s32[]{:S(2)}) async-start(), calls=%async_computation.4 | async-start | bytes 1572864
  6.5 9.5 %collective-permute-start = (bf16[2,64,1024]{2,1,0:T(8,128)(2,1)}, bf16[2,64,1024]{2,1,0:T(8,128)(2,1)S(1)}, u32[]{:S(2)}, u32[]{:S(2)}) collective-permute-start(bf16[2,64,1024]{2,1,0:T(8,128)(2,1)} %bitcast.167), channel_id=1, source_target_pairs={{0,2},{2,0},{4,6},{6,4},{8,10},{10,8},{12,14},{14,12},{1,3},{3,1},... | collective-permute-start | bytes 786440 | tf_op jit(solution)/shard_map/ppermute | solution.py:16
  9.5 17.7 %collective-permute-start.3 = (bf16[2,64,1024]{2,1,0:T(8,128)(2,1)}, bf16[2,64,1024]{2,1,0:T(8,128)(2,1)}, u32[]{:S(2)}, u32[]{:S(2)}) collective-permute-start(bf16[2,64,1024]{2,1,0:T(8,128)(2,1)} %bitcast.168), channel_id=1, source_target_pairs={{0,4},{2,6},{4,0},{6,2},{8,12},{10,14},{12,8},{14,10},{1,5},{3,7},... | collective-permute-start | bytes 786440 | tf_op jit(solution)/shard_map/ppermute | solution.py:16
  11.1 27.0 %collective-permute-start.6 = (bf16[2,64,1024]{2,1,0:T(8,128)(2,1)}, bf16[2,64,1024]{2,1,0:T(8,128)(2,1)S(1)}, u32[]{:S(2)}, u32[]{:S(2)}) collective-permute-start(bf16[2,64,1024]{2,1,0:T(8,128)(2,1)} %bitcast.169), channel_id=1, source_target_pairs={{0,8},{2,10},{4,12},{6,14},{8,0},{10,2},{12,4},{14,6},{1,9},{3,11}... | collective-permute-start | bytes 786440 | tf_op jit(solution)/shard_map/ppermute | solution.py:16
  24.6 22.2 %collective-permute-start.1 = (f32[2,4,4]{2,1,0:T(4,128)S(1)}, f32[2,4,4]{2,1,0:T(4,128)S(1)}, u32[]{:S(2)}, u32[]{:S(2)}) collective-permute-start(f32[2,4,4]{2,1,0:T(4,128)S(1)} %get-tuple-element.28), channel_id=1, source_target_pairs={{0,1},{2,3},{4,5},{6,7},{8,9},{10,11},{12,13},{14,15},{16,17},{18,... | collective-permute-start | bytes 392 | tf_op jit(solution)/shard_map/ppermute | solution.py:26
  25.9 22.4 %collective-permute-start.2 = (f32[2,4,4]{2,1,0:T(4,128)S(1)}, f32[2,4,4]{2,1,0:T(4,128)S(1)}, u32[]{:S(2)}, u32[]{:S(2)}) collective-permute-start(f32[2,4,4]{2,1,0:T(4,128)S(1)} %get-tuple-element.29), channel_id=1, source_target_pairs={{1,0},{3,2},{5,4},{7,6},{9,8},{11,10},{13,12},{15,14},{17,16},{19,... | collective-permute-start | bytes 392 | tf_op jit(solution)/shard_map/ppermute | solution.py:27
  33.8 26.1 %collective-permute-start.4 = (f32[2,4,4]{2,1,0:T(4,128)S(1)}, f32[2,4,4]{2,1,0:T(4,128)S(1)}, u32[]{:S(2)}, u32[]{:S(2)}) collective-permute-start(f32[2,4,4]{2,1,0:T(4,128)S(1)} %get-tuple-element.37), channel_id=1, source_target_pairs={{0,1},{2,3},{4,5},{6,7},{8,9},{10,11},{12,13},{14,15},{16,17},{18,... | collective-permute-start | bytes 392 | tf_op jit(solution)/shard_map/ppermute | solution.py:26
  36.8 23.1 %collective-permute-start.5 = (f32[2,4,4]{2,1,0:T(4,128)S(1)}, f32[2,4,4]{2,1,0:T(4,128)S(1)}, u32[]{:S(2)}, u32[]{:S(2)}) collective-permute-start(f32[2,4,4]{2,1,0:T(4,128)S(1)} %get-tuple-element.38), channel_id=1, source_target_pairs={{1,0},{3,2},{5,4},{7,6},{9,8},{11,10},{13,12},{15,14},{17,16},{19,... | collective-permute-start | bytes 392 | tf_op jit(solution)/shard_map/ppermute | solution.py:27
  43.8 27.6 %collective-permute-start.7 = (f32[2,4,4]{2,1,0:T(4,128)S(1)}, f32[2,4,4]{2,1,0:T(4,128)S(1)}, u32[]{:S(2)}, u32[]{:S(2)}) collective-permute-start(f32[2,4,4]{2,1,0:T(4,128)S(1)} %get-tuple-element.43), channel_id=1, source_target_pairs={{0,1},{2,3},{4,5},{6,7},{8,9},{10,11},{12,13},{14,15},{16,17},{18,... | collective-permute-start | bytes 392 | tf_op jit(solution)/shard_map/ppermute | solution.py:26
  46.8 24.6 %collective-permute-start.8 = (f32[2,4,4]{2,1,0:T(4,128)S(1)}, f32[2,4,4]{2,1,0:T(4,128)S(1)}, u32[]{:S(2)}, u32[]{:S(2)}) collective-permute-start(f32[2,4,4]{2,1,0:T(4,128)S(1)} %get-tuple-element.44), channel_id=1, source_target_pairs={{1,0},{3,2},{5,4},{7,6},{9,8},{11,10},{13,12},{15,14},{17,16},{19,... | collective-permute-start | bytes 392 | tf_op jit(solution)/shard_map/ppermute | solution.py:27
  288.4 33.6 %copy-start = (s32[8,128]{1,0:T(8,128)S(1)}, s32[8,128]{1,0:T(8,128)}, u32[]{:S(2)}) copy-start(s32[8,128]{1,0:T(8,128)} %param.3) | copy-start | bytes 12292
  316.2 22.2 %all-to-all-start = ((f32[3,1,2,8,1024]{4,2,1,0,3:T(2,128)}), f32[3,1,2,8,1024]{4,2,1,0,3:T(2,128)S(1)}, u32[]{:S(2)}, u32[]{:S(2)}) async-start(f32[3,1,2,8,1024]{4,2,1,0,3:T(2,128)} %copy.69), calls=%async_computation | async-start | bytes 393216 | tf_op jit(solution)/shard_map/all_to_all | solution.py:86
  321.9 15.7 %reduce-scatter.5.cloned.1.call-start = ((), (), s32[]{:S(2)}) async-start(), calls=%async_computation.3 | async-start | bytes 98304 | tf_op jit(solution)/shard_map/reduce_scatter | solution.py:84
Sparse Core Ops, SparseCore 0:
  253.8 10.7 reduce-scatter.6
  328.8 8.8 reduce-scatter.4
where the time goes:
time: 363 us; the launch traced here: 361 us
  local copies, waits for them, and re-layouts  264 us (73%)
  other arithmetic  38.4 us (11%)
  starting transfers between devices  24.3 us (7%)
  waiting for transfers between devices  20.4 us (6%)
  between operations  13.9 us (4%)
    unnamed x13, local copies, waits for them, and re-layouts  227 us
    scatter-add x3, other arithmetic, per_device(): jnp.zeros((2, MAPC), jnp.float32).at[:, cell_rows]  17.9 us
    another operation x3, local copies, waits for them, and re-layouts, per_device(): stacked = jnp.stack(map_bins)[:, None]  15.6 us
    unnamed x3, waiting for transfers between devices  11 us
    reduce_scatter x1, waiting for transfers between devices, per_device(): lax.psum_scatter(count_rows, 'rng', scatter_dimension=4, tiled=True)  9.02 us
    ppermute x3, starting transfers between devices, padded_2(): before = lax.ppermute(last, axis, up)  7.34 us
  transfers between devices with their start and end apart: 12, of which 3 were waited for; matrix products, arithmetic and copies ran while one was open for 15% of the time, Pallas kernels for 0%

commit v1 on v0

v1 whole, which is shorter than its diff:
```python
import functools

import jax
import jax.numpy as jnp
from jax import lax
from jax.experimental import pallas as pl
from jax.experimental.pallas import tpu as pltpu
from jax.sharding import PartitionSpec as P

LOOK_A = 8
LOOK_R = 8
HALF_W = 4
ROUNDS = 3
BLOCK = 2**ROUNDS
MAPC = 16384
WIDE = 256
F32 = jnp.float32
BF16 = jnp.bfloat16

VMEM = pl.BlockSpec(memory_space=pltpu.VMEM)
SMEM = pl.BlockSpec(memory_space=pltpu.SMEM)


def in_two(value):
    high = value.astype(BF16)
    return high, (value - high.astype(F32)).astype(BF16)


def dot(left, right):
    return jnp.dot(left, right, preferred_element_type=F32)


def coherence_kernel(round_index, ids, own, other, out):
    half, width = other.shape[1:]
    looks, cells = half // LOOK_A, width // LOOK_R
    upper = (ids[0] >> round_index) & 1
    rows = pl.ds(pl.multiple_of(upper * half, half), half)
    mine_re, mine_im = own[0, rows, :].astype(F32), own[1, rows, :].astype(F32)
    their_re, their_im = other[0].astype(F32), other[1].astype(F32)
    terms = jnp.concatenate(
        [
            mine_re * their_re + mine_im * their_im,
            mine_im * their_re - mine_re * their_im,
            mine_re * mine_re + mine_im * mine_im,
            their_re * their_re + their_im * their_im,
        ],
        axis=0,
    )
    sample = lax.broadcasted_iota(jnp.int32, (width, cells), 0) // LOOK_R
    cell = lax.broadcasted_iota(jnp.int32, (width, cells), 1)
    take = (sample == cell).astype(F32).astype(BF16)
    high, low = in_two(terms)
    sums = dot(high, take) + dot(low, take)
    sums = sums.reshape(4 * looks, LOOK_A, cells).sum(axis=1)
    power = sums[2 * looks : 3 * looks] * sums[3 * looks :]
    inverse = lax.rsqrt(power + 1e-06)
    sign = (1 - 2 * upper).astype(F32)
    out[...] = sums[: 2 * looks] * jnp.concatenate([inverse, inverse * sign], axis=0)


def coherence(round_index, ids, own, other):
    looks, cells = other.shape[1] // LOOK_A, other.shape[2] // LOOK_R
    return pl.pallas_call(
        functools.partial(coherence_kernel, round_index),
        out_shape=jax.ShapeDtypeStruct((2 * looks, cells), F32),
        in_specs=[SMEM, VMEM, VMEM],
        out_specs=VMEM,
        name=f"coherence_{round_index}",
        cost_estimate=pl.CostEstimate(flops=2 * 2**20, bytes_accessed=2**18, transcendentals=0),
    )(ids, own, other)


def select_kernel(blocks, ids, own_cells, other_cells, band, onehot, masks, scale):
    lines, cols = own_cells.shape
    first = (2 * ids[0] + ids[1]) * blocks
    own, other = own_cells[...], other_cells[...]
    left_core = ids[1] == 0
    halves = [jnp.where(left_core, own, other), jnp.where(left_core, other, own)]
    lane = lax.broadcasted_iota(jnp.int32, (cols, WIDE), 1).astype(F32)
    for side, cells in enumerate(halves):
        low = (cells & (WIDE - 1)).astype(F32)
        tall = jnp.concatenate([low] * (cols // lines), axis=0).T
        for line in range(lines):
            hit = tall[:, line : line + 1] == lane
            start = (line * 2 + side) * cols
            onehot[start : start + cols, :] = hit.astype(F32).astype(BF16)
    wide = jnp.concatenate(halves, axis=1) // WIDE
    mine = [(wide == first + block).astype(F32) for block in range(blocks)]
    for line in range(lines):
        for block in range(blocks):
            masks[line * blocks + block : line * blocks + block + 1, :] = mine[block][line : line + 1]
    count = jnp.zeros((blocks * lines, WIDE), F32)
    for line in range(lines):
        rows = masks[line * blocks : (line + 1) * blocks, :]
        rows = jnp.concatenate([rows] * lines, axis=0).astype(BF16)
        count = count + dot(rows, onehot[line * 2 * cols : (line + 1) * 2 * cols, :])
    scale[...] = 1.0 / jnp.maximum(count[:blocks], 1.0)
    shift = lax.broadcasted_iota(jnp.int32, (2 * cols, 2 * cols), 0)
    shift = jnp.abs(shift - lax.broadcasted_iota(jnp.int32, (2 * cols, 2 * cols), 1))
    band[...] = jnp.maximum(HALF_W + 1 - shift, 0).astype(F32).astype(BF16)


def select(blocks, ids, own_cells, other_cells):
    lines, cols = own_cells.shape
    return pl.pallas_call(
        functools.partial(select_kernel, blocks),
        out_shape=(
            jax.ShapeDtypeStruct((2 * cols, 2 * cols), BF16),
            jax.ShapeDtypeStruct((lines * 2 * cols, WIDE), BF16),
            jax.ShapeDtypeStruct((lines * blocks, 2 * cols), F32),
            jax.ShapeDtypeStruct((blocks, WIDE), F32),
        ),
        in_specs=[SMEM, VMEM, VMEM],
        out_specs=(VMEM,) * 4,
        name="select",
        cost_estimate=pl.CostEstimate(flops=2 * 2**20, bytes_accessed=2**20, transcendentals=0),
    )(ids, own_cells, other_cells)


def geocode_kernel(ids, near, far, near_sent, far_sent, band, onehot, masks, scale, out, by_acq, grid, filt):
    pairs = BLOCK // 2
    looks = near.shape[2] // (2 * ROUNDS)
    lines, cols = 2 * looks, near.shape[3]
    planes = ROUNDS * pairs * 2
    blocks = scale.shape[0]

    def keep(first_half, second_half):
        for other in range(BLOCK):
            half = second_half if other & 1 else first_half
            by_acq[ids[0] ^ other] = half[other >> 1]

    @pl.when(ids[1] == 1)
    def _():
        keep(near, far)

    @pl.when(ids[1] == 0)
    def _():
        keep(near_sent, far_sent)

    for acq in range(BLOCK):
        for side in range(2):
            for r in range(ROUNDS):
                upper = acq >> r & 1
                pair = (acq >> (r + 1) << r) | (acq & (2**r - 1))
                for part in range(2):
                    row = ((r * pairs + pair) * 2 + part) * lines + upper * looks
                    start = (r * 2 + part) * looks
                    grid[row : row + looks, side * cols : (side + 1) * cols] = by_acq[
                        acq, side, start : start + looks, :
                    ]
    high, low = in_two(grid[...])
    smooth = (dot(high, band[...]) + dot(low, band[...])) * (1.0 / (HALF_W + 1) ** 2)
    smooth = smooth.reshape(planes // 2, 2, lines, 2 * cols)
    real, imag = smooth[:, 0], smooth[:, 1]
    gain = lax.rsqrt(jnp.sqrt(real * real + imag * imag + 0.01))
    filtered = (smooth * gain[:, None]).reshape(planes * lines, 2 * cols)
    for side in range(2):
        filt[side] = filtered[:, side * cols : (side + 1) * cols]
    left = []
    for line in range(lines):
        value = [filt[side, pl.ds(line, planes, stride=lines), :] for side in range(2)]
        value = jnp.concatenate(value, axis=1)
        top = value.astype(BF16).astype(F32)
        both = jnp.concatenate([top, value - top], axis=0)
        rows = [both * masks[line * blocks + block : line * blocks + block + 1, :] for block in range(blocks)]
        left.append(jnp.concatenate(rows, axis=0).astype(BF16))
    sums = dot(jnp.concatenate(left, axis=1), onehot[...])
    for block in range(blocks):
        start = block * 2 * planes
        total = sums[start : start + planes] + sums[start + planes : start + 2 * planes]
        total = total * scale[block : block + 1, :]
        for plane in range(0, planes, 2):
            r, pair = plane // (2 * pairs), plane // 2 % pairs
            out[r, pair, :, block * WIDE : (block + 1) * WIDE] = total[plane : plane + 2]


def geocode(ids, near, far, near_sent, far_sent, band, onehot, masks, scale):
    pairs, blocks = BLOCK // 2, scale.shape[0]
    _, _, rows, cols = near.shape
    lines = rows // ROUNDS
    return pl.pallas_call(
        geocode_kernel,
        out_shape=jax.ShapeDtypeStruct((ROUNDS, pairs, 2, blocks * WIDE), F32),
        in_specs=[SMEM] + [VMEM] * 8,
        out_specs=VMEM,
        scratch_shapes=[
            pltpu.VMEM((BLOCK, 2, rows, cols), F32),
            pltpu.VMEM((ROUNDS * pairs * 2 * lines, 2 * cols), F32),
            pltpu.VMEM((2, ROUNDS * pairs * 2 * lines, cols), F32),
        ],
        name="geocode",
        cost_estimate=pl.CostEstimate(flops=2**28, bytes_accessed=2**21, transcendentals=2**16),
    )(ids, near, far, near_sent, far_sent, band, onehot, masks, scale)


def over_cores(value, pairs):
    return lax.ppermute(value, "rng", pairs)


def over_chips(value, mask):
    count = lax.axis_size("acq")
    pairs = [(2 * a + 1, 2 * (a ^ mask) + 1) for a in range(count)]
    return lax.ppermute(value, ("acq", "rng"), pairs)


def gather_small(ids, packed, map_cell):
    piece = MAPC // (lax.axis_size("acq") * lax.axis_size("rng"))
    other_cells = over_cores(map_cell, [(0, 1), (1, 0)])
    chosen = select(piece // WIDE, ids, map_cell, other_cells)
    held = jnp.stack([over_cores(packed, [(0, 1)]), packed])[None]
    for bit in range(ROUNDS - 1, 0, -1):
        held = jnp.concatenate([held, over_chips(held, 2**bit)], axis=0)
    order = [0] * held.shape[0]
    for slot in range(held.shape[0]):
        index = 0
        for place, bit in enumerate(range(ROUNDS - 1, 0, -1)):
            index |= (slot >> place & 1) << (bit - 1)
        order[index] = slot
    held = jnp.stack([held[slot] for slot in order])
    far = over_chips(held, 1)
    near_sent, far_sent = over_cores(held, [(1, 0)]), over_cores(far, [(1, 0)])
    return geocode(ids, held, far, near_sent, far_sent, *chosen)


def gather_large(packed, map_cell):
    acq_count, rng_count = lax.axis_size("acq"), lax.axis_size("rng")
    pairs, piece = acq_count // 2, MAPC // (acq_count * rng_count)
    rows, cols = packed.shape
    looks = rows // (2 * ROUNDS)
    whole = lax.all_gather(packed, ("acq", "rng"))
    whole = whole.reshape(acq_count, rng_count, ROUNDS, 2, looks, cols)
    whole = whole.transpose(2, 0, 3, 4, 1, 5).reshape(ROUNDS, acq_count, 2, looks, rng_count * cols)
    grids = []
    for r in range(ROUNDS):
        split = whole[r].reshape(acq_count // 2 ** (r + 1), 2, 2**r, 2, looks, rng_count * cols)
        grids.append(
            split.transpose(0, 2, 3, 1, 4, 5).reshape(pairs, 2, 2 * looks, rng_count * cols)
        )
    gamma = jnp.stack(grids)
    width = gamma.shape[-1]
    padded = jnp.pad(gamma, [(0, 0)] * 4 + [(HALF_W, HALF_W)])
    smooth = jnp.zeros_like(gamma)
    for offset in range(-HALF_W, HALF_W + 1):
        weight = (HALF_W + 1 - abs(offset)) / float((HALF_W + 1) ** 2)
        smooth = smooth + weight * padded[..., HALF_W + offset : HALF_W + offset + width]
    power = smooth[:, :, 0] ** 2 + smooth[:, :, 1] ** 2 + 0.01
    filtered = smooth * (power ** (-0.25))[:, :, None]
    cells = lax.all_gather(map_cell, "rng", axis=1, tiled=True).reshape(-1, 1)
    first = (lax.axis_index("acq") * rng_count + lax.axis_index("rng")) * piece
    onehot = (cells == first + jnp.arange(piece, dtype=jnp.int32)).astype(F32)
    count = onehot.sum(axis=0)
    sums = jnp.dot(
        filtered.reshape(-1, cells.shape[0]), onehot, precision=lax.Precision.HIGHEST
    ).reshape(ROUNDS, pairs, 2, piece)
    return sums / jnp.maximum(count, 1.0)


def per_device(slc, map_cell):
    acq_count = lax.axis_size("acq")
    acq_rank = lax.axis_index("acq")
    ids = jnp.stack([acq_rank, lax.axis_index("rng")]).astype(jnp.int32)
    own = slc[:, 0]
    half = own.shape[1] // 2
    received = [None] * ROUNDS
    for r in range(ROUNDS - 1, -1, -1):
        start = (1 - (acq_rank >> r & 1)) * half
        partner_rows = lax.dynamic_slice_in_dim(own, start, half, 1)
        pairs = [(a, a ^ 2**r) for a in range(acq_count)]
        received[r] = lax.ppermute(partner_rows, "acq", pairs)
    packed = jnp.concatenate([coherence(r, ids, own, received[r]) for r in range(ROUNDS)], axis=0)
    if acq_count == BLOCK:
        return gather_small(ids, packed, map_cell)
    return gather_large(packed, map_cell)


def solution(mesh):
    in_specs = (P(None, ("groups", "acq"), None, "rng"), P("groups", "rng"))
    out_specs = P(None, "groups", None, ("acq", "rng"))
    return jax.shard_map(
        per_device, mesh=mesh, in_specs=in_specs, out_specs=out_specs, check_vma=False
    )
```

time: 363 us -> 46.1 us (0.13)
  local copies, waits for them, and re-layouts: 264 us -> 4.25 us
  other arithmetic: 38.4 us -> 1.35 us
  waiting for transfers between devices: 20.4 us -> 2.98 us
  between operations: 13.9 us -> 0.19 us
  Pallas kernels: 0 us -> 11 us
    unnamed x13 -> x22, local copies, waits for them, and re-layouts: 227 us -> 3.16 us
    scatter-add x4 -> x0, other arithmetic: 23.8 us -> none  [the longest x3 17.9 us: per_device(): jnp.zeros((2, MAPC), jnp.float32).at[:, cell_rows]]
    another operation x5 -> x0, local copies, waits for them, and re-layouts: 20.7 us -> none  [the longest x3 15.6 us: per_device(): stacked = jnp.stack(map_bins)[:, None]]
    add x9 -> x0, local copies, waits for them, and re-layouts: 11.6 us -> none  [the longest x3 4.8 us: per_device(): power_mine = look_sum(mine_f[0] * mine_f[0] + mine_f[1] * mine_f[1])]
    pallas_call x0 -> x5, Pallas kernels: none -> 11 us  [the longest x3 5.93 us: coherence(): pl.pallas_call(functools.partial(coherence_kernel, round_index), out_shap...]
    unnamed x3 -> x0, waiting for transfers between devices: 11 us -> none
    reduce_scatter x1 -> x0, waiting for transfers between devices: 9.02 us -> none  [per_device(): lax.psum_scatter(count_rows, 'rng', scatter_dimension=4, tiled=True)]
    ppermute x9 -> x10, starting transfers between devices: 18.5 us -> 25.9 us  [the longest x4 16.7 us: over_cores(): return lax.ppermute(value, 'rng', pairs)]
  transfers between devices with their start and end apart: 12 -> 10, of which waited for: 3 -> 3; matrix products, arithmetic and copies ran while one was open for 15% -> 1% of each run, Pallas kernels for 0% -> 14%
where the time goes in v1:
time: 46.1 us; the launch traced here: 45.7 us
  starting transfers between devices  25.9 us (56%)
  Pallas kernels  11 us (24%)
  local copies, waits for them, and re-layouts  4.25 us (9%)
  waiting for transfers between devices  2.98 us (6%)
  other arithmetic  1.35 us (3%)
    ppermute x4, starting transfers between devices, over_cores(): return lax.ppermute(value, 'rng', pairs)  16.7 us
    ppermute x3, starting transfers between devices, per_device(): received[r] = lax.ppermute(partner_rows, 'acq', pairs)  7.17 us
    pallas_call x3, Pallas kernels, coherence(): pl.pallas_call(functools.partial(coherence_kernel, round_index), out_shap...  5.93 us
    unnamed x22, local copies, waits for them, and re-layouts  3.16 us
    pallas_call x1, Pallas kernels, geocode(): pl.pallas_call(geocode_kernel, out_shape=jax.ShapeDtypeStruct((ROUNDS, pa...  2.75 us
    pallas_call x1, Pallas kernels, select(): pl.pallas_call(functools.partial(select_kernel, blocks), out_shape=(jax.S...  2.36 us
    ppermute x3, starting transfers between devices, over_chips(): return lax.ppermute(value, ('acq', 'rng'), pairs)  1.98 us
    ppermute x4, waiting for transfers between devices, over_cores(): return lax.ppermute(value, 'rng', pairs)  1.64 us
  transfers between devices with their start and end apart: 10, of which 3 were waited for; matrix products, arithmetic and copies ran while one was open for 1% of the time, Pallas kernels for 14%

profile of v1, /device:TPU:0, one launch (start us, length us, event | category | flops | bytes accessed | tf_op | source)
XLA Modules:
  0.0 45.7 jit_solution(9968780063874503492)
XLA Ops:
  0.0 1.1 %dynamic-slice_bitcast_fusion.2 = (bf16[2,32,1024]{2,1,0:T(8,128)(2,1)S(1)}, bf16[2,32,1024]{2,1,0:T(8,128)(2,1)S(1)}, bf16[2,32,1024]{2,1,0:T(8,128)(2,1)S(1)}) fusion(bf16[2,1,64,1024]{3,2,1,0:T(8,128)(2,1)} %param.2, s32[]{:T(128)S(6)} %select_n.9, s32[]{:T(128)S(6)} %select_n.11, s32[]{:T(128)S(6)} %select_n.10), kind=kLoop, calls=%fused_computation.2 | loop fusion | bytes 786444 | tf_op jit(solution)/shard_map/dynamic_slice | solution.py:267
  1.1 3.0 %collective-permute-start = (bf16[2,32,1024]{2,1,0:T(8,128)(2,1)S(1)}, bf16[2,32,1024]{2,1,0:T(8,128)(2,1)S(1)}, u32[]{:S(2)}, u32[]{:S(2)}) collective-permute-start(bf16[2,32,1024]{2,1,0:T(8,128)(2,1)S(1)} %get-tuple-element.13), channel_id=1, source_target_pairs={{0,2},{2,0},{4,6},{6,4},{8,10},{10,8},{12,14},{14,12},{1,3},{3,1},... | collective-permute-start | bytes 393224 | tf_op jit(solution)/shard_map/ppermute | solution.py:269
  4.1 2.6 %collective-permute-start.2 = (bf16[2,32,1024]{2,1,0:T(8,128)(2,1)S(1)}, bf16[2,32,1024]{2,1,0:T(8,128)(2,1)S(1)}, u32[]{:S(2)}, u32[]{:S(2)}) collective-permute-start(bf16[2,32,1024]{2,1,0:T(8,128)(2,1)S(1)} %get-tuple-element.14), channel_id=1, source_target_pairs={{0,8},{2,10},{4,12},{6,14},{8,0},{10,2},{12,4},{14,6},{1,9},{3,11}... | collective-permute-start | bytes 393224 | tf_op jit(solution)/shard_map/ppermute | solution.py:269
  6.7 1.6 %collective-permute-start.1 = (bf16[2,32,1024]{2,1,0:T(8,128)(2,1)S(1)}, bf16[2,32,1024]{2,1,0:T(8,128)(2,1)S(1)}, u32[]{:S(2)}, u32[]{:S(2)}) collective-permute-start(bf16[2,32,1024]{2,1,0:T(8,128)(2,1)S(1)} %get-tuple-element.15), channel_id=1, source_target_pairs={{0,4},{2,6},{4,0},{6,2},{8,12},{10,14},{12,8},{14,10},{1,5},{3,7},... | collective-permute-start | bytes 393224 | tf_op jit(solution)/shard_map/ppermute | solution.py:269
  8.3 0.6 %pad_add_fusion.ids = s32[2]{0:T(128)} fusion(s32[1]{0:T(128)} %bitcast.1, s32[1]{0:T(128)} %bitcast), kind=kLoop, calls=%fused_computation.7 | loop fusion | flops 2 | bytes 16 | tf_op jit(solution)/shard_map/stack | solution.py:261
  8.9 0.6 %copy-done.3 = bf16[2,32,1024]{2,1,0:T(8,128)(2,1)} copy-done((bf16[2,32,1024]{2,1,0:T(8,128)(2,1)}, bf16[2,32,1024]{2,1,0:T(8,128)(2,1)S(1)}, u32[]{:S(2)}) %copy-start.3) | copy-done | bytes 131096
  9.5 2.0 %coherence_0.1 = f32[8,128]{1,0:T(8,128)} custom-call(s32[2]{0:T(128)} %pad_add_fusion.ids, bf16[2,64,1024]{2,1,0:T(8,128)(2,1)} %bitcast.14, bf16[2,32,1024]{2,1,0:T(8,128)(2,1)} %copy-done.3), custom_call_target="tpu_custom_call" | custom-call | flops 2097152 | bytes 262144 | tf_op jit(solution)/shard_map/coherence_0/pallas_call | solution.py:63
  11.5 1.3 %collective-permute-done.2.other = bf16[2,32,1024]{2,1,0:T(8,128)(2,1)S(1)} collective-permute-done((bf16[2,32,1024]{2,1,0:T(8,128)(2,1)S(1)}, bf16[2,32,1024]{2,1,0:T(8,128)(2,1)S(1)}, u32[]{:S(2)}, u32[]{:S(2)}) %collective-permute-start.2) | collective-permute-done | bytes 131104 | tf_op jit(solution)/shard_map/ppermute | solution.py:269
  12.8 0.6 %copy-done.2 = bf16[2,32,1024]{2,1,0:T(8,128)(2,1)} copy-done((bf16[2,32,1024]{2,1,0:T(8,128)(2,1)}, bf16[2,32,1024]{2,1,0:T(8,128)(2,1)S(1)}, u32[]{:S(2)}) %copy-start.2) | copy-done | bytes 131096
  13.5 2.0 %coherence_2.1 = f32[8,128]{1,0:T(8,128)} custom-call(s32[2]{0:T(128)} %pad_add_fusion.ids, bf16[2,64,1024]{2,1,0:T(8,128)(2,1)} %bitcast.15, bf16[2,32,1024]{2,1,0:T(8,128)(2,1)} %copy-done.2), custom_call_target="tpu_custom_call" | custom-call | flops 2097152 | bytes 262144 | tf_op jit(solution)/shard_map/coherence_2/pallas_call | solution.py:63
  15.5 0.6 %copy-done.1 = bf16[2,32,1024]{2,1,0:T(8,128)(2,1)} copy-done((bf16[2,32,1024]{2,1,0:T(8,128)(2,1)}, bf16[2,32,1024]{2,1,0:T(8,128)(2,1)S(1)}, u32[]{:S(2)}) %copy-start.1) | copy-done | bytes 131096
  16.1 2.0 %coherence_1.1 = f32[8,128]{1,0:T(8,128)} custom-call(s32[2]{0:T(128)} %pad_add_fusion.ids, bf16[2,64,1024]{2,1,0:T(8,128)(2,1)} %bitcast.16, bf16[2,32,1024]{2,1,0:T(8,128)(2,1)} %copy-done.1), custom_call_target="tpu_custom_call" | custom-call | flops 2097152 | bytes 262144 | tf_op jit(solution)/shard_map/coherence_1/pallas_call | solution.py:63
  18.1 0.7 %pad_maximum_fusion.2 = (f32[24,128]{1,0:T(8,128)S(1)}, f32[1,24,128]{2,1,0:T(8,128)S(1)}) fusion(f32[8,128]{1,0:T(8,128)S(1)} %copy-done.8, f32[8,128]{1,0:T(8,128)} %coherence_1.1, f32[8,128]{1,0:T(8,128)S(1)} %copy-done.7), kind=kLoop, calls=%fused_computation.6 | loop fusion | flops 6144 | bytes 36864 | tf_op jit(solution)/shard_map/concatenate | solution.py:270
  18.8 1.3 %collective-permute-start.3 = (f32[24,128]{1,0:T(8,128)S(1)}, f32[24,128]{1,0:T(8,128)S(1)}, u32[]{:S(2)}, u32[]{:S(2)}) collective-permute-start(f32[24,128]{1,0:T(8,128)S(1)} %get-tuple-element.18), channel_id=1, source_target_pairs={{0,1},{2,3},{4,5},{6,7},{8,9},{10,11},{12,13},{14,15},{16,17},{18,... | collective-permute-start | bytes 36872 | tf_op jit(solution)/shard_map/ppermute | solution.py:197
  20.1 0.8 %collective-permute-done.3 = f32[24,128]{1,0:T(8,128)S(1)} collective-permute-done((f32[24,128]{1,0:T(8,128)S(1)}, f32[24,128]{1,0:T(8,128)S(1)}, u32[]{:S(2)}, u32[]{:S(2)}) %collective-permute-start.3) | collective-permute-done | bytes 12320 | tf_op jit(solution)/shard_map/ppermute | solution.py:197
  20.9 0.7 %collective-permute-start.4 = (f32[1,2,24,128]{3,2,1,0:T(8,128)S(1)}, f32[1,2,24,128]{3,2,1,0:T(8,128)S(1)}, u32[]{:S(2)}, u32[]{:S(2)}) collective-permute-start(f32[1,2,24,128]{3,2,1,0:T(8,128)S(1)} %maximum_bitcast_fusion), channel_id=1, source_target_pairs={{1,9},{3,11},{5,13},{7,15},{9,1},{11,3},{13,5},{15,7},{17,25},{19,... | collective-permute-start | bytes 73736 | tf_op jit(solution)/shard_map/ppermute | solution.py:203
  21.6 0.7 %collective-permute-start.5 = (f32[2,2,24,128]{3,2,1,0:T(8,128)S(1)}, f32[2,2,24,128]{3,2,1,0:T(8,128)S(1)}, u32[]{:S(2)}, u32[]{:S(2)}) collective-permute-start(f32[2,2,24,128]{3,2,1,0:T(8,128)S(1)} %pad_maximum_fusion.1), channel_id=1, source_target_pairs={{1,5},{3,7},{5,1},{7,3},{9,13},{11,15},{13,9},{15,11},{17,21},{19,... | collective-permute-start | bytes 147464 | tf_op jit(solution)/shard_map/ppermute | solution.py:203
  22.3 0.7 %collective-permute-start.6 = (f32[4,2,24,128]{3,2,1,0:T(8,128)S(1)}, f32[4,2,24,128]{3,2,1,0:T(8,128)S(1)}, u32[]{:S(2)}, u32[]{:S(2)}) collective-permute-start(f32[4,2,24,128]{3,2,1,0:T(8,128)S(1)} %pad_maximum_fusion.near), channel_id=1, source_target_pairs={{1,3},{3,1},{5,7},{7,5},{9,11},{11,9},{13,15},{15,13},{17,19},{19,... | collective-permute-start | bytes 294920 | tf_op jit(solution)/shard_map/ppermute | solution.py:203
  23.0 1.3 %collective-permute-start.7 = (f32[4,2,24,128]{3,2,1,0:T(8,128)S(1)}, f32[4,2,24,128]{3,2,1,0:T(8,128)S(1)}, u32[]{:S(2)}, u32[]{:S(2)}) collective-permute-start(f32[4,2,24,128]{3,2,1,0:T(8,128)S(1)} %pad_maximum_fusion.near), channel_id=1, source_target_pairs={{1,0},{3,2},{5,4},{7,6},{9,8},{11,10},{13,12},{15,14},{17,16},{19,... | collective-permute-start | bytes 294920 | tf_op jit(solution)/shard_map/ppermute | solution.py:197
  24.3 1.3 %collective-permute-start.8 = (f32[4,2,24,128]{3,2,1,0:T(8,128)S(1)}, f32[4,2,24,128]{3,2,1,0:T(8,128)S(1)}, u32[]{:S(2)}, u32[]{:S(2)}) collective-permute-start(f32[4,2,24,128]{3,2,1,0:T(8,128)S(1)} %collective-permute-done.6.far), channel_id=1, source_target_pairs={{1,0},{3,2},{5,4},{7,6},{9,8},{11,10},{13,12},{15,14},{17,16},{19,... | collective-permute-start | bytes 294920 | tf_op jit(solution)/shard_map/ppermute | solution.py:197
  25.6 12.9 %collective-permute-start.9 = (s32[8,128]{1,0:T(8,128)S(1)}, s32[8,128]{1,0:T(8,128)S(1)}, u32[]{:S(2)}, u32[]{:S(2)}) collective-permute-start(s32[8,128]{1,0:T(8,128)S(1)} %copy-done.9), channel_id=1, source_target_pairs={{0,1},{1,0},{2,3},{3,2},{4,5},{5,4},{6,7},{7,6},{8,9},{9,8},{10,11... | collective-permute-start | bytes 12296 | tf_op jit(solution)/shard_map/ppermute | solution.py:197
  38.5 0.8 %collective-permute-done.9.other_cells = s32[8,128]{1,0:T(8,128)S(1)} collective-permute-done((s32[8,128]{1,0:T(8,128)S(1)}, s32[8,128]{1,0:T(8,128)S(1)}, u32[]{:S(2)}, u32[]{:S(2)}) %collective-permute-start.9) | collective-permute-done | bytes 4128 | tf_op jit(solution)/shard_map/ppermute | solution.py:197
  39.9 2.4 %select.1 = (bf16[256,256]{1,0:T(8,128)(2,1)}, bf16[2048,256]{1,0:T(8,128)(2,1)}, f32[32,256]{1,0:T(8,128)}, f32[4,256]{1,0:T(4,128)}) custom-call(s32[2]{0:T(128)} %pad_add_fusion.ids, s32[8,128]{1,0:T(8,128)} %own_cells.1, s32[8,128]{1,0:T(8,128)} %copy-done.10), custom_call_target="tpu_custom_call" | custom-call | flops 2097152 | bytes 1048576 | tf_op jit(solution)/shard_map/select/pallas_call | solution.py:105
  42.9 2.7 %geocode.1 = f32[3,4,2,1024]{3,2,1,0:T(2,128)} custom-call(s32[2]{0:T(128)} %pad_add_fusion.ids, f32[4,2,24,128]{3,2,1,0:T(8,128)} %copy-done, f32[4,2,24,128]{3,2,1,0:T(8,128)} %copy-done.4, f32[4,2,24,128]{3,2,1,0:T(8,128)} %copy-done.5, f32[4,2,24,128]{3,2,1,0:T(8,128)} %copy-done.6, bf16[256,256]{1,0:T(8,128)(2,1)} %get-tuple-element.9.band, ...), custom_call_target="tpu_custom_call" | custom-call | flops 268435456 | bytes 2097152 | tf_op jit(solution)/shard_map/geocode/pallas_call | solution.py:181
  (30 shorter events, 1.3 us)
Async XLA Ops:
  1.1 7.8 %collective-permute-start = (bf16[2,32,1024]{2,1,0:T(8,128)(2,1)S(1)}, bf16[2,32,1024]{2,1,0:T(8,128)(2,1)S(1)}, u32[]{:S(2)}, u32[]{:S(2)}) collective-permute-start(bf16[2,32,1024]{2,1,0:T(8,128)(2,1)S(1)} %get-tuple-element.13), channel_id=1, source_target_pairs={{0,2},{2,0},{4,6},{6,4},{8,10},{10,8},{12,14},{14,12},{1,3},{3,1},... | collective-permute-start | bytes 393224 | tf_op jit(solution)/shard_map/ppermute | solution.py:269
  4.1 8.8 %collective-permute-start.2 = (bf16[2,32,1024]{2,1,0:T(8,128)(2,1)S(1)}, bf16[2,32,1024]{2,1,0:T(8,128)(2,1)S(1)}, u32[]{:S(2)}, u32[]{:S(2)}) collective-permute-start(bf16[2,32,1024]{2,1,0:T(8,128)(2,1)S(1)} %get-tuple-element.14), channel_id=1, source_target_pairs={{0,8},{2,10},{4,12},{6,14},{8,0},{10,2},{12,4},{14,6},{1,9},{3,11}... | collective-permute-start | bytes 393224 | tf_op jit(solution)/shard_map/ppermute | solution.py:269
  6.7 8.8 %collective-permute-start.1 = (bf16[2,32,1024]{2,1,0:T(8,128)(2,1)S(1)}, bf16[2,32,1024]{2,1,0:T(8,128)(2,1)S(1)}, u32[]{:S(2)}, u32[]{:S(2)}) collective-permute-start(bf16[2,32,1024]{2,1,0:T(8,128)(2,1)S(1)} %get-tuple-element.15), channel_id=1, source_target_pairs={{0,4},{2,6},{4,0},{6,2},{8,12},{10,14},{12,8},{14,10},{1,5},{3,7},... | collective-permute-start | bytes 393224 | tf_op jit(solution)/shard_map/ppermute | solution.py:269
  8.9 0.6 %copy-start.3 = (bf16[2,32,1024]{2,1,0:T(8,128)(2,1)}, bf16[2,32,1024]{2,1,0:T(8,128)(2,1)S(1)}, u32[]{:S(2)}) copy-start(bf16[2,32,1024]{2,1,0:T(8,128)(2,1)S(1)} %collective-permute-done.other) | copy-start | bytes 393220
  12.8 0.6 %copy-start.2 = (bf16[2,32,1024]{2,1,0:T(8,128)(2,1)}, bf16[2,32,1024]{2,1,0:T(8,128)(2,1)S(1)}, u32[]{:S(2)}) copy-start(bf16[2,32,1024]{2,1,0:T(8,128)(2,1)S(1)} %collective-permute-done.2.other) | copy-start | bytes 393220
  15.5 2.6 %copy-start.7 = (f32[8,128]{1,0:T(8,128)S(1)}, f32[8,128]{1,0:T(8,128)}, u32[]{:S(2)}) copy-start(f32[8,128]{1,0:T(8,128)} %coherence_0.1) | copy-start | bytes 12292
  15.5 2.6 %copy-start.8 = (f32[8,128]{1,0:T(8,128)S(1)}, f32[8,128]{1,0:T(8,128)}, u32[]{:S(2)}) copy-start(f32[8,128]{1,0:T(8,128)} %coherence_2.1) | copy-start | bytes 12292
  15.5 0.6 %copy-start.1 = (bf16[2,32,1024]{2,1,0:T(8,128)(2,1)}, bf16[2,32,1024]{2,1,0:T(8,128)(2,1)S(1)}, u32[]{:S(2)}) copy-start(bf16[2,32,1024]{2,1,0:T(8,128)(2,1)S(1)} %collective-permute-done.1.other) | copy-start | bytes 393220
  18.8 2.1 %collective-permute-start.3 = (f32[24,128]{1,0:T(8,128)S(1)}, f32[24,128]{1,0:T(8,128)S(1)}, u32[]{:S(2)}, u32[]{:S(2)}) collective-permute-start(f32[24,128]{1,0:T(8,128)S(1)} %get-tuple-element.18), channel_id=1, source_target_pairs={{0,1},{2,3},{4,5},{6,7},{8,9},{10,11},{12,13},{14,15},{16,17},{18,... | collective-permute-start | bytes 36872 | tf_op jit(solution)/shard_map/ppermute | solution.py:197
  20.9 0.7 %collective-permute-start.4 = (f32[1,2,24,128]{3,2,1,0:T(8,128)S(1)}, f32[1,2,24,128]{3,2,1,0:T(8,128)S(1)}, u32[]{:S(2)}, u32[]{:S(2)}) collective-permute-start(f32[1,2,24,128]{3,2,1,0:T(8,128)S(1)} %maximum_bitcast_fusion), channel_id=1, source_target_pairs={{1,9},{3,11},{5,13},{7,15},{9,1},{11,3},{13,5},{15,7},{17,25},{19,... | collective-permute-start | bytes 73736 | tf_op jit(solution)/shard_map/ppermute | solution.py:203
  21.6 0.7 %collective-permute-start.5 = (f32[2,2,24,128]{3,2,1,0:T(8,128)S(1)}, f32[2,2,24,128]{3,2,1,0:T(8,128)S(1)}, u32[]{:S(2)}, u32[]{:S(2)}) collective-permute-start(f32[2,2,24,128]{3,2,1,0:T(8,128)S(1)} %pad_maximum_fusion.1), channel_id=1, source_target_pairs={{1,5},{3,7},{5,1},{7,3},{9,13},{11,15},{13,9},{15,11},{17,21},{19,... | collective-permute-start | bytes 147464 | tf_op jit(solution)/shard_map/ppermute | solution.py:203
  22.3 3.3 %copy-start.9 = (s32[8,128]{1,0:T(8,128)S(1)}, s32[8,128]{1,0:T(8,128)}, u32[]{:S(2)}) copy-start(s32[8,128]{1,0:T(8,128)} %own_cells.1) | copy-start | bytes 12292
  22.3 20.0 %copy-start = (f32[4,2,24,128]{3,2,1,0:T(8,128)}, f32[4,2,24,128]{3,2,1,0:T(8,128)S(1)}, u32[]{:S(2)}) copy-start(f32[4,2,24,128]{3,2,1,0:T(8,128)S(1)} %pad_maximum_fusion.near) | copy-start | bytes 294916
  22.3 2.0 %collective-permute-start.6 = (f32[4,2,24,128]{3,2,1,0:T(8,128)S(1)}, f32[4,2,24,128]{3,2,1,0:T(8,128)S(1)}, u32[]{:S(2)}, u32[]{:S(2)}) collective-permute-start(f32[4,2,24,128]{3,2,1,0:T(8,128)S(1)} %pad_maximum_fusion.near), channel_id=1, source_target_pairs={{1,3},{3,1},{5,7},{7,5},{9,11},{11,9},{13,15},{15,13},{17,19},{19,... | collective-permute-start | bytes 294920 | tf_op jit(solution)/shard_map/ppermute | solution.py:203
  23.0 19.3 %collective-permute-start.7 = (f32[4,2,24,128]{3,2,1,0:T(8,128)S(1)}, f32[4,2,24,128]{3,2,1,0:T(8,128)S(1)}, u32[]{:S(2)}, u32[]{:S(2)}) collective-permute-start(f32[4,2,24,128]{3,2,1,0:T(8,128)S(1)} %pad_maximum_fusion.near), channel_id=1, source_target_pairs={{1,0},{3,2},{5,4},{7,6},{9,8},{11,10},{13,12},{15,14},{17,16},{19,... | collective-permute-start | bytes 294920 | tf_op jit(solution)/shard_map/ppermute | solution.py:197
  24.3 18.0 %copy-start.4 = (f32[4,2,24,128]{3,2,1,0:T(8,128)}, f32[4,2,24,128]{3,2,1,0:T(8,128)S(1)}, u32[]{:S(2)}) copy-start(f32[4,2,24,128]{3,2,1,0:T(8,128)S(1)} %collective-permute-done.6.far) | copy-start | bytes 294916
  24.3 18.0 %collective-permute-start.8 = (f32[4,2,24,128]{3,2,1,0:T(8,128)S(1)}, f32[4,2,24,128]{3,2,1,0:T(8,128)S(1)}, u32[]{:S(2)}, u32[]{:S(2)}) collective-permute-start(f32[4,2,24,128]{3,2,1,0:T(8,128)S(1)} %collective-permute-done.6.far), channel_id=1, source_target_pairs={{1,0},{3,2},{5,4},{7,6},{9,8},{11,10},{13,12},{15,14},{17,16},{19,... | collective-permute-start | bytes 294920 | tf_op jit(solution)/shard_map/ppermute | solution.py:197
  25.6 13.7 %collective-permute-start.9 = (s32[8,128]{1,0:T(8,128)S(1)}, s32[8,128]{1,0:T(8,128)S(1)}, u32[]{:S(2)}, u32[]{:S(2)}) collective-permute-start(s32[8,128]{1,0:T(8,128)S(1)} %copy-done.9), channel_id=1, source_target_pairs={{0,1},{1,0},{2,3},{3,2},{4,5},{5,4},{6,7},{7,6},{8,9},{9,8},{10,11... | collective-permute-start | bytes 12296 | tf_op jit(solution)/shard_map/ppermute | solution.py:197
  39.3 0.6 %copy-start.10 = (s32[8,128]{1,0:T(8,128)}, s32[8,128]{1,0:T(8,128)S(1)}, u32[]{:S(2)}) copy-start(s32[8,128]{1,0:T(8,128)S(1)} %collective-permute-done.9.other_cells) | copy-start | bytes 12292
  42.3 0.6 %copy-start.5 = (f32[4,2,24,128]{3,2,1,0:T(8,128)}, f32[4,2,24,128]{3,2,1,0:T(8,128)S(1)}, u32[]{:S(2)}) copy-start(f32[4,2,24,128]{3,2,1,0:T(8,128)S(1)} %collective-permute-done.7.near_sent) | copy-start | bytes 294916
  42.3 0.7 %copy-start.6 = (f32[4,2,24,128]{3,2,1,0:T(8,128)}, f32[4,2,24,128]{3,2,1,0:T(8,128)S(1)}, u32[]{:S(2)}) copy-start(f32[4,2,24,128]{3,2,1,0:T(8,128)S(1)} %collective-permute-done.8.far_sent) | copy-start | bytes 294916

commit v2 on v1

--- a/solution.py
+++ b/solution.py
@@ -12,13 +12,13 @@
 HALF_W = 4
 ROUNDS = 3
 BLOCK = 2**ROUNDS
+STEPS = (4, 2, 1)
 MAPC = 16384
 WIDE = 256
 F32 = jnp.float32
 BF16 = jnp.bfloat16
 
 VMEM = pl.BlockSpec(memory_space=pltpu.VMEM)
-SMEM = pl.BlockSpec(memory_space=pltpu.SMEM)
 
 
 def in_two(value):
@@ -30,10 +30,10 @@
     return jnp.dot(left, right, preferred_element_type=F32)
 
 
-def coherence_kernel(round_index, ids, own, other, out):
+def coherence_kernel(round_index, own, other, out):
     half, width = other.shape[1:]
     looks, cells = half // LOOK_A, width // LOOK_R
-    upper = (ids[0] >> round_index) & 1
+    upper = (lax.axis_index("acq") >> round_index) & 1
     rows = pl.ds(pl.multiple_of(upper * half, half), half)
     mine_re, mine_im = own[0, rows, :].astype(F32), own[1, rows, :].astype(F32)
     their_re, their_im = other[0].astype(F32), other[1].astype(F32)
@@ -58,23 +58,25 @@
     out[...] = sums[: 2 * looks] * jnp.concatenate([inverse, inverse * sign], axis=0)
 
 
-def coherence(round_index, ids, own, other):
+def coherence(round_index, own, other):
     looks, cells = other.shape[1] // LOOK_A, other.shape[2] // LOOK_R
     return pl.pallas_call(
         functools.partial(coherence_kernel, round_index),
         out_shape=jax.ShapeDtypeStruct((2 * looks, cells), F32),
-        in_specs=[SMEM, VMEM, VMEM],
+        in_specs=[VMEM, VMEM],
         out_specs=VMEM,
         name=f"coherence_{round_index}",
+        compiler_params=pltpu.CompilerParams(vmem_limit_bytes=4 * 2**20),
         cost_estimate=pl.CostEstimate(flops=2 * 2**20, bytes_accessed=2**18, transcendentals=0),
-    )(ids, own, other)
-
-
-def select_kernel(blocks, ids, own_cells, other_cells, band, onehot, masks, scale):
+    )(own, other)
+
+
+def select_kernel(blocks, own_cells, other_cells, band, onehot, masks, scale):
     lines, cols = own_cells.shape
-    first = (2 * ids[0] + ids[1]) * blocks
+    core = lax.axis_index("rng")
+    first = (2 * lax.axis_index("acq") + core) * blocks
     own, other = own_cells[...], other_cells[...]
-    left_core = ids[1] == 0
+    left_core = core == 0
     halves = [jnp.where(left_core, own, other), jnp.where(left_core, other, own)]
     lane = lax.broadcasted_iota(jnp.int32, (cols, WIDE), 1).astype(F32)
     for side, cells in enumerate(halves):
@@ -100,7 +102,7 @@
     band[...] = jnp.maximum(HALF_W + 1 - shift, 0).astype(F32).astype(BF16)
 
 
-def select(blocks, ids, own_cells, other_cells):
+def select(blocks, own_cells, other_cells):
     lines, cols = own_cells.shape
     return pl.pallas_call(
         functools.partial(select_kernel, blocks),
@@ -110,33 +112,27 @@
             jax.ShapeDtypeStruct((lines * blocks, 2 * cols), F32),
             jax.ShapeDtypeStruct((blocks, WIDE), F32),
         ),
-        in_specs=[SMEM, VMEM, VMEM],
+        in_specs=[VMEM, VMEM],
         out_specs=(VMEM,) * 4,
         name="select",
+        compiler_params=pltpu.CompilerParams(vmem_limit_bytes=8 * 2**20),
         cost_estimate=pl.CostEstimate(flops=2 * 2**20, bytes_accessed=2**20, transcendentals=0),
-    )(ids, own_cells, other_cells)
-
-
-def geocode_kernel(ids, near, far, near_sent, far_sent, band, onehot, masks, scale, out, by_acq, grid, filt):
+    )(own_cells, other_cells)
+
+
+def geocode_kernel(held, sent, band, onehot, masks, scale, out, by_acq, grid, filt):
     pairs = BLOCK // 2
-    looks = near.shape[2] // (2 * ROUNDS)
-    lines, cols = 2 * looks, near.shape[3]
+    looks = held.shape[1] // (2 * ROUNDS)
+    lines, cols = 2 * looks, held.shape[2]
     planes = ROUNDS * pairs * 2
     blocks = scale.shape[0]
-
-    def keep(first_half, second_half):
-        for other in range(BLOCK):
-            half = second_half if other & 1 else first_half
-            by_acq[ids[0] ^ other] = half[other >> 1]
-
-    @pl.when(ids[1] == 1)
-    def _():
-        keep(near, far)
-
-    @pl.when(ids[1] == 0)
-    def _():
-        keep(near_sent, far_sent)
-
+    rank, core = lax.axis_index("acq"), lax.axis_index("rng")
+
+    for slot in range(BLOCK):
+        steps = [mask for i, mask in enumerate(STEPS) if slot >> i & 1]
+        acq, side = rank ^ sum(steps), core ^ (len(steps) % 2)
+        by_acq[acq, side] = held[slot]
+        by_acq[acq, 1 - side] = sent[slot]
     for acq in range(BLOCK):
         for side in range(2):
             for r in range(ROUNDS):
@@ -174,14 +170,14 @@
             out[r, pair, :, block * WIDE : (block + 1) * WIDE] = total[plane : plane + 2]
 
 
-def geocode(ids, near, far, near_sent, far_sent, band, onehot, masks, scale):
+def geocode(held, sent, band, onehot, masks, scale):
     pairs, blocks = BLOCK // 2, scale.shape[0]
-    _, _, rows, cols = near.shape
+    _, rows, cols = held.shape
     lines = rows // ROUNDS
     return pl.pallas_call(
         geocode_kernel,
         out_shape=jax.ShapeDtypeStruct((ROUNDS, pairs, 2, blocks * WIDE), F32),
-        in_specs=[SMEM] + [VMEM] * 8,
+        in_specs=[VMEM] * 6,
         out_specs=VMEM,
         scratch_shapes=[
             pltpu.VMEM((BLOCK, 2, rows, cols), F32),
@@ -189,37 +185,17 @@
             pltpu.VMEM((2, ROUNDS * pairs * 2 * lines, cols), F32),
         ],
         name="geocode",
+        compiler_params=pltpu.CompilerParams(vmem_limit_bytes=8 * 2**20),
         cost_estimate=pl.CostEstimate(flops=2**28, bytes_accessed=2**21, transcendentals=2**16),
-    )(ids, near, far, near_sent, far_sent, band, onehot, masks, scale)
-
-
-def over_cores(value, pairs):
-    return lax.ppermute(value, "rng", pairs)
-
-
-def over_chips(value, mask):
-    count = lax.axis_size("acq")
-    pairs = [(2 * a + 1, 2 * (a ^ mask) + 1) for a in range(count)]
-    return lax.ppermute(value, ("acq", "rng"), pairs)
-
-
-def gather_small(ids, packed, map_cell):
-    piece = MAPC // (lax.axis_size("acq") * lax.axis_size("rng"))
-    other_cells = over_cores(map_cell, [(0, 1), (1, 0)])
-    chosen = select(piece // WIDE, ids, map_cell, other_cells)
-    held = jnp.stack([over_cores(packed, [(0, 1)]), packed])[None]
-    for bit in range(ROUNDS - 1, 0, -1):
-        held = jnp.concatenate([held, over_chips(held, 2**bit)], axis=0)
-    order = [0] * held.shape[0]
-    for slot in range(held.shape[0]):
-        index = 0
-        for place, bit in enumerate(range(ROUNDS - 1, 0, -1)):
-            index |= (slot >> place & 1) << (bit - 1)
-        order[index] = slot
-    held = jnp.stack([held[slot] for slot in order])
-    far = over_chips(held, 1)
-    near_sent, far_sent = over_cores(held, [(1, 0)]), over_cores(far, [(1, 0)])
-    return geocode(ids, held, far, near_sent, far_sent, *chosen)
+    )(held, sent, band, onehot, masks, scale)
+
+
+def gather_small(packed, chosen):
+    held = packed[None]
+    for mask in STEPS:
+        pairs = [(2 * a + c, 2 * (a ^ mask) + 1 - c) for a in range(BLOCK) for c in range(2)]
+        held = jnp.concatenate([held, lax.ppermute(held, ("acq", "rng"), pairs)], axis=0)
+    return geocode(held, lax.ppermute(held, "rng", [(0, 1), (1, 0)]), *chosen)
 
 
 def gather_large(packed, map_cell):
@@ -258,19 +234,28 @@
 def per_device(slc, map_cell):
     acq_count = lax.axis_size("acq")
     acq_rank = lax.axis_index("acq")
-    ids = jnp.stack([acq_rank, lax.axis_index("rng")]).astype(jnp.int32)
     own = slc[:, 0]
     half = own.shape[1] // 2
     received = [None] * ROUNDS
+    source = own
     for r in range(ROUNDS - 1, -1, -1):
         start = (1 - (acq_rank >> r & 1)) * half
-        partner_rows = lax.dynamic_slice_in_dim(own, start, half, 1)
+        partner_rows = lax.dynamic_slice_in_dim(source, start, half, 1)
         pairs = [(a, a ^ 2**r) for a in range(acq_count)]
         received[r] = lax.ppermute(partner_rows, "acq", pairs)
-    packed = jnp.concatenate([coherence(r, ids, own, received[r]) for r in range(ROUNDS)], axis=0)
-    if acq_count == BLOCK:
-        return gather_small(ids, packed, map_cell)
-    return gather_large(packed, map_cell)
+        if r == ROUNDS - 1:
+            source, _ = lax.optimization_barrier((own, partner_rows))
+    small = acq_count == BLOCK
+    if small:
+        blocks = MAPC // (acq_count * lax.axis_size("rng")) // WIDE
+        chosen = select(blocks, map_cell, lax.ppermute(map_cell, "rng", [(0, 1), (1, 0)]))
+        own, chosen = lax.optimization_barrier((own, chosen))
+    grids = []
+    for r in range(ROUNDS):
+        grids.append(coherence(r, own, received[r]))
+        own, grids[r] = lax.optimization_barrier((own, grids[r]))
+    packed = jnp.concatenate(grids, axis=0)
+    return gather_small(packed, chosen) if small else gather_large(packed, map_cell)
 
 
 def solution(mesh):

time: 46.1 us -> 28.2 us (0.61)
  starting transfers between devices: 25.9 us -> 7.44 us
  waiting for transfers between devices: 2.98 us -> 16.2 us
  Pallas kernels: 11 us -> 3.25 us
  local copies, waits for them, and re-layouts: 4.25 us -> 1.04 us
  other arithmetic: 1.35 us -> 0.02 us
    ppermute x7 -> x5, starting transfers between devices: 18.7 us -> 0.27 us  [the longest x3 0.19 us: gather_small(): lax.ppermute(held, ('acq', 'rng'), pairs)]
    ppermute x7 -> x5, waiting for transfers between devices: 1.65 us -> 13.1 us  [the longest x3 10.6 us: gather_small(): lax.ppermute(held, ('acq', 'rng'), pairs)]
    pallas_call x3, Pallas kernels: 5.93 us -> 1.17 us  [coherence(): pl.pallas_call(functools.partial(coherence_kernel, round_index), out_shap...]
    unnamed x22 -> x4, local copies, waits for them, and re-layouts: 3.16 us -> 0.03 us
    ppermute x3, waiting for transfers between devices: 1.32 us -> 3.14 us  [per_device(): received[r] = lax.ppermute(partner_rows, 'acq', pairs)]
    pallas_call x1, Pallas kernels: 2.36 us -> 0.73 us  [select(): pl.pallas_call(functools.partial(select_kernel, blocks), out_shape=(jax.S...]
    pallas_call x1, Pallas kernels: 2.75 us -> 1.35 us  [geocode(): pl.pallas_call(geocode_kernel, out_shape=jax.ShapeDtypeStruct((ROUNDS, pa...]
    concatenate x2 -> x3, other arithmetic: 0.69 us -> 0.02 us  [gather_small(): jnp.concatenate([held, lax.ppermute(held, ('acq', 'rng'), pairs)], axis=0)]
  transfers between devices with their start and end apart: 10 -> 8, of which waited for: 3 -> 7; matrix products, arithmetic and copies ran while one was open for 1% -> 0% of each run, Pallas kernels for 14% -> 5%
where the time goes in v2:
time: 28.2 us; the launch traced here: 28.1 us
  waiting for transfers between devices  16.2 us (57%)
  starting transfers between devices  7.44 us (26%)
  Pallas kernels  3.25 us (12%)
  local copies, waits for them, and re-layouts  1.04 us (4%)
    ppermute x3, waiting for transfers between devices, gather_small(): lax.ppermute(held, ('acq', 'rng'), pairs)  10.6 us
    ppermute x3, starting transfers between devices, per_device(): received[r] = lax.ppermute(partner_rows, 'acq', pairs)  7.17 us
    ppermute x3, waiting for transfers between devices, per_device(): received[r] = lax.ppermute(partner_rows, 'acq', pairs)  3.14 us
    pallas_call x1, Pallas kernels, geocode(): pl.pallas_call(geocode_kernel, out_shape=jax.ShapeDtypeStruct((ROUNDS, pa...  1.35 us
    ppermute x1, waiting for transfers between devices, gather_small(): return geocode(held, lax.ppermute(held, 'rng', [(0, 1), (1, 0)]), *chosen)  1.29 us
    pallas_call x3, Pallas kernels, coherence(): pl.pallas_call(functools.partial(coherence_kernel, round_index), out_shap...  1.17 us
    ppermute x1, waiting for transfers between devices, per_device(): lax.ppermute(map_cell, 'rng', [(0, 1), (1, 0)])  1.16 us
    dynamic_slice x2, local copies, waits for them, and re-layouts, per_device(): partner_rows = lax.dynamic_slice_in_dim(source, start, half, 1)  1.01 us
  transfers between devices with their start and end apart: 8, of which 7 were waited for; matrix products, arithmetic and copies ran while one was open for 0% of the time, Pallas kernels for 5%

profile of v2, /device:TPU:0, one launch (start us, length us, event | category | flops | bytes accessed | tf_op | source)
XLA Modules:
  0.0 28.1 jit_solution(4496763190231795979)
XLA Ops:
  0.0 1.0 %dynamic-slice_bitcast_fusion = bf16[2,32,1024]{2,1,0:T(8,128)(2,1)S(1)} fusion(bf16[2,1,64,1024]{3,2,1,0:T(8,128)(2,1)} %param.2, s32[]{:T(128)S(6)} %select_n.9), kind=kLoop, calls=%fused_computation | loop fusion | bytes 262148 | tf_op jit(solution)/shard_map/dynamic_slice | solution.py:243
  1.0 0.0 copy-done
  1.0 3.0 %collective-permute-start.1 = (bf16[2,32,1024]{2,1,0:T(8,128)(2,1)S(1)}, bf16[2,32,1024]{2,1,0:T(8,128)(2,1)S(1)}, u32[]{:S(2)}, u32[]{:S(2)}) collective-permute-start(bf16[2,32,1024]{2,1,0:T(8,128)(2,1)S(1)} %get-tuple-element.36), channel_id=1, source_target_pairs={{0,2},{2,0},{4,6},{6,4},{8,10},{10,8},{12,14},{14,12},{1,3},{3,1},... | collective-permute-start | bytes 393224 | tf_op jit(solution)/shard_map/ppermute | solution.py:245
  4.1 1.6 %collective-permute-start.2 = (bf16[2,32,1024]{2,1,0:T(8,128)(2,1)S(1)}, bf16[2,32,1024]{2,1,0:T(8,128)(2,1)S(1)}, u32[]{:S(2)}, u32[]{:S(2)}) collective-permute-start(bf16[2,32,1024]{2,1,0:T(8,128)(2,1)S(1)} %get-tuple-element.35), channel_id=1, source_target_pairs={{0,4},{2,6},{4,0},{6,2},{8,12},{10,14},{12,8},{14,10},{1,5},{3,7},... | collective-permute-start | bytes 393224 | tf_op jit(solution)/shard_map/ppermute | solution.py:245
  5.6 2.6 %collective-permute-start.3 = (bf16[2,32,1024]{2,1,0:T(8,128)(2,1)S(1)}, bf16[2,32,1024]{2,1,0:T(8,128)(2,1)S(1)}, u32[]{:S(2)}, u32[]{:S(2)}) collective-permute-start(bf16[2,32,1024]{2,1,0:T(8,128)(2,1)S(1)} %dynamic-slice_bitcast_fusion), channel_id=1, source_target_pairs={{0,8},{2,10},{4,12},{6,14},{8,0},{10,2},{12,4},{14,6},{1,9},{3,11}... | collective-permute-start | bytes 393224 | tf_op jit(solution)/shard_map/ppermute | solution.py:245
  8.2 0.0 copy-done.1
  8.2 0.0 collective-permute-start
  8.2 1.2 %collective-permute-done.other_cells = s32[8,128]{1,0:T(8,128)S(1)} collective-permute-done((s32[8,128]{1,0:T(8,128)S(1)}, s32[8,128]{1,0:T(8,128)S(1)}, u32[]{:S(2)}, u32[]{:S(2)}) %collective-permute-start) | collective-permute-done | bytes 4128 | tf_op jit(solution)/shard_map/ppermute | solution.py:251
  9.4 0.7 %select.1 = (bf16[256,256]{1,0:T(8,128)(2,1)S(1)}, bf16[2048,256]{1,0:T(8,128)(2,1)S(1)}, f32[32,256]{1,0:T(8,128)S(1)}, f32[4,256]{1,0:T(4,128)S(1)}) custom-call(s32[8,128]{1,0:T(8,128)S(1)} %copy-done.1, s32[8,128]{1,0:T(8,128)S(1)} %collective-permute-done.other_cells), custom_call_target="tpu_custom_call" | custom-call | flops 2097152 | bytes 1048576 | tf_op jit(solution)/shard_map/select/pallas_call | solution.py:107
  10.1 0.0 collective-permute-done.1.other
  10.1 0.4 %coherence_0.1 = f32[8,128]{1,0:T(8,128)S(1)} custom-call(bf16[2,64,1024]{2,1,0:T(8,128)(2,1)S(1)} %bitcast.6, bf16[2,32,1024]{2,1,0:T(8,128)(2,1)S(1)} %collective-permute-done.1.other), custom_call_target="tpu_custom_call" | custom-call | flops 2097152 | bytes 262144 | tf_op jit(solution)/shard_map/coherence_0/pallas_call | solution.py:63
  10.5 0.2 collective-permute-done.2.other
  10.7 0.4 %coherence_1.1 = f32[8,128]{1,0:T(8,128)S(1)} custom-call(bf16[2,64,1024]{2,1,0:T(8,128)(2,1)S(1)} %bitcast.7, bf16[2,32,1024]{2,1,0:T(8,128)(2,1)S(1)} %collective-permute-done.2.other), custom_call_target="tpu_custom_call" | custom-call | flops 2097152 | bytes 262144 | tf_op jit(solution)/shard_map/coherence_1/pallas_call | solution.py:63
  11.1 2.9 %collective-permute-done.3.other = bf16[2,32,1024]{2,1,0:T(8,128)(2,1)S(1)} collective-permute-done((bf16[2,32,1024]{2,1,0:T(8,128)(2,1)S(1)}, bf16[2,32,1024]{2,1,0:T(8,128)(2,1)S(1)}, u32[]{:S(2)}, u32[]{:S(2)}) %collective-permute-start.3) | collective-permute-done | bytes 131104 | tf_op jit(solution)/shard_map/ppermute | solution.py:245
  14.1 0.4 %coherence_2.1 = f32[8,128]{1,0:T(8,128)S(1)} custom-call(bf16[2,64,1024]{2,1,0:T(8,128)(2,1)S(1)} %bitcast.8, bf16[2,32,1024]{2,1,0:T(8,128)(2,1)S(1)} %collective-permute-done.3.other), custom_call_target="tpu_custom_call" | custom-call | flops 2097152 | bytes 262144 | tf_op jit(solution)/shard_map/coherence_2/pallas_call | solution.py:63
  14.5 0.1 collective-permute-start.4
  14.5 4.0 %collective-permute-done.4 = f32[1,24,128]{2,1,0:T(8,128)S(1)} collective-permute-done((f32[1,24,128]{2,1,0:T(8,128)S(1)}, f32[1,24,128]{2,1,0:T(8,128)S(1)}, u32[]{:S(2)}, u32[]{:S(2)}) %collective-permute-start.4) | collective-permute-done | bytes 12320 | tf_op jit(solution)/shard_map/ppermute | solution.py:197
  18.6 0.1 collective-permute-start.5
  18.7 3.1 %collective-permute-done.5 = f32[2,24,128]{2,1,0:T(8,128)S(1)} collective-permute-done((f32[2,24,128]{2,1,0:T(8,128)S(1)}, f32[2,24,128]{2,1,0:T(8,128)S(1)}, u32[]{:S(2)}, u32[]{:S(2)}) %collective-permute-start.5) | collective-permute-done | bytes 24608 | tf_op jit(solution)/shard_map/ppermute | solution.py:197
  21.8 0.0 collective-permute-start.6
  21.8 3.5 %collective-permute-done.6 = f32[4,24,128]{2,1,0:T(8,128)S(1)} collective-permute-done((f32[4,24,128]{2,1,0:T(8,128)S(1)}, f32[4,24,128]{2,1,0:T(8,128)S(1)}, u32[]{:S(2)}, u32[]{:S(2)}) %collective-permute-start.6) | collective-permute-done | bytes 49184 | tf_op jit(solution)/shard_map/ppermute | solution.py:197
  25.3 0.1 collective-permute-start.7
  25.4 1.3 %collective-permute-done.7.sent = f32[8,24,128]{2,1,0:T(8,128)S(1)} collective-permute-done((f32[8,24,128]{2,1,0:T(8,128)S(1)}, f32[8,24,128]{2,1,0:T(8,128)S(1)}, u32[]{:S(2)}, u32[]{:S(2)}) %collective-permute-start.7) | collective-permute-done | bytes 98336 | tf_op jit(solution)/shard_map/ppermute | solution.py:198
  26.7 1.3 %geocode.1 = f32[3,4,2,1024]{3,2,1,0:T(2,128)} custom-call(f32[8,24,128]{2,1,0:T(8,128)S(1)} %pad_maximum_fusion.held, f32[8,24,128]{2,1,0:T(8,128)S(1)} %collective-permute-done.7.sent, bf16[256,256]{1,0:T(8,128)(2,1)S(1)} %get-tuple-element.31.band, bf16[2048,256]{1,0:T(8,128)(2,1)S(1)} %get-tuple-element.32.onehot, ...), custom_call_target="tpu_custom_call" | custom-call | flops 268435456 | bytes 2097152 | tf_op jit(solution)/shard_map/geocode/pallas_call | solution.py:177
  (7 shorter events, 0.0 us)
Async XLA Ops:
  0.0 1.0 %copy-start = (bf16[2,1,64,1024]{3,2,1,0:T(8,128)(2,1)S(1)}, bf16[2,1,64,1024]{3,2,1,0:T(8,128)(2,1)}, u32[]{:S(2)}) copy-start(bf16[2,1,64,1024]{3,2,1,0:T(8,128)(2,1)} %param.2) | copy-start | bytes 786436
  1.0 7.2 %copy-start.1 = (s32[8,128]{1,0:T(8,128)S(1)}, s32[8,128]{1,0:T(8,128)}, u32[]{:S(2)}) copy-start(s32[8,128]{1,0:T(8,128)} %own_cells.1) | copy-start | bytes 12292
  1.0 9.1 %collective-permute-start.1 = (bf16[2,32,1024]{2,1,0:T(8,128)(2,1)S(1)}, bf16[2,32,1024]{2,1,0:T(8,128)(2,1)S(1)}, u32[]{:S(2)}, u32[]{:S(2)}) collective-permute-start(bf16[2,32,1024]{2,1,0:T(8,128)(2,1)S(1)} %get-tuple-element.36), channel_id=1, source_target_pairs={{0,2},{2,0},{4,6},{6,4},{8,10},{10,8},{12,14},{14,12},{1,3},{3,1},... | collective-permute-start | bytes 393224 | tf_op jit(solution)/shard_map/ppermute | solution.py:245
  4.1 6.7 %collective-permute-start.2 = (bf16[2,32,1024]{2,1,0:T(8,128)(2,1)S(1)}, bf16[2,32,1024]{2,1,0:T(8,128)(2,1)S(1)}, u32[]{:S(2)}, u32[]{:S(2)}) collective-permute-start(bf16[2,32,1024]{2,1,0:T(8,128)(2,1)S(1)} %get-tuple-element.35), channel_id=1, source_target_pairs={{0,4},{2,6},{4,0},{6,2},{8,12},{10,14},{12,8},{14,10},{1,5},{3,7},... | collective-permute-start | bytes 393224 | tf_op jit(solution)/shard_map/ppermute | solution.py:245
  5.6 8.4 %collective-permute-start.3 = (bf16[2,32,1024]{2,1,0:T(8,128)(2,1)S(1)}, bf16[2,32,1024]{2,1,0:T(8,128)(2,1)S(1)}, u32[]{:S(2)}, u32[]{:S(2)}) collective-permute-start(bf16[2,32,1024]{2,1,0:T(8,128)(2,1)S(1)} %dynamic-slice_bitcast_fusion), channel_id=1, source_target_pairs={{0,8},{2,10},{4,12},{6,14},{8,0},{10,2},{12,4},{14,6},{1,9},{3,11}... | collective-permute-start | bytes 393224 | tf_op jit(solution)/shard_map/ppermute | solution.py:245
  8.2 1.2 %collective-permute-start = (s32[8,128]{1,0:T(8,128)S(1)}, s32[8,128]{1,0:T(8,128)S(1)}, u32[]{:S(2)}, u32[]{:S(2)}) collective-permute-start(s32[8,128]{1,0:T(8,128)S(1)} %copy-done.1), channel_id=1, source_target_pairs={{0,1},{1,0},{2,3},{3,2},{4,5},{5,4},{6,7},{7,6},{8,9},{9,8},{10,11... | collective-permute-start | bytes 12296 | tf_op jit(solution)/shard_map/ppermute | solution.py:251
  14.5 4.1 %collective-permute-start.4 = (f32[1,24,128]{2,1,0:T(8,128)S(1)}, f32[1,24,128]{2,1,0:T(8,128)S(1)}, u32[]{:S(2)}, u32[]{:S(2)}) collective-permute-start(f32[1,24,128]{2,1,0:T(8,128)S(1)} %maximum_bitcast_fusion), channel_id=1, source_target_pairs={{0,9},{1,8},{2,11},{3,10},{4,13},{5,12},{6,15},{7,14},{8,1},{9,0},... | collective-permute-start | bytes 36872 | tf_op jit(solution)/shard_map/ppermute | solution.py:197
  18.6 3.3 %collective-permute-start.5 = (f32[2,24,128]{2,1,0:T(8,128)S(1)}, f32[2,24,128]{2,1,0:T(8,128)S(1)}, u32[]{:S(2)}, u32[]{:S(2)}) collective-permute-start(f32[2,24,128]{2,1,0:T(8,128)S(1)} %pad_maximum_fusion.2), channel_id=1, source_target_pairs={{0,5},{1,4},{2,7},{3,6},{4,1},{5,0},{6,3},{7,2},{8,13},{9,12},{10,... | collective-permute-start | bytes 73736 | tf_op jit(solution)/shard_map/ppermute | solution.py:197
  21.8 3.5 %collective-permute-start.6 = (f32[4,24,128]{2,1,0:T(8,128)S(1)}, f32[4,24,128]{2,1,0:T(8,128)S(1)}, u32[]{:S(2)}, u32[]{:S(2)}) collective-permute-start(f32[4,24,128]{2,1,0:T(8,128)S(1)} %pad_maximum_fusion.1), channel_id=1, source_target_pairs={{0,3},{1,2},{2,1},{3,0},{4,7},{5,6},{6,5},{7,4},{8,11},{9,10},{10,... | collective-permute-start | bytes 147464 | tf_op jit(solution)/shard_map/ppermute | solution.py:197
  25.3 1.4 %collective-permute-start.7 = (f32[8,24,128]{2,1,0:T(8,128)S(1)}, f32[8,24,128]{2,1,0:T(8,128)S(1)}, u32[]{:S(2)}, u32[]{:S(2)}) collective-permute-start(f32[8,24,128]{2,1,0:T(8,128)S(1)} %pad_maximum_fusion.held), channel_id=1, source_target_pairs={{0,1},{1,0},{2,3},{3,2},{4,5},{5,4},{6,7},{7,6},{8,9},{9,8},{10,11... | collective-permute-start | bytes 294920 | tf_op jit(solution)/shard_map/ppermute | solution.py:198

commit v3 on v2

--- a/solution.py
+++ b/solution.py
@@ -30,45 +30,48 @@
     return jnp.dot(left, right, preferred_element_type=F32)
 
 
-def coherence_kernel(round_index, own, other, out):
-    half, width = other.shape[1:]
+def coherence_kernel(own, *refs):
+    others, out = refs[:-1], refs[-1]
+    half, width = others[0].shape[1:]
     looks, cells = half // LOOK_A, width // LOOK_R
-    upper = (lax.axis_index("acq") >> round_index) & 1
-    rows = pl.ds(pl.multiple_of(upper * half, half), half)
-    mine_re, mine_im = own[0, rows, :].astype(F32), own[1, rows, :].astype(F32)
-    their_re, their_im = other[0].astype(F32), other[1].astype(F32)
-    terms = jnp.concatenate(
-        [
-            mine_re * their_re + mine_im * their_im,
-            mine_im * their_re - mine_re * their_im,
-            mine_re * mine_re + mine_im * mine_im,
-            their_re * their_re + their_im * their_im,
-        ],
-        axis=0,
-    )
     sample = lax.broadcasted_iota(jnp.int32, (width, cells), 0) // LOOK_R
     cell = lax.broadcasted_iota(jnp.int32, (width, cells), 1)
     take = (sample == cell).astype(F32).astype(BF16)
-    high, low = in_two(terms)
-    sums = dot(high, take) + dot(low, take)
-    sums = sums.reshape(4 * looks, LOOK_A, cells).sum(axis=1)
-    power = sums[2 * looks : 3 * looks] * sums[3 * looks :]
-    inverse = lax.rsqrt(power + 1e-06)
-    sign = (1 - 2 * upper).astype(F32)
-    out[...] = sums[: 2 * looks] * jnp.concatenate([inverse, inverse * sign], axis=0)
-
-
-def coherence(round_index, own, other):
-    looks, cells = other.shape[1] // LOOK_A, other.shape[2] // LOOK_R
+    for r, other in enumerate(others):
+        upper = (lax.axis_index("acq") >> r) & 1
+        rows = pl.ds(pl.multiple_of(upper * half, half), half)
+        mine_re, mine_im = own[0, rows, :].astype(F32), own[1, rows, :].astype(F32)
+        their_re, their_im = other[0].astype(F32), other[1].astype(F32)
+        terms = jnp.concatenate(
+            [
+                mine_re * their_re + mine_im * their_im,
+                mine_im * their_re - mine_re * their_im,
+                mine_re * mine_re + mine_im * mine_im,
+                their_re * their_re + their_im * their_im,
+            ],
+            axis=0,
+        )
+        high, low = in_two(terms)
+        sums = dot(high, take) + dot(low, take)
+        sums = sums.reshape(4 * looks, LOOK_A, cells).sum(axis=1)
+        power = sums[2 * looks : 3 * looks] * sums[3 * looks :]
+        inverse = lax.rsqrt(power + 1e-06)
+        sign = (1 - 2 * upper).astype(F32)
+        scale = jnp.concatenate([inverse, inverse * sign], axis=0)
+        out[2 * looks * r : 2 * looks * (r + 1)] = sums[: 2 * looks] * scale
+
+
+def coherence(own, others):
+    looks, cells = others[0].shape[1] // LOOK_A, others[0].shape[2] // LOOK_R
     return pl.pallas_call(
-        functools.partial(coherence_kernel, round_index),
-        out_shape=jax.ShapeDtypeStruct((2 * looks, cells), F32),
-        in_specs=[VMEM, VMEM],
+        coherence_kernel,
+        out_shape=jax.ShapeDtypeStruct((2 * ROUNDS * looks, cells), F32),
+        in_specs=[VMEM] * (1 + ROUNDS),
         out_specs=VMEM,
-        name=f"coherence_{round_index}",
+        name="coherence",
         compiler_params=pltpu.CompilerParams(vmem_limit_bytes=4 * 2**20),
-        cost_estimate=pl.CostEstimate(flops=2 * 2**20, bytes_accessed=2**18, transcendentals=0),
-    )(own, other)
+        cost_estimate=pl.CostEstimate(flops=6 * 2**20, bytes_accessed=2**18, transcendentals=0),
+    )(own, *others)
 
 
 def select_kernel(blocks, own_cells, other_cells, band, onehot, masks, scale):
@@ -250,11 +253,7 @@
         blocks = MAPC // (acq_count * lax.axis_size("rng")) // WIDE
         chosen = select(blocks, map_cell, lax.ppermute(map_cell, "rng", [(0, 1), (1, 0)]))
         own, chosen = lax.optimization_barrier((own, chosen))
-    grids = []
-    for r in range(ROUNDS):
-        grids.append(coherence(r, own, received[r]))
-        own, grids[r] = lax.optimization_barrier((own, grids[r]))
-    packed = jnp.concatenate(grids, axis=0)
+    packed = coherence(own, received)
     return gather_small(packed, chosen) if small else gather_large(packed, map_cell)
 
 

time: 28.2 us -> 26.7 us (0.947)
  waiting for transfers between devices: 16.2 us -> 12.8 us
  starting transfers between devices: 7.44 us -> 9.89 us
  Pallas kernels: 3.25 us -> 2.82 us
    ppermute x3, starting transfers between devices: 0.19 us -> 2.48 us  [gather_small(): lax.ppermute(held, ('acq', 'rng'), pairs)]
    ppermute x3, waiting for transfers between devices: 10.6 us -> 8.84 us  [gather_small(): lax.ppermute(held, ('acq', 'rng'), pairs)]
    ppermute x3, waiting for transfers between devices: 3.14 us -> 1.63 us  [per_device(): received[r] = lax.ppermute(partner_rows, 'acq', pairs)]
    pallas_call x3 -> x1, Pallas kernels: 1.17 us -> 0.75 us  [coherence(): pl.pallas_call(coherence_kernel, out_shape=jax.ShapeDtypeStruct((2 * ROUN...]
  transfers between devices with their start and end apart: 8 -> 8, of which waited for: 7 -> 7; matrix products, arithmetic and copies ran while one was open for 0% -> 0% of each run, Pallas kernels for 5% -> 3%
where the time goes in v3:
time: 26.7 us; the launch traced here: 26.6 us
  waiting for transfers between devices  12.8 us (48%)
  starting transfers between devices  9.89 us (37%)
  Pallas kernels  2.82 us (11%)
  local copies, waits for them, and re-layouts  1.01 us (4%)
    ppermute x3, waiting for transfers between devices, gather_small(): lax.ppermute(held, ('acq', 'rng'), pairs)  8.84 us
    ppermute x3, starting transfers between devices, per_device(): received[r] = lax.ppermute(partner_rows, 'acq', pairs)  7.23 us
    ppermute x3, starting transfers between devices, gather_small(): lax.ppermute(held, ('acq', 'rng'), pairs)  2.48 us
    ppermute x3, waiting for transfers between devices, per_device(): received[r] = lax.ppermute(partner_rows, 'acq', pairs)  1.63 us
    pallas_call x1, Pallas kernels, geocode(): pl.pallas_call(geocode_kernel, out_shape=jax.ShapeDtypeStruct((ROUNDS, pa...  1.35 us
    ppermute x1, waiting for transfers between devices, gather_small(): return geocode(held, lax.ppermute(held, 'rng', [(0, 1), (1, 0)]), *chosen)  1.18 us
    ppermute x1, waiting for transfers between devices, per_device(): lax.ppermute(map_cell, 'rng', [(0, 1), (1, 0)])  1.16 us
    dynamic_slice x2, local copies, waits for them, and re-layouts, per_device(): partner_rows = lax.dynamic_slice_in_dim(source, start, half, 1)  1 us
  transfers between devices with their start and end apart: 8, of which 7 were waited for; matrix products, arithmetic and copies ran while one was open for 0% of the time, Pallas kernels for 3%

profile of v3, /device:TPU:0, one launch (start us, length us, event | category | flops | bytes accessed | tf_op | source)
XLA Modules:
  0.0 26.6 jit_solution(11319266182883618086)
XLA Ops:
  0.0 0.0 copy-start
  0.0 1.0 %dynamic-slice_bitcast_fusion = bf16[2,32,1024]{2,1,0:T(8,128)(2,1)S(1)} fusion(bf16[2,1,64,1024]{3,2,1,0:T(8,128)(2,1)} %param.2, s32[]{:T(128)S(6)} %select_n.9), kind=kLoop, calls=%fused_computation | loop fusion | bytes 262148 | tf_op jit(solution)/shard_map/dynamic_slice | solution.py:246
  1.0 4.1 %collective-permute-start.3 = (bf16[2,32,1024]{2,1,0:T(8,128)(2,1)S(1)}, bf16[2,32,1024]{2,1,0:T(8,128)(2,1)S(1)}, u32[]{:S(2)}, u32[]{:S(2)}) collective-permute-start(bf16[2,32,1024]{2,1,0:T(8,128)(2,1)S(1)} %dynamic-slice_bitcast_fusion), channel_id=1, source_target_pairs={{0,8},{2,10},{4,12},{6,14},{8,0},{10,2},{12,4},{14,6},{1,9},{3,11}... | collective-permute-start | bytes 393224 | tf_op jit(solution)/shard_map/ppermute | solution.py:248
  5.1 0.0 copy-done
  5.1 0.0 copy-start.1
  5.1 1.6 %collective-permute-start.2 = (bf16[2,32,1024]{2,1,0:T(8,128)(2,1)S(1)}, bf16[2,32,1024]{2,1,0:T(8,128)(2,1)S(1)}, u32[]{:S(2)}, u32[]{:S(2)}) collective-permute-start(bf16[2,32,1024]{2,1,0:T(8,128)(2,1)S(1)} %get-tuple-element.25), channel_id=1, source_target_pairs={{0,4},{2,6},{4,0},{6,2},{8,12},{10,14},{12,8},{14,10},{1,5},{3,7},... | collective-permute-start | bytes 393224 | tf_op jit(solution)/shard_map/ppermute | solution.py:248
  6.8 1.5 %collective-permute-start.1 = (bf16[2,32,1024]{2,1,0:T(8,128)(2,1)S(1)}, bf16[2,32,1024]{2,1,0:T(8,128)(2,1)S(1)}, u32[]{:S(2)}, u32[]{:S(2)}) collective-permute-start(bf16[2,32,1024]{2,1,0:T(8,128)(2,1)S(1)} %get-tuple-element.26), channel_id=1, source_target_pairs={{0,2},{2,0},{4,6},{6,4},{8,10},{10,8},{12,14},{14,12},{1,3},{3,1},... | collective-permute-start | bytes 393224 | tf_op jit(solution)/shard_map/ppermute | solution.py:248
  8.3 0.0 copy-done.1
  8.3 0.0 collective-permute-start
  8.3 1.2 %collective-permute-done.other_cells = s32[8,128]{1,0:T(8,128)S(1)} collective-permute-done((s32[8,128]{1,0:T(8,128)S(1)}, s32[8,128]{1,0:T(8,128)S(1)}, u32[]{:S(2)}, u32[]{:S(2)}) %collective-permute-start) | collective-permute-done | bytes 4128 | tf_op jit(solution)/shard_map/ppermute | solution.py:254
  9.4 0.7 %select.1 = (bf16[256,256]{1,0:T(8,128)(2,1)S(1)}, bf16[2048,256]{1,0:T(8,128)(2,1)S(1)}, f32[32,256]{1,0:T(8,128)S(1)}, f32[4,256]{1,0:T(4,128)S(1)}) custom-call(s32[8,128]{1,0:T(8,128)S(1)} %copy-done.1, s32[8,128]{1,0:T(8,128)S(1)} %collective-permute-done.other_cells), custom_call_target="tpu_custom_call" | custom-call | flops 2097152 | bytes 1048576 | tf_op jit(solution)/shard_map/select/pallas_call | solution.py:110
  10.2 1.4 %collective-permute-done.3.refs_2_ = bf16[2,32,1024]{2,1,0:T(8,128)(2,1)S(1)} collective-permute-done((bf16[2,32,1024]{2,1,0:T(8,128)(2,1)S(1)}, bf16[2,32,1024]{2,1,0:T(8,128)(2,1)S(1)}, u32[]{:S(2)}, u32[]{:S(2)}) %collective-permute-start.3) | collective-permute-done | bytes 131104 | tf_op jit(solution)/shard_map/ppermute | solution.py:248
  11.5 0.3 %collective-permute-done.2.refs_1_ = bf16[2,32,1024]{2,1,0:T(8,128)(2,1)S(1)} collective-permute-done((bf16[2,32,1024]{2,1,0:T(8,128)(2,1)S(1)}, bf16[2,32,1024]{2,1,0:T(8,128)(2,1)S(1)}, u32[]{:S(2)}, u32[]{:S(2)}) %collective-permute-start.2) | collective-permute-done | bytes 131104 | tf_op jit(solution)/shard_map/ppermute | solution.py:248
  11.8 0.0 collective-permute-done.1.refs_0_
  11.8 0.8 %coherence.1 = f32[24,128]{1,0:T(8,128)S(1)} custom-call(bf16[2,64,1024]{2,1,0:T(8,128)(2,1)S(1)} %bitcast.5, bf16[2,32,1024]{2,1,0:T(8,128)(2,1)S(1)} %collective-permute-done.1.refs_0_, bf16[2,32,1024]{2,1,0:T(8,128)(2,1)S(1)} %collective-permute-done.2.refs_1_, bf16[2,32,1024]{2,1,0:T(8,128)(2,1)S(1)} %collective-permute-done.3.refs_2_), custom_call_target="tpu_custom_call" | custom-call | flops 6291456 | bytes 262144 | tf_op jit(solution)/shard_map/coherence/pallas_call | solution.py:66
  12.5 0.1 collective-permute-start.4
  12.6 4.0 %collective-permute-done.4 = f32[1,24,128]{2,1,0:T(8,128)S(1)} collective-permute-done((f32[1,24,128]{2,1,0:T(8,128)S(1)}, f32[1,24,128]{2,1,0:T(8,128)S(1)}, u32[]{:S(2)}, u32[]{:S(2)}) %collective-permute-start.4) | collective-permute-done | bytes 12320 | tf_op jit(solution)/shard_map/ppermute | solution.py:200
  16.6 1.2 %collective-permute-start.5 = (f32[2,24,128]{2,1,0:T(8,128)S(1)}, f32[2,24,128]{2,1,0:T(8,128)S(1)}, u32[]{:S(2)}, u32[]{:S(2)}) collective-permute-start(f32[2,24,128]{2,1,0:T(8,128)S(1)} %pad_maximum_fusion.2), channel_id=1, source_target_pairs={{0,5},{1,4},{2,7},{3,6},{4,1},{5,0},{6,3},{7,2},{8,13},{9,12},{10,... | collective-permute-start | bytes 73736 | tf_op jit(solution)/shard_map/ppermute | solution.py:200
  17.8 2.3 %collective-permute-done.5 = f32[2,24,128]{2,1,0:T(8,128)S(1)} collective-permute-done((f32[2,24,128]{2,1,0:T(8,128)S(1)}, f32[2,24,128]{2,1,0:T(8,128)S(1)}, u32[]{:S(2)}, u32[]{:S(2)}) %collective-permute-start.5) | collective-permute-done | bytes 24608 | tf_op jit(solution)/shard_map/ppermute | solution.py:200
  20.1 1.2 %collective-permute-start.6 = (f32[4,24,128]{2,1,0:T(8,128)S(1)}, f32[4,24,128]{2,1,0:T(8,128)S(1)}, u32[]{:S(2)}, u32[]{:S(2)}) collective-permute-start(f32[4,24,128]{2,1,0:T(8,128)S(1)} %pad_maximum_fusion.1), channel_id=1, source_target_pairs={{0,3},{1,2},{2,1},{3,0},{4,7},{5,6},{6,5},{7,4},{8,11},{9,10},{10,... | collective-permute-start | bytes 147464 | tf_op jit(solution)/shard_map/ppermute | solution.py:200
  21.4 2.5 %collective-permute-done.6 = f32[4,24,128]{2,1,0:T(8,128)S(1)} collective-permute-done((f32[4,24,128]{2,1,0:T(8,128)S(1)}, f32[4,24,128]{2,1,0:T(8,128)S(1)}, u32[]{:S(2)}, u32[]{:S(2)}) %collective-permute-start.6) | collective-permute-done | bytes 49184 | tf_op jit(solution)/shard_map/ppermute | solution.py:200
  23.9 0.2 collective-permute-start.7
  24.1 1.2 %collective-permute-done.7.sent = f32[8,24,128]{2,1,0:T(8,128)S(1)} collective-permute-done((f32[8,24,128]{2,1,0:T(8,128)S(1)}, f32[8,24,128]{2,1,0:T(8,128)S(1)}, u32[]{:S(2)}, u32[]{:S(2)}) %collective-permute-start.7) | collective-permute-done | bytes 98336 | tf_op jit(solution)/shard_map/ppermute | solution.py:201
  25.3 1.3 %geocode.1 = f32[3,4,2,1024]{3,2,1,0:T(2,128)} custom-call(f32[8,24,128]{2,1,0:T(8,128)S(1)} %pad_maximum_fusion.held, f32[8,24,128]{2,1,0:T(8,128)S(1)} %collective-permute-done.7.sent, bf16[256,256]{1,0:T(8,128)(2,1)S(1)} %get-tuple-element.21.band, bf16[2048,256]{1,0:T(8,128)(2,1)S(1)} %get-tuple-element.22.onehot, ...), custom_call_target="tpu_custom_call" | custom-call | flops 268435456 | bytes 2097152 | tf_op jit(solution)/shard_map/geocode/pallas_call | solution.py:180
  (4 shorter events, 0.0 us)
Async XLA Ops:
  0.0 5.1 %copy-start = (bf16[2,1,64,1024]{3,2,1,0:T(8,128)(2,1)S(1)}, bf16[2,1,64,1024]{3,2,1,0:T(8,128)(2,1)}, u32[]{:S(2)}) copy-start(bf16[2,1,64,1024]{3,2,1,0:T(8,128)(2,1)} %param.2) | copy-start | bytes 786436
  1.0 10.5 %collective-permute-start.3 = (bf16[2,32,1024]{2,1,0:T(8,128)(2,1)S(1)}, bf16[2,32,1024]{2,1,0:T(8,128)(2,1)S(1)}, u32[]{:S(2)}, u32[]{:S(2)}) collective-permute-start(bf16[2,32,1024]{2,1,0:T(8,128)(2,1)S(1)} %dynamic-slice_bitcast_fusion), channel_id=1, source_target_pairs={{0,8},{2,10},{4,12},{6,14},{8,0},{10,2},{12,4},{14,6},{1,9},{3,11}... | collective-permute-start | bytes 393224 | tf_op jit(solution)/shard_map/ppermute | solution.py:248
  5.1 3.2 %copy-start.1 = (s32[8,128]{1,0:T(8,128)S(1)}, s32[8,128]{1,0:T(8,128)}, u32[]{:S(2)}) copy-start(s32[8,128]{1,0:T(8,128)} %own_cells.1) | copy-start | bytes 12292
  5.1 6.7 %collective-permute-start.2 = (bf16[2,32,1024]{2,1,0:T(8,128)(2,1)S(1)}, bf16[2,32,1024]{2,1,0:T(8,128)(2,1)S(1)}, u32[]{:S(2)}, u32[]{:S(2)}) collective-permute-start(bf16[2,32,1024]{2,1,0:T(8,128)(2,1)S(1)} %get-tuple-element.25), channel_id=1, source_target_pairs={{0,4},{2,6},{4,0},{6,2},{8,12},{10,14},{12,8},{14,10},{1,5},{3,7},... | collective-permute-start | bytes 393224 | tf_op jit(solution)/shard_map/ppermute | solution.py:248
  6.8 5.0 %collective-permute-start.1 = (bf16[2,32,1024]{2,1,0:T(8,128)(2,1)S(1)}, bf16[2,32,1024]{2,1,0:T(8,128)(2,1)S(1)}, u32[]{:S(2)}, u32[]{:S(2)}) collective-permute-start(bf16[2,32,1024]{2,1,0:T(8,128)(2,1)S(1)} %get-tuple-element.26), channel_id=1, source_target_pairs={{0,2},{2,0},{4,6},{6,4},{8,10},{10,8},{12,14},{14,12},{1,3},{3,1},... | collective-permute-start | bytes 393224 | tf_op jit(solution)/shard_map/ppermute | solution.py:248
  8.3 1.2 %collective-permute-start = (s32[8,128]{1,0:T(8,128)S(1)}, s32[8,128]{1,0:T(8,128)S(1)}, u32[]{:S(2)}, u32[]{:S(2)}) collective-permute-start(s32[8,128]{1,0:T(8,128)S(1)} %copy-done.1), channel_id=1, source_target_pairs={{0,1},{1,0},{2,3},{3,2},{4,5},{5,4},{6,7},{7,6},{8,9},{9,8},{10,11... | collective-permute-start | bytes 12296 | tf_op jit(solution)/shard_map/ppermute | solution.py:254
  12.5 4.1 %collective-permute-start.4 = (f32[1,24,128]{2,1,0:T(8,128)S(1)}, f32[1,24,128]{2,1,0:T(8,128)S(1)}, u32[]{:S(2)}, u32[]{:S(2)}) collective-permute-start(f32[1,24,128]{2,1,0:T(8,128)S(1)} %bitcast.6), channel_id=1, source_target_pairs={{0,9},{1,8},{2,11},{3,10},{4,13},{5,12},{6,15},{7,14},{8,1},{9,0},... | collective-permute-start | bytes 36872 | tf_op jit(solution)/shard_map/ppermute | solution.py:200
  16.6 3.5 %collective-permute-start.5 = (f32[2,24,128]{2,1,0:T(8,128)S(1)}, f32[2,24,128]{2,1,0:T(8,128)S(1)}, u32[]{:S(2)}, u32[]{:S(2)}) collective-permute-start(f32[2,24,128]{2,1,0:T(8,128)S(1)} %pad_maximum_fusion.2), channel_id=1, source_target_pairs={{0,5},{1,4},{2,7},{3,6},{4,1},{5,0},{6,3},{7,2},{8,13},{9,12},{10,... | collective-permute-start | bytes 73736 | tf_op jit(solution)/shard_map/ppermute | solution.py:200
  20.1 3.7 %collective-permute-start.6 = (f32[4,24,128]{2,1,0:T(8,128)S(1)}, f32[4,24,128]{2,1,0:T(8,128)S(1)}, u32[]{:S(2)}, u32[]{:S(2)}) collective-permute-start(f32[4,24,128]{2,1,0:T(8,128)S(1)} %pad_maximum_fusion.1), channel_id=1, source_target_pairs={{0,3},{1,2},{2,1},{3,0},{4,7},{5,6},{6,5},{7,4},{8,11},{9,10},{10,... | collective-permute-start | bytes 147464 | tf_op jit(solution)/shard_map/ppermute | solution.py:200
  23.9 1.4 %collective-permute-start.7 = (f32[8,24,128]{2,1,0:T(8,128)S(1)}, f32[8,24,128]{2,1,0:T(8,128)S(1)}, u32[]{:S(2)}, u32[]{:S(2)}) collective-permute-start(f32[8,24,128]{2,1,0:T(8,128)S(1)} %pad_maximum_fusion.held), channel_id=1, source_target_pairs={{0,1},{1,0},{2,3},{3,2},{4,5},{5,4},{6,7},{7,6},{8,9},{9,8},{10,11... | collective-permute-start | bytes 294920 | tf_op jit(solution)/shard_map/ppermute | solution.py:201

commit v4 on v2

--- a/solution.py
+++ b/solution.py
@@ -13,6 +13,8 @@
 ROUNDS = 3
 BLOCK = 2**ROUNDS
 STEPS = (4, 2, 1)
+SEND = (2, 0, 3, 1)
+WHOLE = ((1, 0), (2, 2), (2, 0), (1, 2))
 MAPC = 16384
 WIDE = 256
 F32 = jnp.float32
@@ -30,11 +32,12 @@
     return jnp.dot(left, right, preferred_element_type=F32)
 
 
-def coherence_kernel(round_index, own, other, out):
-    half, width = other.shape[1:]
-    looks, cells = half // LOOK_A, width // LOOK_R
-    upper = (lax.axis_index("acq") >> round_index) & 1
-    rows = pl.ds(pl.multiple_of(upper * half, half), half)
+def coherence_kernel(bit, own, other, out):
+    lines, width = own.shape[1:]
+    count = other.shape[1]
+    cells, looks = width // LOOK_R, count // LOOK_A
+    upper = (lax.axis_index("acq") >> bit) & 1
+    rows = pl.ds(pl.multiple_of(upper * count, count), count) if count < lines else slice(None)
     mine_re, mine_im = own[0, rows, :].astype(F32), own[1, rows, :].astype(F32)
     their_re, their_im = other[0].astype(F32), other[1].astype(F32)
     terms = jnp.concatenate(
@@ -58,14 +61,14 @@
     out[...] = sums[: 2 * looks] * jnp.concatenate([inverse, inverse * sign], axis=0)
 
 
-def coherence(round_index, own, other):
-    looks, cells = other.shape[1] // LOOK_A, other.shape[2] // LOOK_R
+def coherence(bit, own, other):
+    looks, cells = other.shape[1] // LOOK_A, own.shape[2] // LOOK_R
     return pl.pallas_call(
-        functools.partial(coherence_kernel, round_index),
+        functools.partial(coherence_kernel, bit),
         out_shape=jax.ShapeDtypeStruct((2 * looks, cells), F32),
         in_specs=[VMEM, VMEM],
         out_specs=VMEM,
-        name=f"coherence_{round_index}",
+        name=f"coherence_{bit}",
         compiler_params=pltpu.CompilerParams(vmem_limit_bytes=4 * 2**20),
         cost_estimate=pl.CostEstimate(flops=2 * 2**20, bytes_accessed=2**18, transcendentals=0),
     )(own, other)
@@ -122,28 +125,25 @@
 
 def geocode_kernel(held, sent, band, onehot, masks, scale, out, by_acq, grid, filt):
     pairs = BLOCK // 2
-    looks = held.shape[1] // (2 * ROUNDS)
+    looks = held.shape[1] // 6
     lines, cols = 2 * looks, held.shape[2]
     planes = ROUNDS * pairs * 2
     blocks = scale.shape[0]
     rank, core = lax.axis_index("acq"), lax.axis_index("rng")
-
     for slot in range(BLOCK):
         steps = [mask for i, mask in enumerate(STEPS) if slot >> i & 1]
         acq, side = rank ^ sum(steps), core ^ (len(steps) % 2)
         by_acq[acq, side] = held[slot]
         by_acq[acq, 1 - side] = sent[slot]
-    for acq in range(BLOCK):
-        for side in range(2):
-            for r in range(ROUNDS):
-                upper = acq >> r & 1
-                pair = (acq >> (r + 1) << r) | (acq & (2**r - 1))
-                for part in range(2):
-                    row = ((r * pairs + pair) * 2 + part) * lines + upper * looks
-                    start = (r * 2 + part) * looks
-                    grid[row : row + looks, side * cols : (side + 1) * cols] = by_acq[
-                        acq, side, start : start + looks, :
-                    ]
+    for side in range(2):
+        columns = slice(side * cols, (side + 1) * cols)
+        for acq in range(BLOCK):
+            for part in range(2):
+                row = (acq // 2 * 2 + part) * lines + (acq & 1) * looks
+                grid[row : row + looks, columns] = by_acq[acq, side, part * looks : (part + 1) * looks, :]
+            r, pair = WHOLE[acq >> 1]
+            row = (r * pairs + pair + (acq & 1)) * 2 * lines
+            grid[row : row + 2 * lines, columns] = by_acq[acq, side, lines:, :]
     high, low = in_two(grid[...])
     smooth = (dot(high, band[...]) + dot(low, band[...])) * (1.0 / (HALF_W + 1) ** 2)
     smooth = smooth.reshape(planes // 2, 2, lines, 2 * cols)
@@ -173,7 +173,7 @@
 def geocode(held, sent, band, onehot, masks, scale):
     pairs, blocks = BLOCK // 2, scale.shape[0]
     _, rows, cols = held.shape
-    lines = rows // ROUNDS
+    lines = rows // 3
     return pl.pallas_call(
         geocode_kernel,
         out_shape=jax.ShapeDtypeStruct((ROUNDS, pairs, 2, blocks * WIDE), F32),
@@ -190,11 +190,15 @@
     )(held, sent, band, onehot, masks, scale)
 
 
+def across(value, mask):
+    pairs = [(2 * a + c, 2 * (a ^ mask) + 1 - c) for a in range(BLOCK) for c in range(2)]
+    return lax.ppermute(value, ("acq", "rng"), pairs)
+
+
 def gather_small(packed, chosen):
     held = packed[None]
     for mask in STEPS:
-        pairs = [(2 * a + c, 2 * (a ^ mask) + 1 - c) for a in range(BLOCK) for c in range(2)]
-        held = jnp.concatenate([held, lax.ppermute(held, ("acq", "rng"), pairs)], axis=0)
+        held = jnp.concatenate([held, across(held, mask)], axis=0)
     return geocode(held, lax.ppermute(held, "rng", [(0, 1), (1, 0)]), *chosen)
 
 
@@ -202,18 +206,17 @@
     acq_count, rng_count = lax.axis_size("acq"), lax.axis_size("rng")
     pairs, piece = acq_count // 2, MAPC // (acq_count * rng_count)
     rows, cols = packed.shape
-    looks = rows // (2 * ROUNDS)
-    whole = lax.all_gather(packed, ("acq", "rng"))
-    whole = whole.reshape(acq_count, rng_count, ROUNDS, 2, looks, cols)
-    whole = whole.transpose(2, 0, 3, 4, 1, 5).reshape(ROUNDS, acq_count, 2, looks, rng_count * cols)
-    grids = []
-    for r in range(ROUNDS):
-        split = whole[r].reshape(acq_count // 2 ** (r + 1), 2, 2**r, 2, looks, rng_count * cols)
-        grids.append(
-            split.transpose(0, 2, 3, 1, 4, 5).reshape(pairs, 2, 2 * looks, rng_count * cols)
-        )
+    lines, looks, width = rows // 3, rows // 6, rng_count * cols
+    whole = lax.all_gather(packed, ("acq", "rng")).reshape(acq_count, rng_count, rows, cols)
+    whole = whole.transpose(0, 2, 1, 3).reshape(acq_count, rows, width)
+    halves = whole[:, :lines].reshape(pairs, 2, 2, looks, width)
+    grids = [halves.transpose(0, 2, 1, 3, 4).reshape(pairs, 2, lines, width)]
+    planes = whole[:, lines:].reshape(acq_count // BLOCK, 4, 2, 2, lines, width)
+    for r in range(1, ROUNDS):
+        quads = sorted((pair, quad) for quad, (found, pair) in enumerate(WHOLE) if found == r)
+        grid = jnp.stack([planes[:, quad] for _, quad in quads], axis=1)
+        grids.append(grid.reshape(pairs, 2, lines, width))
     gamma = jnp.stack(grids)
-    width = gamma.shape[-1]
     padded = jnp.pad(gamma, [(0, 0)] * 4 + [(HALF_W, HALF_W)])
     smooth = jnp.zeros_like(gamma)
     for offset in range(-HALF_W, HALF_W + 1):
@@ -236,25 +239,16 @@
     acq_rank = lax.axis_index("acq")
     own = slc[:, 0]
     half = own.shape[1] // 2
-    received = [None] * ROUNDS
-    source = own
-    for r in range(ROUNDS - 1, -1, -1):
-        start = (1 - (acq_rank >> r & 1)) * half
-        partner_rows = lax.dynamic_slice_in_dim(source, start, half, 1)
-        pairs = [(a, a ^ 2**r) for a in range(acq_count)]
-        received[r] = lax.ppermute(partner_rows, "acq", pairs)
-        if r == ROUNDS - 1:
-            source, _ = lax.optimization_barrier((own, partner_rows))
+    quarter = [(a & -BLOCK) + 2 * SEND[a % BLOCK // 2] + a % 2 for a in range(acq_count)]
+    whole = lax.ppermute(own, "acq", list(enumerate(quarter)))
+    part = lax.dynamic_slice_in_dim(own, (1 - acq_rank % 2) * half, half, 1)
+    part = lax.ppermute(part, "acq", [(a, a ^ 1) for a in range(acq_count)])
     small = acq_count == BLOCK
     if small:
         blocks = MAPC // (acq_count * lax.axis_size("rng")) // WIDE
         chosen = select(blocks, map_cell, lax.ppermute(map_cell, "rng", [(0, 1), (1, 0)]))
         own, chosen = lax.optimization_barrier((own, chosen))
-    grids = []
-    for r in range(ROUNDS):
-        grids.append(coherence(r, own, received[r]))
-        own, grids[r] = lax.optimization_barrier((own, grids[r]))
-    packed = jnp.concatenate(grids, axis=0)
+    packed = jnp.concatenate([coherence(0, own, part), coherence(2, own, whole)], axis=0)
     return gather_small(packed, chosen) if small else gather_large(packed, map_cell)
 
 

time: 28.2 us -> 24.9 us (0.88)
  waiting for transfers between devices: 16.2 us -> 11.6 us
  starting transfers between devices: 7.44 us -> 9.11 us
    ppermute x6 -> x5, waiting for transfers between devices: 13.8 us -> 9.32 us  [the longest x3 7.74 us: across(): return lax.ppermute(value, ('acq', 'rng'), pairs)]
    ppermute x6 -> x5, starting transfers between devices: 7.36 us -> 8.87 us  [the longest x1 4.04 us: per_device(): whole = lax.ppermute(own, 'acq', list(enumerate(quarter)))]
    pallas_call x3 -> x2, Pallas kernels: 1.17 us -> 0.98 us  [coherence(): pl.pallas_call(functools.partial(coherence_kernel, bit), out_shape=jax.Sh...]
    dynamic_slice x2 -> x1, local copies, waits for them, and re-layouts: 1.01 us -> 0.94 us  [per_device(): part = lax.dynamic_slice_in_dim(own, (1 - acq_rank % 2) * half, half, 1)]
  transfers between devices with their start and end apart: 8 -> 7, of which waited for: 7 -> 6; matrix products, arithmetic and copies ran while one was open for 0% -> 4% of each run, Pallas kernels for 5% -> 5%
where the time goes in v4:
time: 24.9 us; the launch traced here: 24.8 us
  waiting for transfers between devices  11.6 us (47%)
  starting transfers between devices  9.11 us (37%)
  Pallas kernels  3.04 us (12%)
  local copies, waits for them, and re-layouts  0.95 us (4%)
    ppermute x3, waiting for transfers between devices, across(): return lax.ppermute(value, ('acq', 'rng'), pairs)  7.74 us
    ppermute x1, starting transfers between devices, per_device(): whole = lax.ppermute(own, 'acq', list(enumerate(quarter)))  4.04 us
    ppermute x3, starting transfers between devices, across(): return lax.ppermute(value, ('acq', 'rng'), pairs)  3.28 us
    ppermute x1, waiting for transfers between devices, per_device(): part = lax.ppermute(part, 'acq', [(a, a ^ 1) for a in range(acq_count)])  1.57 us
    ppermute x1, starting transfers between devices, per_device(): part = lax.ppermute(part, 'acq', [(a, a ^ 1) for a in range(acq_count)])  1.56 us
    pallas_call x1, Pallas kernels, geocode(): pl.pallas_call(geocode_kernel, out_shape=jax.ShapeDtypeStruct((ROUNDS, pa...  1.34 us
    ppermute x1, waiting for transfers between devices, per_device(): lax.ppermute(map_cell, 'rng', [(0, 1), (1, 0)])  1.16 us
    ppermute x1, waiting for transfers between devices, gather_small(): return geocode(held, lax.ppermute(held, 'rng', [(0, 1), (1, 0)]), *chosen)  1.13 us
  transfers between devices with their start and end apart: 7, of which 6 were waited for; matrix products, arithmetic and copies ran while one was open for 4% of the time, Pallas kernels for 5%

profile of v4, /device:TPU:0, one launch (start us, length us, event | category | flops | bytes accessed | tf_op | source)
XLA Modules:
  0.0 24.8 jit_solution(8047743198872646169)
XLA Ops:
  0.0 0.0 copy-start
  0.0 4.0 %collective-permute-start.2 = (bf16[2,64,1024]{2,1,0:T(8,128)(2,1)}, bf16[2,64,1024]{2,1,0:T(8,128)(2,1)S(1)}, u32[]{:S(2)}, u32[]{:S(2)}) collective-permute-start(bf16[2,64,1024]{2,1,0:T(8,128)(2,1)} %bitcast.5), channel_id=1, source_target_pairs={{0,8},{2,10},{4,0},{6,2},{8,12},{10,14},{12,4},{14,6},{1,9},{3,11}... | collective-permute-start | bytes 786440 | tf_op jit(solution)/shard_map/ppermute | solution.py:243
  4.0 0.0 copy-start.1
  4.0 0.9 %dynamic-slice_bitcast_fusion = bf16[2,32,1024]{2,1,0:T(8,128)(2,1)S(1)} fusion(bf16[2,1,64,1024]{3,2,1,0:T(8,128)(2,1)} %param.2, s32[]{:T(128)S(6)} %select_n.11), kind=kLoop, calls=%fused_computation | loop fusion | bytes 262148 | tf_op jit(solution)/shard_map/dynamic_slice | solution.py:244
  5.0 1.6 %collective-permute-start.1 = (bf16[2,32,1024]{2,1,0:T(8,128)(2,1)S(1)}, bf16[2,32,1024]{2,1,0:T(8,128)(2,1)S(1)}, u32[]{:S(2)}, u32[]{:S(2)}) collective-permute-start(bf16[2,32,1024]{2,1,0:T(8,128)(2,1)S(1)} %dynamic-slice_bitcast_fusion), channel_id=1, source_target_pairs={{0,2},{2,0},{4,6},{6,4},{8,10},{10,8},{12,14},{14,12},{1,3},{3,1},... | collective-permute-start | bytes 393224 | tf_op jit(solution)/shard_map/ppermute | solution.py:245
  6.5 0.0 copy-done.1
  6.5 0.0 collective-permute-start
  6.6 1.2 %collective-permute-done.other_cells = s32[8,128]{1,0:T(8,128)S(1)} collective-permute-done((s32[8,128]{1,0:T(8,128)S(1)}, s32[8,128]{1,0:T(8,128)S(1)}, u32[]{:S(2)}, u32[]{:S(2)}) %collective-permute-start) | collective-permute-done | bytes 4128 | tf_op jit(solution)/shard_map/ppermute | solution.py:249
  7.7 0.7 %select.3 = (bf16[256,256]{1,0:T(8,128)(2,1)S(1)}, bf16[2048,256]{1,0:T(8,128)(2,1)S(1)}, f32[32,256]{1,0:T(8,128)S(1)}, f32[4,256]{1,0:T(4,128)S(1)}) custom-call(s32[8,128]{1,0:T(8,128)S(1)} %copy-done.1, s32[8,128]{1,0:T(8,128)S(1)} %collective-permute-done.other_cells), custom_call_target="tpu_custom_call" | custom-call | flops 2097152 | bytes 1048576 | tf_op jit(solution)/shard_map/select/pallas_call | solution.py:110
  8.4 1.6 %collective-permute-done.1.other = bf16[2,32,1024]{2,1,0:T(8,128)(2,1)S(1)} collective-permute-done((bf16[2,32,1024]{2,1,0:T(8,128)(2,1)S(1)}, bf16[2,32,1024]{2,1,0:T(8,128)(2,1)S(1)}, u32[]{:S(2)}, u32[]{:S(2)}) %collective-permute-start.1) | collective-permute-done | bytes 131104 | tf_op jit(solution)/shard_map/ppermute | solution.py:245
  10.0 0.0 copy-done
  10.0 0.4 %coherence_0.1 = f32[8,128]{1,0:T(8,128)S(1)} custom-call(bf16[2,64,1024]{2,1,0:T(8,128)(2,1)S(1)} %bitcast.6, bf16[2,32,1024]{2,1,0:T(8,128)(2,1)S(1)} %collective-permute-done.1.other), custom_call_target="tpu_custom_call" | custom-call | flops 2097152 | bytes 262144 | tf_op jit(solution)/shard_map/coherence_0/pallas_call | solution.py:66
  10.4 0.0 collective-permute-done.2.other
  10.4 0.6 %coherence_2.1 = f32[16,128]{1,0:T(8,128)S(1)} custom-call(bf16[2,64,1024]{2,1,0:T(8,128)(2,1)S(1)} %bitcast.7, bf16[2,64,1024]{2,1,0:T(8,128)(2,1)S(1)} %collective-permute-done.2.other), custom_call_target="tpu_custom_call" | custom-call | flops 2097152 | bytes 262144 | tf_op jit(solution)/shard_map/coherence_2/pallas_call | solution.py:66
  11.0 1.4 %collective-permute-start.3 = (f32[1,24,128]{2,1,0:T(8,128)S(1)}, f32[1,24,128]{2,1,0:T(8,128)S(1)}, u32[]{:S(2)}, u32[]{:S(2)}) collective-permute-start(f32[1,24,128]{2,1,0:T(8,128)S(1)} %maximum_bitcast_fusion), channel_id=1, source_target_pairs={{0,9},{1,8},{2,11},{3,10},{4,13},{5,12},{6,15},{7,14},{8,1},{9,0},... | collective-permute-start | bytes 36872 | tf_op jit(solution)/shard_map/ppermute | solution.py:195
  12.4 2.7 %collective-permute-done.3 = f32[1,24,128]{2,1,0:T(8,128)S(1)} collective-permute-done((f32[1,24,128]{2,1,0:T(8,128)S(1)}, f32[1,24,128]{2,1,0:T(8,128)S(1)}, u32[]{:S(2)}, u32[]{:S(2)}) %collective-permute-start.3) | collective-permute-done | bytes 12320 | tf_op jit(solution)/shard_map/ppermute | solution.py:195
  15.1 0.5 %collective-permute-start.4 = (f32[2,24,128]{2,1,0:T(8,128)S(1)}, f32[2,24,128]{2,1,0:T(8,128)S(1)}, u32[]{:S(2)}, u32[]{:S(2)}) collective-permute-start(f32[2,24,128]{2,1,0:T(8,128)S(1)} %pad_maximum_fusion.2), channel_id=1, source_target_pairs={{0,5},{1,4},{2,7},{3,6},{4,1},{5,0},{6,3},{7,2},{8,13},{9,12},{10,... | collective-permute-start | bytes 73736 | tf_op jit(solution)/shard_map/ppermute | solution.py:195
  15.7 2.7 %collective-permute-done.4 = f32[2,24,128]{2,1,0:T(8,128)S(1)} collective-permute-done((f32[2,24,128]{2,1,0:T(8,128)S(1)}, f32[2,24,128]{2,1,0:T(8,128)S(1)}, u32[]{:S(2)}, u32[]{:S(2)}) %collective-permute-start.4) | collective-permute-done | bytes 24608 | tf_op jit(solution)/shard_map/ppermute | solution.py:195
  18.4 1.3 %collective-permute-start.5 = (f32[4,24,128]{2,1,0:T(8,128)S(1)}, f32[4,24,128]{2,1,0:T(8,128)S(1)}, u32[]{:S(2)}, u32[]{:S(2)}) collective-permute-start(f32[4,24,128]{2,1,0:T(8,128)S(1)} %pad_maximum_fusion.1), channel_id=1, source_target_pairs={{0,3},{1,2},{2,1},{3,0},{4,7},{5,6},{6,5},{7,4},{8,11},{9,10},{10,... | collective-permute-start | bytes 147464 | tf_op jit(solution)/shard_map/ppermute | solution.py:195
  19.7 2.3 %collective-permute-done.5 = f32[4,24,128]{2,1,0:T(8,128)S(1)} collective-permute-done((f32[4,24,128]{2,1,0:T(8,128)S(1)}, f32[4,24,128]{2,1,0:T(8,128)S(1)}, u32[]{:S(2)}, u32[]{:S(2)}) %collective-permute-start.5) | collective-permute-done | bytes 49184 | tf_op jit(solution)/shard_map/ppermute | solution.py:195
  22.1 0.2 collective-permute-start.6
  22.3 1.1 %collective-permute-done.6.sent = f32[8,24,128]{2,1,0:T(8,128)S(1)} collective-permute-done((f32[8,24,128]{2,1,0:T(8,128)S(1)}, f32[8,24,128]{2,1,0:T(8,128)S(1)}, u32[]{:S(2)}, u32[]{:S(2)}) %collective-permute-start.6) | collective-permute-done | bytes 98336 | tf_op jit(solution)/shard_map/ppermute | solution.py:202
  23.5 1.3 %geocode.1 = f32[3,4,2,1024]{3,2,1,0:T(2,128)} custom-call(f32[8,24,128]{2,1,0:T(8,128)S(1)} %pad_maximum_fusion.held, f32[8,24,128]{2,1,0:T(8,128)S(1)} %collective-permute-done.6.sent, bf16[256,256]{1,0:T(8,128)(2,1)S(1)} %get-tuple-element.19.band, bf16[2048,256]{1,0:T(8,128)(2,1)S(1)} %get-tuple-element.20.onehot, ...), custom_call_target="tpu_custom_call" | custom-call | flops 268435456 | bytes 2097152 | tf_op jit(solution)/shard_map/geocode/pallas_call | solution.py:177
  (4 shorter events, 0.0 us)
Async XLA Ops:
  0.0 10.0 %copy-start = (bf16[2,1,64,1024]{3,2,1,0:T(8,128)(2,1)S(1)}, bf16[2,1,64,1024]{3,2,1,0:T(8,128)(2,1)}, u32[]{:S(2)}) copy-start(bf16[2,1,64,1024]{3,2,1,0:T(8,128)(2,1)} %param.2) | copy-start | bytes 786436
  0.0 10.4 %collective-permute-start.2 = (bf16[2,64,1024]{2,1,0:T(8,128)(2,1)}, bf16[2,64,1024]{2,1,0:T(8,128)(2,1)S(1)}, u32[]{:S(2)}, u32[]{:S(2)}) collective-permute-start(bf16[2,64,1024]{2,1,0:T(8,128)(2,1)} %bitcast.5), channel_id=1, source_target_pairs={{0,8},{2,10},{4,0},{6,2},{8,12},{10,14},{12,4},{14,6},{1,9},{3,11}... | collective-permute-start | bytes 786440 | tf_op jit(solution)/shard_map/ppermute | solution.py:243
  4.0 2.5 %copy-start.1 = (s32[8,128]{1,0:T(8,128)S(1)}, s32[8,128]{1,0:T(8,128)}, u32[]{:S(2)}) copy-start(s32[8,128]{1,0:T(8,128)} %own_cells.1) | copy-start | bytes 12292
  5.0 5.0 %collective-permute-start.1 = (bf16[2,32,1024]{2,1,0:T(8,128)(2,1)S(1)}, bf16[2,32,1024]{2,1,0:T(8,128)(2,1)S(1)}, u32[]{:S(2)}, u32[]{:S(2)}) collective-permute-start(bf16[2,32,1024]{2,1,0:T(8,128)(2,1)S(1)} %dynamic-slice_bitcast_fusion), channel_id=1, source_target_pairs={{0,2},{2,0},{4,6},{6,4},{8,10},{10,8},{12,14},{14,12},{1,3},{3,1},... | collective-permute-start | bytes 393224 | tf_op jit(solution)/shard_map/ppermute | solution.py:245
  6.5 1.2 %collective-permute-start = (s32[8,128]{1,0:T(8,128)S(1)}, s32[8,128]{1,0:T(8,128)S(1)}, u32[]{:S(2)}, u32[]{:S(2)}) collective-permute-start(s32[8,128]{1,0:T(8,128)S(1)} %copy-done.1), channel_id=1, source_target_pairs={{0,1},{1,0},{2,3},{3,2},{4,5},{5,4},{6,7},{7,6},{8,9},{9,8},{10,11... | collective-permute-start | bytes 12296 | tf_op jit(solution)/shard_map/ppermute | solution.py:249
  11.0 4.1 %collective-permute-start.3 = (f32[1,24,128]{2,1,0:T(8,128)S(1)}, f32[1,24,128]{2,1,0:T(8,128)S(1)}, u32[]{:S(2)}, u32[]{:S(2)}) collective-permute-start(f32[1,24,128]{2,1,0:T(8,128)S(1)} %maximum_bitcast_fusion), channel_id=1, source_target_pairs={{0,9},{1,8},{2,11},{3,10},{4,13},{5,12},{6,15},{7,14},{8,1},{9,0},... | collective-permute-start | bytes 36872 | tf_op jit(solution)/shard_map/ppermute | solution.py:195
  15.1 3.3 %collective-permute-start.4 = (f32[2,24,128]{2,1,0:T(8,128)S(1)}, f32[2,24,128]{2,1,0:T(8,128)S(1)}, u32[]{:S(2)}, u32[]{:S(2)}) collective-permute-start(f32[2,24,128]{2,1,0:T(8,128)S(1)} %pad_maximum_fusion.2), channel_id=1, source_target_pairs={{0,5},{1,4},{2,7},{3,6},{4,1},{5,0},{6,3},{7,2},{8,13},{9,12},{10,... | collective-permute-start | bytes 73736 | tf_op jit(solution)/shard_map/ppermute | solution.py:195
  18.4 3.7 %collective-permute-start.5 = (f32[4,24,128]{2,1,0:T(8,128)S(1)}, f32[4,24,128]{2,1,0:T(8,128)S(1)}, u32[]{:S(2)}, u32[]{:S(2)}) collective-permute-start(f32[4,24,128]{2,1,0:T(8,128)S(1)} %pad_maximum_fusion.1), channel_id=1, source_target_pairs={{0,3},{1,2},{2,1},{3,0},{4,7},{5,6},{6,5},{7,4},{8,11},{9,10},{10,... | collective-permute-start | bytes 147464 | tf_op jit(solution)/shard_map/ppermute | solution.py:195
  22.1 1.4 %collective-permute-start.6 = (f32[8,24,128]{2,1,0:T(8,128)S(1)}, f32[8,24,128]{2,1,0:T(8,128)S(1)}, u32[]{:S(2)}, u32[]{:S(2)}) collective-permute-start(f32[8,24,128]{2,1,0:T(8,128)S(1)} %pad_maximum_fusion.held), channel_id=1, source_target_pairs={{0,1},{1,0},{2,3},{3,2},{4,5},{5,4},{6,7},{7,6},{8,9},{9,8},{10,11... | collective-permute-start | bytes 294920 | tf_op jit(solution)/shard_map/ppermute | solution.py:202

commit v5 on v4

--- a/solution.py
+++ b/solution.py
@@ -17,6 +17,7 @@
 WHOLE = ((1, 0), (2, 2), (2, 0), (1, 2))
 MAPC = 16384
 WIDE = 256
+UNIT = 32760.0
 F32 = jnp.float32
 BF16 = jnp.bfloat16
 
@@ -28,50 +29,119 @@
     return high, (value - high.astype(F32)).astype(BF16)
 
 
+def squared(root):
+    root = root.astype(F32)
+    return root * jnp.abs(root)
+
+
 def dot(left, right):
     return jnp.dot(left, right, preferred_element_type=F32)
 
 
-def coherence_kernel(bit, own, other, out):
-    lines, width = own.shape[1:]
-    count = other.shape[1]
-    cells, looks = width // LOOK_R, count // LOOK_A
-    upper = (lax.axis_index("acq") >> bit) & 1
-    rows = pl.ds(pl.multiple_of(upper * count, count), count) if count < lines else slice(None)
-    mine_re, mine_im = own[0, rows, :].astype(F32), own[1, rows, :].astype(F32)
-    their_re, their_im = other[0].astype(F32), other[1].astype(F32)
-    terms = jnp.concatenate(
-        [
-            mine_re * their_re + mine_im * their_im,
-            mine_im * their_re - mine_re * their_im,
-            mine_re * mine_re + mine_im * mine_im,
-            their_re * their_re + their_im * their_im,
-        ],
-        axis=0,
-    )
-    sample = lax.broadcasted_iota(jnp.int32, (width, cells), 0) // LOOK_R
-    cell = lax.broadcasted_iota(jnp.int32, (width, cells), 1)
-    take = (sample == cell).astype(F32).astype(BF16)
+def pick_kernel(own, out):
+    half = out.shape[1]
+    upper = lax.axis_index("acq") & 1
+    out[...] = own[:, pl.ds(pl.multiple_of((1 - upper) * half, half), half), :]
+
+
+def pick(own):
+    parts, lines, width = own.shape
+    return pl.pallas_call(
+        pick_kernel,
+        out_shape=jax.ShapeDtypeStruct((parts, lines // 2, width), own.dtype),
+        in_specs=[VMEM],
+        out_specs=VMEM,
+        name="pick",
+        compiler_params=pltpu.CompilerParams(vmem_limit_bytes=2 * 2**20),
+        cost_estimate=pl.CostEstimate(flops=2**10, bytes_accessed=2**18, transcendentals=0),
+    )(own)
+
+
+def look_sums(terms, take):
     high, low = in_two(terms)
     sums = dot(high, take) + dot(low, take)
-    sums = sums.reshape(4 * looks, LOOK_A, cells).sum(axis=1)
-    power = sums[2 * looks : 3 * looks] * sums[3 * looks :]
-    inverse = lax.rsqrt(power + 1e-06)
-    sign = (1 - 2 * upper).astype(F32)
-    out[...] = sums[: 2 * looks] * jnp.concatenate([inverse, inverse * sign], axis=0)
-
-
-def coherence(bit, own, other):
+    return sums.reshape(terms.shape[0] // LOOK_A, LOOK_A, take.shape[1]).sum(axis=1)
+
+
+def products(mine_re, mine_im, their_re, their_im):
+    return [
+        mine_re * their_re + mine_im * their_im,
+        mine_im * their_re - mine_re * their_im,
+        their_re * their_re + their_im * their_im,
+    ]
+
+
+def normalised(sums, power, sign):
+    looks = power.shape[0]
+    inverse = lax.rsqrt(power * sums[2 * looks :] + 1e-06)
+    return sums[: 2 * looks] * jnp.concatenate([inverse, inverse * sign], axis=0)
+
+
+def first_kernel(own, other, take, out, power):
+    half = other.shape[1]
+    looks = half // LOOK_A
+    mine_re, mine_im = own[0].astype(F32), own[1].astype(F32)
+    power[...] = look_sums(mine_re * mine_re + mine_im * mine_im, take[...])
+    upper = lax.axis_index("acq") & 1
+    rows = pl.ds(pl.multiple_of(upper * half, half), half)
+    terms = products(own[0, rows, :].astype(F32), own[1, rows, :].astype(F32), other[0].astype(F32), other[1].astype(F32))
+    sums = look_sums(jnp.concatenate(terms, axis=0), take[...])
+    mine = jnp.where(upper == 1, power[looks:], power[:looks])
+    out[...] = normalised(sums, mine, (1 - 2 * upper).astype(F32))
+
+
+def first_matching(own, other, take):
     looks, cells = other.shape[1] // LOOK_A, own.shape[2] // LOOK_R
-    return pl.pallas_call(
-        functools.partial(coherence_kernel, bit),
-        out_shape=jax.ShapeDtypeStruct((2 * looks, cells), F32),
-        in_specs=[VMEM, VMEM],
-        out_specs=VMEM,
-        name=f"coherence_{bit}",
+    shape = jax.ShapeDtypeStruct((2 * looks, cells), F32)
+    return pl.pallas_call(
+        first_kernel,
+        out_shape=(shape, shape),
+        in_specs=[VMEM] * 3,
+        out_specs=(VMEM, VMEM),
+        name="first_matching",
         compiler_params=pltpu.CompilerParams(vmem_limit_bytes=4 * 2**20),
         cost_estimate=pl.CostEstimate(flops=2 * 2**20, bytes_accessed=2**18, transcendentals=0),
-    )(own, other)
+    )(own, other, take)
+
+
+def whole_kernel(own, other, take, power, first, out):
+    upper = (lax.axis_index("acq") >> 2) & 1
+    terms = products(own[0].astype(F32), own[1].astype(F32), other[0].astype(F32), other[1].astype(F32))
+    sums = look_sums(jnp.concatenate(terms, axis=0), take[...])
+    whole = normalised(sums, power[...], (1 - 2 * upper).astype(F32))
+    packed = jnp.concatenate([first[...], whole], axis=0)
+    root = jnp.sqrt(jnp.abs(packed)) * UNIT
+    out[...] = jnp.round(jnp.where(packed < 0, -root, root)).astype(jnp.int32).astype(jnp.int16)
+
+
+def whole_pair(own, other, take, power, first):
+    rows, cells = first.shape
+    return pl.pallas_call(
+        whole_kernel,
+        out_shape=jax.ShapeDtypeStruct((3 * rows, cells), jnp.int16),
+        in_specs=[VMEM] * 5,
+        out_specs=VMEM,
+        name="whole_pair",
+        compiler_params=pltpu.CompilerParams(vmem_limit_bytes=4 * 2**20),
+        cost_estimate=pl.CostEstimate(flops=2 * 2**20, bytes_accessed=2**18, transcendentals=0),
+    )(own, other, take, power, first)
+
+
+def take_kernel(take):
+    sample = lax.broadcasted_iota(jnp.int32, take.shape, 0) // LOOK_R
+    cell = lax.broadcasted_iota(jnp.int32, take.shape, 1)
+    take[...] = (sample == cell).astype(F32).astype(BF16)
+
+
+def taking(width):
+    return pl.pallas_call(
+        take_kernel,
+        out_shape=jax.ShapeDtypeStruct((width, width // LOOK_R), BF16),
+        out_specs=VMEM,
+        name="taking",
+        compiler_params=pltpu.CompilerParams(vmem_limit_bytes=2 * 2**20),
+        cost_estimate=pl.CostEstimate(flops=2**17, bytes_accessed=2**18, transcendentals=0),
+    )()
 
 
 def select_kernel(blocks, own_cells, other_cells, band, onehot, masks, scale):
@@ -133,8 +203,8 @@
     for slot in range(BLOCK):
         steps = [mask for i, mask in enumerate(STEPS) if slot >> i & 1]
         acq, side = rank ^ sum(steps), core ^ (len(steps) % 2)
-        by_acq[acq, side] = held[slot]
-        by_acq[acq, 1 - side] = sent[slot]
+        by_acq[acq, side] = squared(held[slot].astype(jnp.int32))
+        by_acq[acq, 1 - side] = squared(sent[slot].astype(jnp.int32))
     for side in range(2):
         columns = slice(side * cols, (side + 1) * cols)
         for acq in range(BLOCK):
@@ -145,7 +215,7 @@
             row = (r * pairs + pair + (acq & 1)) * 2 * lines
             grid[row : row + 2 * lines, columns] = by_acq[acq, side, lines:, :]
     high, low = in_two(grid[...])
-    smooth = (dot(high, band[...]) + dot(low, band[...])) * (1.0 / (HALF_W + 1) ** 2)
+    smooth = (dot(high, band[...]) + dot(low, band[...])) * (1.0 / (UNIT * (HALF_W + 1)) ** 2)
     smooth = smooth.reshape(planes // 2, 2, lines, 2 * cols)
     real, imag = smooth[:, 0], smooth[:, 1]
     gain = lax.rsqrt(jnp.sqrt(real * real + imag * imag + 0.01))
@@ -209,6 +279,7 @@
     lines, looks, width = rows // 3, rows // 6, rng_count * cols
     whole = lax.all_gather(packed, ("acq", "rng")).reshape(acq_count, rng_count, rows, cols)
     whole = whole.transpose(0, 2, 1, 3).reshape(acq_count, rows, width)
+    whole = squared(whole) / UNIT**2
     halves = whole[:, :lines].reshape(pairs, 2, 2, looks, width)
     grids = [halves.transpose(0, 2, 1, 3, 4).reshape(pairs, 2, lines, width)]
     planes = whole[:, lines:].reshape(acq_count // BLOCK, 4, 2, 2, lines, width)
@@ -236,19 +307,18 @@
 
 def per_device(slc, map_cell):
     acq_count = lax.axis_size("acq")
-    acq_rank = lax.axis_index("acq")
     own = slc[:, 0]
-    half = own.shape[1] // 2
     quarter = [(a & -BLOCK) + 2 * SEND[a % BLOCK // 2] + a % 2 for a in range(acq_count)]
     whole = lax.ppermute(own, "acq", list(enumerate(quarter)))
-    part = lax.dynamic_slice_in_dim(own, (1 - acq_rank % 2) * half, half, 1)
-    part = lax.ppermute(part, "acq", [(a, a ^ 1) for a in range(acq_count)])
+    half = lax.ppermute(pick(own), "acq", [(a, a ^ 1) for a in range(acq_count)])
     small = acq_count == BLOCK
+    take = taking(own.shape[2])
     if small:
         blocks = MAPC // (acq_count * lax.axis_size("rng")) // WIDE
         chosen = select(blocks, map_cell, lax.ppermute(map_cell, "rng", [(0, 1), (1, 0)]))
-        own, chosen = lax.optimization_barrier((own, chosen))
-    packed = jnp.concatenate([coherence(0, own, part), coherence(2, own, whole)], axis=0)
+        take, chosen = lax.optimization_barrier((take, chosen))
+    first, power = first_matching(own, half, take)
+    packed = whole_pair(own, whole, take, power, first)
     return gather_small(packed, chosen) if small else gather_large(packed, map_cell)
 
 

time: 24.9 us -> 24.1 us (0.968)
  waiting for transfers between devices: 11.6 us -> 11 us
  starting transfers between devices: 9.11 us -> 8.85 us
    unnamed x4 -> x6, local copies, waits for them, and re-layouts: 0.01 us -> 0.99 us
    dynamic_slice x1 -> x0, local copies, waits for them, and re-layouts: 0.94 us -> none  [per_device(): part = lax.dynamic_slice_in_dim(own, (1 - acq_rank % 2) * half, half, 1)]
    ppermute x3, waiting for transfers between devices: 7.74 us -> 7.32 us  [across(): return lax.ppermute(value, ('acq', 'rng'), pairs)]
    pallas_call x2 -> x4, Pallas kernels: 0.98 us -> 0.96 us  [the longest x1 0.47 us: whole_pair(): pl.pallas_call(whole_kernel, out_shape=jax.ShapeDtypeStruct((3 * rows, ce...]
  transfers between devices with their start and end apart: 7 -> 7, of which waited for: 6 -> 6; matrix products, arithmetic and copies ran while one was open for 4% -> 0% of each run, Pallas kernels for 5% -> 5%
where the time goes in v5:
time: 24.1 us; the launch traced here: 24 us
  waiting for transfers between devices  11 us (46%)
  starting transfers between devices  8.85 us (37%)
  Pallas kernels  3.03 us (13%)
  local copies, waits for them, and re-layouts  0.99 us (4%)
    ppermute x3, waiting for transfers between devices, across(): return lax.ppermute(value, ('acq', 'rng'), pairs)  7.32 us
    ppermute x1, starting transfers between devices, per_device(): whole = lax.ppermute(own, 'acq', list(enumerate(quarter)))  4.04 us
    ppermute x3, starting transfers between devices, across(): return lax.ppermute(value, ('acq', 'rng'), pairs)  3.07 us
    ppermute x1, waiting for transfers between devices, per_device(): lax.ppermute(pick(own), 'acq', [(a, a ^ 1) for a in range(acq_count)])  1.57 us
    ppermute x1, starting transfers between devices, per_device(): lax.ppermute(pick(own), 'acq', [(a, a ^ 1) for a in range(acq_count)])  1.56 us
    pallas_call x1, Pallas kernels, geocode(): pl.pallas_call(geocode_kernel, out_shape=jax.ShapeDtypeStruct((ROUNDS, pa...  1.35 us
    ppermute x1, waiting for transfers between devices, per_device(): lax.ppermute(map_cell, 'rng', [(0, 1), (1, 0)])  1.08 us
    ppermute x1, waiting for transfers between devices, gather_small(): return geocode(held, lax.ppermute(held, 'rng', [(0, 1), (1, 0)]), *chosen)  1.05 us
  transfers between devices with their start and end apart: 7, of which 6 were waited for; matrix products, arithmetic and copies ran while one was open for 0% of the time, Pallas kernels for 5%

profile of v5, /device:TPU:0, one launch (start us, length us, event | category | flops | bytes accessed | tf_op | source)
XLA Modules:
  0.0 24.0 jit_solution(11084416639009454212)
XLA Ops:
  0.0 4.0 %collective-permute-start = (bf16[2,64,1024]{2,1,0:T(8,128)(2,1)}, bf16[2,64,1024]{2,1,0:T(8,128)(2,1)S(1)}, u32[]{:S(2)}, u32[]{:S(2)}) collective-permute-start(bf16[2,64,1024]{2,1,0:T(8,128)(2,1)} %bitcast.2), channel_id=1, source_target_pairs={{0,8},{2,10},{4,0},{6,2},{8,12},{10,14},{12,4},{14,6},{1,9},{3,11}... | collective-permute-start | bytes 786440 | tf_op jit(solution)/shard_map/ppermute | solution.py:312
  4.0 0.0 copy-start
  4.0 1.0 %copy-done = bf16[2,1,64,1024]{3,2,1,0:T(8,128)(2,1)S(1)} copy-done((bf16[2,1,64,1024]{3,2,1,0:T(8,128)(2,1)S(1)}, bf16[2,1,64,1024]{3,2,1,0:T(8,128)(2,1)}, u32[]{:S(2)}) %copy-start) | copy-done | bytes 262168
  5.0 0.0 copy-start.2
  5.0 1.6 %collective-permute-start.2 = (bf16[2,32,1024]{2,1,0:T(8,128)(2,1)S(1)}, bf16[2,32,1024]{2,1,0:T(8,128)(2,1)S(1)}, u32[]{:S(2)}, u32[]{:S(2)}) collective-permute-start(bf16[2,32,1024]{2,1,0:T(8,128)(2,1)S(1)} %pick.1), channel_id=1, source_target_pairs={{0,2},{2,0},{4,6},{6,4},{8,10},{10,8},{12,14},{14,12},{1,3},{3,1},... | collective-permute-start | bytes 393224 | tf_op jit(solution)/shard_map/ppermute | solution.py:313
  6.6 0.0 copy-done.2
  6.6 0.0 collective-permute-start.1
  6.6 0.1 taking.1.take
  6.7 1.1 %collective-permute-done.1.other_cells = s32[8,128]{1,0:T(8,128)S(1)} collective-permute-done((s32[8,128]{1,0:T(8,128)S(1)}, s32[8,128]{1,0:T(8,128)S(1)}, u32[]{:S(2)}, u32[]{:S(2)}) %collective-permute-start.1) | collective-permute-done | bytes 4128 | tf_op jit(solution)/shard_map/ppermute | solution.py:318
  7.8 0.7 %select.1 = (bf16[256,256]{1,0:T(8,128)(2,1)S(1)}, bf16[2048,256]{1,0:T(8,128)(2,1)S(1)}, f32[32,256]{1,0:T(8,128)S(1)}, f32[4,256]{1,0:T(4,128)S(1)}) custom-call(s32[8,128]{1,0:T(8,128)S(1)} %copy-done.2, s32[8,128]{1,0:T(8,128)S(1)} %collective-permute-done.1.other_cells), custom_call_target="tpu_custom_call" | custom-call | flops 2097152 | bytes 1048576 | tf_op jit(solution)/shard_map/select/pallas_call | solution.py:180
  8.5 1.6 %collective-permute-done.2.other = bf16[2,32,1024]{2,1,0:T(8,128)(2,1)S(1)} collective-permute-done((bf16[2,32,1024]{2,1,0:T(8,128)(2,1)S(1)}, bf16[2,32,1024]{2,1,0:T(8,128)(2,1)S(1)}, u32[]{:S(2)}, u32[]{:S(2)}) %collective-permute-start.2) | collective-permute-done | bytes 131104 | tf_op jit(solution)/shard_map/ppermute | solution.py:313
  10.1 0.0 copy-done.1
  10.1 0.4 %first_matching.1 = (f32[8,128]{1,0:T(8,128)S(1)}, f32[8,128]{1,0:T(8,128)S(1)}) custom-call(bf16[2,64,1024]{2,1,0:T(8,128)(2,1)S(1)} %bitcast.4, bf16[2,32,1024]{2,1,0:T(8,128)(2,1)S(1)} %collective-permute-done.2.other, bf16[1024,128]{1,0:T(8,128)(2,1)S(1)} %taking.1.take), custom_call_target="tpu_custom_call" | custom-call | flops 2097152 | bytes 262144 | tf_op jit(solution)/shard_map/first_matching/pallas_call | solution.py:96
  10.5 0.0 collective-permute-done.other
  10.5 0.5 %whole_pair.1 = s16[24,128]{1,0:T(8,128)(2,1)S(1)} custom-call(bf16[2,64,1024]{2,1,0:T(8,128)(2,1)S(1)} %bitcast.5, bf16[2,64,1024]{2,1,0:T(8,128)(2,1)S(1)} %collective-permute-done.other, bf16[1024,128]{1,0:T(8,128)(2,1)S(1)} %taking.1.take, f32[8,128]{1,0:T(8,128)S(1)} %get-tuple-element.21.power, f32[8,128]{1,0:T(8,128)S(1)} %get-tuple-element.22.first), custom_call_target="tpu_custom_call" | custom-call | flops 2097152 | bytes 262144 | tf_op jit(solution)/shard_map/whole_pair/pallas_call | solution.py:119
  11.0 1.3 %collective-permute-start.3 = (s16[1,24,128]{2,1,0:T(8,128)(2,1)S(1)}, s16[1,24,128]{2,1,0:T(8,128)(2,1)S(1)}, u32[]{:S(2)}, u32[]{:S(2)}) collective-permute-start(s16[1,24,128]{2,1,0:T(8,128)(2,1)S(1)} %bitcast.6), channel_id=1, source_target_pairs={{0,9},{1,8},{2,11},{3,10},{4,13},{5,12},{6,15},{7,14},{8,1},{9,0},... | collective-permute-start | bytes 18440 | tf_op jit(solution)/shard_map/ppermute | solution.py:265
  12.3 2.7 %collective-permute-done.3 = s16[1,24,128]{2,1,0:T(8,128)(2,1)S(1)} collective-permute-done((s16[1,24,128]{2,1,0:T(8,128)(2,1)S(1)}, s16[1,24,128]{2,1,0:T(8,128)(2,1)S(1)}, u32[]{:S(2)}, u32[]{:S(2)}) %collective-permute-start.3) | collective-permute-done | bytes 6176 | tf_op jit(solution)/shard_map/ppermute | solution.py:265
  15.0 0.5 %collective-permute-start.4 = (s16[2,24,128]{2,1,0:T(8,128)(2,1)S(1)}, s16[2,24,128]{2,1,0:T(8,128)(2,1)S(1)}, u32[]{:S(2)}, u32[]{:S(2)}) collective-permute-start(s16[2,24,128]{2,1,0:T(8,128)(2,1)S(1)} %pad_add_fusion.2), channel_id=1, source_target_pairs={{0,5},{1,4},{2,7},{3,6},{4,1},{5,0},{6,3},{7,2},{8,13},{9,12},{10,... | collective-permute-start | bytes 36872 | tf_op jit(solution)/shard_map/ppermute | solution.py:265
  15.4 2.7 %collective-permute-done.4 = s16[2,24,128]{2,1,0:T(8,128)(2,1)S(1)} collective-permute-done((s16[2,24,128]{2,1,0:T(8,128)(2,1)S(1)}, s16[2,24,128]{2,1,0:T(8,128)(2,1)S(1)}, u32[]{:S(2)}, u32[]{:S(2)}) %collective-permute-start.4) | collective-permute-done | bytes 12320 | tf_op jit(solution)/shard_map/ppermute | solution.py:265
  18.1 1.3 %collective-permute-start.5 = (s16[4,24,128]{2,1,0:T(8,128)(2,1)S(1)}, s16[4,24,128]{2,1,0:T(8,128)(2,1)S(1)}, u32[]{:S(2)}, u32[]{:S(2)}) collective-permute-start(s16[4,24,128]{2,1,0:T(8,128)(2,1)S(1)} %pad_add_fusion.1), channel_id=1, source_target_pairs={{0,3},{1,2},{2,1},{3,0},{4,7},{5,6},{6,5},{7,4},{8,11},{9,10},{10,... | collective-permute-start | bytes 73736 | tf_op jit(solution)/shard_map/ppermute | solution.py:265
  19.4 2.0 %collective-permute-done.5 = s16[4,24,128]{2,1,0:T(8,128)(2,1)S(1)} collective-permute-done((s16[4,24,128]{2,1,0:T(8,128)(2,1)S(1)}, s16[4,24,128]{2,1,0:T(8,128)(2,1)S(1)}, u32[]{:S(2)}, u32[]{:S(2)}) %collective-permute-start.5) | collective-permute-done | bytes 24608 | tf_op jit(solution)/shard_map/ppermute | solution.py:265
  21.4 0.2 collective-permute-start.6
  21.6 1.1 %collective-permute-done.6.sent = s16[8,24,128]{2,1,0:T(8,128)(2,1)S(1)} collective-permute-done((s16[8,24,128]{2,1,0:T(8,128)(2,1)S(1)}, s16[8,24,128]{2,1,0:T(8,128)(2,1)S(1)}, u32[]{:S(2)}, u32[]{:S(2)}) %collective-permute-start.6) | collective-permute-done | bytes 49184 | tf_op jit(solution)/shard_map/ppermute | solution.py:272
  22.6 1.3 %geocode.1 = f32[3,4,2,1024]{3,2,1,0:T(2,128)} custom-call(s16[8,24,128]{2,1,0:T(8,128)(2,1)S(1)} %pad_add_fusion.held, s16[8,24,128]{2,1,0:T(8,128)(2,1)S(1)} %collective-permute-done.6.sent, bf16[256,256]{1,0:T(8,128)(2,1)S(1)} %get-tuple-element.23.band, bf16[2048,256]{1,0:T(8,128)(2,1)S(1)} %get-tuple-element.24.onehot, ...), custom_call_target="tpu_custom_call" | custom-call | flops 268435456 | bytes 2097152 | tf_op jit(solution)/shard_map/geocode/pallas_call | solution.py:247
  (5 shorter events, 0.0 us)
Async XLA Ops:
  0.0 10.5 %collective-permute-start = (bf16[2,64,1024]{2,1,0:T(8,128)(2,1)}, bf16[2,64,1024]{2,1,0:T(8,128)(2,1)S(1)}, u32[]{:S(2)}, u32[]{:S(2)}) collective-permute-start(bf16[2,64,1024]{2,1,0:T(8,128)(2,1)} %bitcast.2), channel_id=1, source_target_pairs={{0,8},{2,10},{4,0},{6,2},{8,12},{10,14},{12,4},{14,6},{1,9},{3,11}... | collective-permute-start | bytes 786440 | tf_op jit(solution)/shard_map/ppermute | solution.py:312
  4.0 1.0 %copy-start = (bf16[2,1,64,1024]{3,2,1,0:T(8,128)(2,1)S(1)}, bf16[2,1,64,1024]{3,2,1,0:T(8,128)(2,1)}, u32[]{:S(2)}) copy-start(bf16[2,1,64,1024]{3,2,1,0:T(8,128)(2,1)} %param.2) | copy-start | bytes 786436
  5.0 1.6 %copy-start.2 = (s32[8,128]{1,0:T(8,128)S(1)}, s32[8,128]{1,0:T(8,128)}, u32[]{:S(2)}) copy-start(s32[8,128]{1,0:T(8,128)} %own_cells.1) | copy-start | bytes 12292
  5.0 5.1 %copy-start.1 = (bf16[2,1,64,1024]{3,2,1,0:T(8,128)(2,1)S(1)}, bf16[2,1,64,1024]{3,2,1,0:T(8,128)(2,1)}, u32[]{:S(2)}) copy-start(bf16[2,1,64,1024]{3,2,1,0:T(8,128)(2,1)} %param.2) | copy-start | bytes 786436
  5.0 5.0 %collective-permute-start.2 = (bf16[2,32,1024]{2,1,0:T(8,128)(2,1)S(1)}, bf16[2,32,1024]{2,1,0:T(8,128)(2,1)S(1)}, u32[]{:S(2)}, u32[]{:S(2)}) collective-permute-start(bf16[2,32,1024]{2,1,0:T(8,128)(2,1)S(1)} %pick.1), channel_id=1, source_target_pairs={{0,2},{2,0},{4,6},{6,4},{8,10},{10,8},{12,14},{14,12},{1,3},{3,1},... | collective-permute-start | bytes 393224 | tf_op jit(solution)/shard_map/ppermute | solution.py:313
  6.6 1.2 %collective-permute-start.1 = (s32[8,128]{1,0:T(8,128)S(1)}, s32[8,128]{1,0:T(8,128)S(1)}, u32[]{:S(2)}, u32[]{:S(2)}) collective-permute-start(s32[8,128]{1,0:T(8,128)S(1)} %copy-done.2), channel_id=1, source_target_pairs={{0,1},{1,0},{2,3},{3,2},{4,5},{5,4},{6,7},{7,6},{8,9},{9,8},{10,11... | collective-permute-start | bytes 12296 | tf_op jit(solution)/shard_map/ppermute | solution.py:318
  11.0 4.0 %collective-permute-start.3 = (s16[1,24,128]{2,1,0:T(8,128)(2,1)S(1)}, s16[1,24,128]{2,1,0:T(8,128)(2,1)S(1)}, u32[]{:S(2)}, u32[]{:S(2)}) collective-permute-start(s16[1,24,128]{2,1,0:T(8,128)(2,1)S(1)} %bitcast.6), channel_id=1, source_target_pairs={{0,9},{1,8},{2,11},{3,10},{4,13},{5,12},{6,15},{7,14},{8,1},{9,0},... | collective-permute-start | bytes 18440 | tf_op jit(solution)/shard_map/ppermute | solution.py:265
  15.0 3.1 %collective-permute-start.4 = (s16[2,24,128]{2,1,0:T(8,128)(2,1)S(1)}, s16[2,24,128]{2,1,0:T(8,128)(2,1)S(1)}, u32[]{:S(2)}, u32[]{:S(2)}) collective-permute-start(s16[2,24,128]{2,1,0:T(8,128)(2,1)S(1)} %pad_add_fusion.2), channel_id=1, source_target_pairs={{0,5},{1,4},{2,7},{3,6},{4,1},{5,0},{6,3},{7,2},{8,13},{9,12},{10,... | collective-permute-start | bytes 36872 | tf_op jit(solution)/shard_map/ppermute | solution.py:265
  18.1 3.3 %collective-permute-start.5 = (s16[4,24,128]{2,1,0:T(8,128)(2,1)S(1)}, s16[4,24,128]{2,1,0:T(8,128)(2,1)S(1)}, u32[]{:S(2)}, u32[]{:S(2)}) collective-permute-start(s16[4,24,128]{2,1,0:T(8,128)(2,1)S(1)} %pad_add_fusion.1), channel_id=1, source_target_pairs={{0,3},{1,2},{2,1},{3,0},{4,7},{5,6},{6,5},{7,4},{8,11},{9,10},{10,... | collective-permute-start | bytes 73736 | tf_op jit(solution)/shard_map/ppermute | solution.py:265
  21.4 1.2 %collective-permute-start.6 = (s16[8,24,128]{2,1,0:T(8,128)(2,1)S(1)}, s16[8,24,128]{2,1,0:T(8,128)(2,1)S(1)}, u32[]{:S(2)}, u32[]{:S(2)}) collective-permute-start(s16[8,24,128]{2,1,0:T(8,128)(2,1)S(1)} %pad_add_fusion.held), channel_id=1, source_target_pairs={{0,1},{1,0},{2,3},{3,2},{4,5},{5,4},{6,7},{7,6},{8,9},{9,8},{10,11... | collective-permute-start | bytes 147464 | tf_op jit(solution)/shard_map/ppermute | solution.py:272

commit v6 on v5

--- a/solution.py
+++ b/solution.py
@@ -12,10 +12,11 @@
 HALF_W = 4
 ROUNDS = 3
 BLOCK = 2**ROUNDS
-STEPS = (4, 2, 1)
+STEPS = ((1,), (6, 4, 2))
 SEND = (2, 0, 3, 1)
 WHOLE = ((1, 0), (2, 2), (2, 0), (1, 2))
 MAPC = 16384
+LANES = 128
 WIDE = 256
 UNIT = 32760.0
 F32 = jnp.float32
@@ -24,18 +25,20 @@
 VMEM = pl.BlockSpec(memory_space=pltpu.VMEM)
 
 
-def in_two(value):
-    high = value.astype(BF16)
-    return high, (value - high.astype(F32)).astype(BF16)
+def dot(left, right):
+    return jnp.dot(left, right, preferred_element_type=F32)
+
+
+def dot_in_two(left, right):
+    rows = left.shape[0]
+    high = left.astype(BF16).astype(F32)
+    both = dot(jnp.concatenate([high, left - high], axis=0).astype(BF16), right)
+    return both[:rows] + both[rows:]
 
 
 def squared(root):
     root = root.astype(F32)
     return root * jnp.abs(root)
-
-
-def dot(left, right):
-    return jnp.dot(left, right, preferred_element_type=F32)
 
 
 def pick_kernel(own, out):
@@ -58,8 +61,7 @@
 
 
 def look_sums(terms, take):
-    high, low = in_two(terms)
-    sums = dot(high, take) + dot(low, take)
+    sums = dot_in_two(terms, take)
     return sums.reshape(terms.shape[0] // LOOK_A, LOOK_A, take.shape[1]).sum(axis=1)
 
 
@@ -77,54 +79,79 @@
     return sums[: 2 * looks] * jnp.concatenate([inverse, inverse * sign], axis=0)
 
 
-def first_kernel(own, other, take, out, power):
+def spread(samples, part, wide, out):
+    blocks, looks = wide.shape[1], out.shape[3]
+    for j in range(blocks):
+        wide[part, j] = samples[part, :, j * LANES : (j + 1) * LANES].astype(F32)
+        for i in range(LOOK_A):
+            out[part, j, i] = wide[part, j, pl.ds(i, looks, stride=LOOK_A), :]
+
+
+def first_kernel(own, other, take, out, power, mine, wide):
     half = other.shape[1]
     looks = half // LOOK_A
-    mine_re, mine_im = own[0].astype(F32), own[1].astype(F32)
-    power[...] = look_sums(mine_re * mine_re + mine_im * mine_im, take[...])
+    own_re, own_im = own[0].astype(F32), own[1].astype(F32)
+    power[...] = look_sums(own_re * own_re + own_im * own_im, take[...])
     upper = lax.axis_index("acq") & 1
     rows = pl.ds(pl.multiple_of(upper * half, half), half)
     terms = products(own[0, rows, :].astype(F32), own[1, rows, :].astype(F32), other[0].astype(F32), other[1].astype(F32))
     sums = look_sums(jnp.concatenate(terms, axis=0), take[...])
-    mine = jnp.where(upper == 1, power[looks:], power[:looks])
-    out[...] = normalised(sums, mine, (1 - 2 * upper).astype(F32))
+    half_power = jnp.where(upper == 1, power[looks:], power[:looks])
+    out[...] = normalised(sums, half_power, (1 - 2 * upper).astype(F32))
+    for part in range(2):
+        spread(own, part, wide, mine)
 
 
 def first_matching(own, other, take):
-    looks, cells = other.shape[1] // LOOK_A, own.shape[2] // LOOK_R
-    shape = jax.ShapeDtypeStruct((2 * looks, cells), F32)
+    parts, lines, width = own.shape
+    looks, cells = lines // LOOK_A, width // LOOK_R
+    blocks = width // LANES
+    shape = jax.ShapeDtypeStruct((looks, cells), F32)
     return pl.pallas_call(
         first_kernel,
-        out_shape=(shape, shape),
+        out_shape=(shape, shape, jax.ShapeDtypeStruct((parts, blocks, LOOK_A, looks, LANES), F32)),
         in_specs=[VMEM] * 3,
-        out_specs=(VMEM, VMEM),
+        out_specs=(VMEM,) * 3,
+        scratch_shapes=[pltpu.VMEM((parts, blocks, lines, LANES), F32)],
         name="first_matching",
         compiler_params=pltpu.CompilerParams(vmem_limit_bytes=4 * 2**20),
         cost_estimate=pl.CostEstimate(flops=2 * 2**20, bytes_accessed=2**18, transcendentals=0),
     )(own, other, take)
 
 
-def whole_kernel(own, other, take, power, first, out):
+def whole_kernel(mine, other, take, power, first, out, wide):
     upper = (lax.axis_index("acq") >> 2) & 1
-    terms = products(own[0].astype(F32), own[1].astype(F32), other[0].astype(F32), other[1].astype(F32))
-    sums = look_sums(jnp.concatenate(terms, axis=0), take[...])
+    blocks, looks = mine.shape[1], mine.shape[3]
+    columns = []
+    for j in range(blocks):
+        for part in range(2):
+            wide[part, j] = other[part, :, j * LANES : (j + 1) * LANES].astype(F32)
+        total = 0.0
+        for i in range(LOOK_A):
+            their_re, their_im = (wide[part, j, pl.ds(i, looks, stride=LOOK_A), :] for part in range(2))
+            terms = products(mine[0, j, i], mine[1, j, i], their_re, their_im)
+            total = total + jnp.concatenate(terms, axis=0)
+        columns.append(total)
+    sums = dot_in_two(jnp.concatenate(columns, axis=1), take[...])
     whole = normalised(sums, power[...], (1 - 2 * upper).astype(F32))
     packed = jnp.concatenate([first[...], whole], axis=0)
     root = jnp.sqrt(jnp.abs(packed)) * UNIT
     out[...] = jnp.round(jnp.where(packed < 0, -root, root)).astype(jnp.int32).astype(jnp.int16)
 
 
-def whole_pair(own, other, take, power, first):
+def whole_pair(mine, other, take, power, first):
     rows, cells = first.shape
+    parts, lines, width = other.shape
     return pl.pallas_call(
         whole_kernel,
         out_shape=jax.ShapeDtypeStruct((3 * rows, cells), jnp.int16),
         in_specs=[VMEM] * 5,
         out_specs=VMEM,
+        scratch_shapes=[pltpu.VMEM((parts, width // LANES, lines, LANES), F32)],
         name="whole_pair",
         compiler_params=pltpu.CompilerParams(vmem_limit_bytes=4 * 2**20),
         cost_estimate=pl.CostEstimate(flops=2 * 2**20, bytes_accessed=2**18, transcendentals=0),
-    )(own, other, take, power, first)
+    )(mine, other, take, power, first)
 
 
 def take_kernel(take):
@@ -200,9 +227,11 @@
     planes = ROUNDS * pairs * 2
     blocks = scale.shape[0]
     rank, core = lax.axis_index("acq"), lax.axis_index("rng")
-    for slot in range(BLOCK):
-        steps = [mask for i, mask in enumerate(STEPS) if slot >> i & 1]
-        acq, side = rank ^ sum(steps), core ^ (len(steps) % 2)
+    origins = [(0, 0)]
+    for step in STEPS:
+        origins = origins + [(bits ^ mask, 1 - other) for mask in step for bits, other in origins]
+    for slot, (bits, other) in enumerate(origins):
+        acq, side = rank ^ bits, core ^ other
         by_acq[acq, side] = squared(held[slot].astype(jnp.int32))
         by_acq[acq, 1 - side] = squared(sent[slot].astype(jnp.int32))
     for side in range(2):
@@ -214,8 +243,7 @@
             r, pair = WHOLE[acq >> 1]
             row = (r * pairs + pair + (acq & 1)) * 2 * lines
             grid[row : row + 2 * lines, columns] = by_acq[acq, side, lines:, :]
-    high, low = in_two(grid[...])
-    smooth = (dot(high, band[...]) + dot(low, band[...])) * (1.0 / (UNIT * (HALF_W + 1)) ** 2)
+    smooth = dot_in_two(grid[...], band[...]) * (1.0 / (UNIT * (HALF_W + 1)) ** 2)
     smooth = smooth.reshape(planes // 2, 2, lines, 2 * cols)
     real, imag = smooth[:, 0], smooth[:, 1]
     gain = lax.rsqrt(jnp.sqrt(real * real + imag * imag + 0.01))
@@ -267,8 +295,8 @@
 
 def gather_small(packed, chosen):
     held = packed[None]
-    for mask in STEPS:
-        held = jnp.concatenate([held, across(held, mask)], axis=0)
+    for step in STEPS:
+        held = jnp.concatenate([held] + [across(held, mask) for mask in step], axis=0)
     return geocode(held, lax.ppermute(held, "rng", [(0, 1), (1, 0)]), *chosen)
 
 
@@ -317,8 +345,8 @@
         blocks = MAPC // (acq_count * lax.axis_size("rng")) // WIDE
         chosen = select(blocks, map_cell, lax.ppermute(map_cell, "rng", [(0, 1), (1, 0)]))
         take, chosen = lax.optimization_barrier((take, chosen))
-    first, power = first_matching(own, half, take)
-    packed = whole_pair(own, whole, take, power, first)
+    first, power, mine = first_matching(own, half, take)
+    packed = whole_pair(mine, whole, take, power, first)
     return gather_small(packed, chosen) if small else gather_large(packed, map_cell)
 
 

time: 24.1 us -> 23.4 us (0.971)
  waiting for transfers between devices: 11 us -> 9.29 us
  starting transfers between devices: 8.85 us -> 9.98 us
    ppermute x3 -> x4, waiting for transfers between devices: 7.32 us -> 5.75 us  [across(): return lax.ppermute(value, ('acq', 'rng'), pairs)]
    ppermute x3 -> x4, starting transfers between devices: 3.07 us -> 3.9 us  [across(): return lax.ppermute(value, ('acq', 'rng'), pairs)]
    ppermute x1, starting transfers between devices: 0.18 us -> 0.49 us  [gather_small(): return geocode(held, lax.ppermute(held, 'rng', [(0, 1), (1, 0)]), *chosen)]
    unnamed x6 -> x10, local copies, waits for them, and re-layouts: 0.99 us -> 1.02 us
  transfers between devices with their start and end apart: 7 -> 8, of which waited for: 6 -> 6; matrix products, arithmetic and copies ran while one was open for 0% -> 0% of each run, Pallas kernels for 5% -> 5%
where the time goes in v6:
time: 23.4 us; the launch traced here: 23.3 us
  starting transfers between devices  9.98 us (43%)
  waiting for transfers between devices  9.29 us (40%)
  Pallas kernels  2.93 us (13%)
  local copies, waits for them, and re-layouts  1.02 us (4%)
    ppermute x4, waiting for transfers between devices, across(): return lax.ppermute(value, ('acq', 'rng'), pairs)  5.75 us
    ppermute x1, starting transfers between devices, per_device(): whole = lax.ppermute(own, 'acq', list(enumerate(quarter)))  4.04 us
    ppermute x4, starting transfers between devices, across(): return lax.ppermute(value, ('acq', 'rng'), pairs)  3.9 us
    ppermute x1, waiting for transfers between devices, per_device(): lax.ppermute(pick(own), 'acq', [(a, a ^ 1) for a in range(acq_count)])  1.57 us
    ppermute x1, starting transfers between devices, per_device(): lax.ppermute(pick(own), 'acq', [(a, a ^ 1) for a in range(acq_count)])  1.56 us
    pallas_call x1, Pallas kernels, geocode(): pl.pallas_call(geocode_kernel, out_shape=jax.ShapeDtypeStruct((ROUNDS, pa...  1.34 us
    ppermute x1, waiting for transfers between devices, per_device(): lax.ppermute(map_cell, 'rng', [(0, 1), (1, 0)])  1.08 us
    unnamed x10, local copies, waits for them, and re-layouts  1.02 us
  transfers between devices with their start and end apart: 8, of which 6 were waited for; matrix products, arithmetic and copies ran while one was open for 0% of the time, Pallas kernels for 5%

profile of v6, /device:TPU:0, one launch (start us, length us, event | category | flops | bytes accessed | tf_op | source)
XLA Modules:
  0.0 23.3 jit_solution(636712226447017209)
XLA Ops:
  0.0 4.0 %collective-permute-start.2 = (bf16[2,64,1024]{2,1,0:T(8,128)(2,1)}, bf16[2,64,1024]{2,1,0:T(8,128)(2,1)S(1)}, u32[]{:S(2)}, u32[]{:S(2)}) collective-permute-start(bf16[2,64,1024]{2,1,0:T(8,128)(2,1)} %bitcast.3), channel_id=1, source_target_pairs={{0,8},{2,10},{4,0},{6,2},{8,12},{10,14},{12,4},{14,6},{1,9},{3,11}... | collective-permute-start | bytes 786440 | tf_op jit(solution)/shard_map/ppermute | solution.py:340
  4.0 1.0 %copy-done = bf16[2,1,64,1024]{3,2,1,0:T(8,128)(2,1)S(1)} copy-done((bf16[2,1,64,1024]{3,2,1,0:T(8,128)(2,1)S(1)}, bf16[2,1,64,1024]{3,2,1,0:T(8,128)(2,1)}, u32[]{:S(2)}) %copy-start) | copy-done | bytes 262168
  5.0 1.6 %collective-permute-start = (bf16[2,32,1024]{2,1,0:T(8,128)(2,1)S(1)}, bf16[2,32,1024]{2,1,0:T(8,128)(2,1)S(1)}, u32[]{:S(2)}, u32[]{:S(2)}) collective-permute-start(bf16[2,32,1024]{2,1,0:T(8,128)(2,1)S(1)} %pick.1), channel_id=1, source_target_pairs={{0,2},{2,0},{4,6},{6,4},{8,10},{10,8},{12,14},{14,12},{1,3},{3,1},... | collective-permute-start | bytes 393224 | tf_op jit(solution)/shard_map/ppermute | solution.py:341
  6.6 0.0 copy-done.2
  6.6 0.0 collective-permute-start.1
  6.6 0.1 taking.1.take
  6.7 1.1 %collective-permute-done.1.other_cells = s32[8,128]{1,0:T(8,128)S(1)} collective-permute-done((s32[8,128]{1,0:T(8,128)S(1)}, s32[8,128]{1,0:T(8,128)S(1)}, u32[]{:S(2)}, u32[]{:S(2)}) %collective-permute-start.1) | collective-permute-done | bytes 4128 | tf_op jit(solution)/shard_map/ppermute | solution.py:346
  7.8 0.7 %select.1 = (bf16[256,256]{1,0:T(8,128)(2,1)S(1)}, bf16[2048,256]{1,0:T(8,128)(2,1)S(1)}, f32[32,256]{1,0:T(8,128)S(1)}, f32[4,256]{1,0:T(4,128)S(1)}) custom-call(s32[8,128]{1,0:T(8,128)S(1)} %copy-done.2, s32[8,128]{1,0:T(8,128)S(1)} %collective-permute-done.1.other_cells), custom_call_target="tpu_custom_call" | custom-call | flops 2097152 | bytes 1048576 | tf_op jit(solution)/shard_map/select/pallas_call | solution.py:207
  8.5 1.6 %collective-permute-done.other = bf16[2,32,1024]{2,1,0:T(8,128)(2,1)S(1)} collective-permute-done((bf16[2,32,1024]{2,1,0:T(8,128)(2,1)S(1)}, bf16[2,32,1024]{2,1,0:T(8,128)(2,1)S(1)}, u32[]{:S(2)}, u32[]{:S(2)}) %collective-permute-start) | collective-permute-done | bytes 131104 | tf_op jit(solution)/shard_map/ppermute | solution.py:341
  10.1 0.0 copy-done.1
  10.1 0.4 %first_matching.1 = (f32[8,128]{1,0:T(8,128)S(1)}, f32[8,128]{1,0:T(8,128)S(1)}, f32[2,8,8,8,128]{4,3,2,1,0:T(8,128)S(1)}) custom-call(bf16[2,64,1024]{2,1,0:T(8,128)(2,1)S(1)} %bitcast.5, bf16[2,32,1024]{2,1,0:T(8,128)(2,1)S(1)} %collective-permute-done.other, bf16[1024,128]{1,0:T(8,128)(2,1)S(1)} %taking.1.take), custom_call_target="tpu_custom_call" | custom-call | flops 2097152 | bytes 262144 | tf_op jit(solution)/shard_map/first_matching/pallas_call | solution.py:110
  10.5 0.0 collective-permute-done.2.other
  10.5 0.3 %whole_pair.1 = s16[24,128]{1,0:T(8,128)(2,1)S(1)} custom-call(f32[2,8,8,8,128]{4,3,2,1,0:T(8,128)S(1)} %get-tuple-element.22.mine, bf16[2,64,1024]{2,1,0:T(8,128)(2,1)S(1)} %collective-permute-done.2.other, bf16[1024,128]{1,0:T(8,128)(2,1)S(1)} %taking.1.take, f32[8,128]{1,0:T(8,128)S(1)} %get-tuple-element.23.power, f32[8,128]{1,0:T(8,128)S(1)} %get-tuple-element.24.first), custom_call_target="tpu_custom_call" | custom-call | flops 2097152 | bytes 262144 | tf_op jit(solution)/shard_map/whole_pair/pallas_call | solution.py:145
  10.9 0.1 collective-permute-start.3
  11.0 3.0 %collective-permute-done.3 = s16[1,24,128]{2,1,0:T(8,128)(2,1)S(1)} collective-permute-done((s16[1,24,128]{2,1,0:T(8,128)(2,1)S(1)}, s16[1,24,128]{2,1,0:T(8,128)(2,1)S(1)}, u32[]{:S(2)}, u32[]{:S(2)}) %collective-permute-start.3) | collective-permute-done | bytes 6176 | tf_op jit(solution)/shard_map/ppermute | solution.py:293
  14.0 2.5 %collective-permute-start.4 = (s16[2,24,128]{2,1,0:T(8,128)(2,1)S(1)}, s16[2,24,128]{2,1,0:T(8,128)(2,1)S(1)}, u32[]{:S(2)}, u32[]{:S(2)}) collective-permute-start(s16[2,24,128]{2,1,0:T(8,128)(2,1)S(1)} %pad_add_fusion), channel_id=1, source_target_pairs={{0,13},{1,12},{2,15},{3,14},{4,9},{5,8},{6,11},{7,10},{8,5},{9,4},... | collective-permute-start | bytes 36872 | tf_op jit(solution)/shard_map/ppermute | solution.py:293
  16.5 0.4 %collective-permute-start.5 = (s16[2,24,128]{2,1,0:T(8,128)(2,1)S(1)}, s16[2,24,128]{2,1,0:T(8,128)(2,1)S(1)}, u32[]{:S(2)}, u32[]{:S(2)}) collective-permute-start(s16[2,24,128]{2,1,0:T(8,128)(2,1)S(1)} %pad_add_fusion), channel_id=1, source_target_pairs={{0,9},{1,8},{2,11},{3,10},{4,13},{5,12},{6,15},{7,14},{8,1},{9,0},... | collective-permute-start | bytes 36872 | tf_op jit(solution)/shard_map/ppermute | solution.py:293
  16.9 0.9 %collective-permute-start.6 = (s16[2,24,128]{2,1,0:T(8,128)(2,1)S(1)}, s16[2,24,128]{2,1,0:T(8,128)(2,1)S(1)}, u32[]{:S(2)}, u32[]{:S(2)}) collective-permute-start(s16[2,24,128]{2,1,0:T(8,128)(2,1)S(1)} %pad_add_fusion), channel_id=1, source_target_pairs={{0,5},{1,4},{2,7},{3,6},{4,1},{5,0},{6,3},{7,2},{8,13},{9,12},{10,... | collective-permute-start | bytes 36872 | tf_op jit(solution)/shard_map/ppermute | solution.py:293
  17.8 1.1 %collective-permute-done.4 = s16[2,24,128]{2,1,0:T(8,128)(2,1)S(1)} collective-permute-done((s16[2,24,128]{2,1,0:T(8,128)(2,1)S(1)}, s16[2,24,128]{2,1,0:T(8,128)(2,1)S(1)}, u32[]{:S(2)}, u32[]{:S(2)}) %collective-permute-start.4) | collective-permute-done | bytes 12320 | tf_op jit(solution)/shard_map/ppermute | solution.py:293
  18.9 1.6 %collective-permute-done.5 = s16[2,24,128]{2,1,0:T(8,128)(2,1)S(1)} collective-permute-done((s16[2,24,128]{2,1,0:T(8,128)(2,1)S(1)}, s16[2,24,128]{2,1,0:T(8,128)(2,1)S(1)}, u32[]{:S(2)}, u32[]{:S(2)}) %collective-permute-start.5) | collective-permute-done | bytes 12320 | tf_op jit(solution)/shard_map/ppermute | solution.py:293
  20.6 0.0 collective-permute-done.6
  20.6 0.5 %collective-permute-start.7 = (s16[8,24,128]{2,1,0:T(8,128)(2,1)S(1)}, s16[8,24,128]{2,1,0:T(8,128)(2,1)S(1)}, u32[]{:S(2)}, u32[]{:S(2)}) collective-permute-start(s16[8,24,128]{2,1,0:T(8,128)(2,1)S(1)} %constant_dynamic-update-slice_fusion.held), channel_id=1, source_target_pairs={{0,1},{1,0},{2,3},{3,2},{4,5},{5,4},{6,7},{7,6},{8,9},{9,8},{10,11... | collective-permute-start | bytes 147464 | tf_op jit(solution)/shard_map/ppermute | solution.py:300
  21.1 0.9 %collective-permute-done.7.sent = s16[8,24,128]{2,1,0:T(8,128)(2,1)S(1)} collective-permute-done((s16[8,24,128]{2,1,0:T(8,128)(2,1)S(1)}, s16[8,24,128]{2,1,0:T(8,128)(2,1)S(1)}, u32[]{:S(2)}, u32[]{:S(2)}) %collective-permute-start.7) | collective-permute-done | bytes 49184 | tf_op jit(solution)/shard_map/ppermute | solution.py:300
  21.9 1.3 %geocode.1 = f32[3,4,2,1024]{3,2,1,0:T(2,128)} custom-call(s16[8,24,128]{2,1,0:T(8,128)(2,1)S(1)} %constant_dynamic-update-slice_fusion.held, s16[8,24,128]{2,1,0:T(8,128)(2,1)S(1)} %collective-permute-done.7.sent, bf16[256,256]{1,0:T(8,128)(2,1)S(1)} %get-tuple-element.25.band, bf16[2048,256]{1,0:T(8,128)(2,1)S(1)} %get-tuple-element.26.onehot, ...), custom_call_target="tpu_custom_call" | custom-call | flops 268435456 | bytes 2097152 | tf_op jit(solution)/shard_map/geocode/pallas_call | solution.py:275
  (10 shorter events, 0.1 us)
Async XLA Ops:
  0.0 10.5 %collective-permute-start.2 = (bf16[2,64,1024]{2,1,0:T(8,128)(2,1)}, bf16[2,64,1024]{2,1,0:T(8,128)(2,1)S(1)}, u32[]{:S(2)}, u32[]{:S(2)}) collective-permute-start(bf16[2,64,1024]{2,1,0:T(8,128)(2,1)} %bitcast.3), channel_id=1, source_target_pairs={{0,8},{2,10},{4,0},{6,2},{8,12},{10,14},{12,4},{14,6},{1,9},{3,11}... | collective-permute-start | bytes 786440 | tf_op jit(solution)/shard_map/ppermute | solution.py:340
  4.0 1.0 %copy-start = (bf16[2,1,64,1024]{3,2,1,0:T(8,128)(2,1)S(1)}, bf16[2,1,64,1024]{3,2,1,0:T(8,128)(2,1)}, u32[]{:S(2)}) copy-start(bf16[2,1,64,1024]{3,2,1,0:T(8,128)(2,1)} %param.2) | copy-start | bytes 786436
  5.0 1.6 %copy-start.2 = (s32[8,128]{1,0:T(8,128)S(1)}, s32[8,128]{1,0:T(8,128)}, u32[]{:S(2)}) copy-start(s32[8,128]{1,0:T(8,128)} %own_cells.1) | copy-start | bytes 12292
  5.0 5.1 %copy-start.1 = (bf16[2,1,64,1024]{3,2,1,0:T(8,128)(2,1)S(1)}, bf16[2,1,64,1024]{3,2,1,0:T(8,128)(2,1)}, u32[]{:S(2)}) copy-start(bf16[2,1,64,1024]{3,2,1,0:T(8,128)(2,1)} %param.2) | copy-start | bytes 786436
  5.0 5.0 %collective-permute-start = (bf16[2,32,1024]{2,1,0:T(8,128)(2,1)S(1)}, bf16[2,32,1024]{2,1,0:T(8,128)(2,1)S(1)}, u32[]{:S(2)}, u32[]{:S(2)}) collective-permute-start(bf16[2,32,1024]{2,1,0:T(8,128)(2,1)S(1)} %pick.1), channel_id=1, source_target_pairs={{0,2},{2,0},{4,6},{6,4},{8,10},{10,8},{12,14},{14,12},{1,3},{3,1},... | collective-permute-start | bytes 393224 | tf_op jit(solution)/shard_map/ppermute | solution.py:341
  6.6 1.2 %collective-permute-start.1 = (s32[8,128]{1,0:T(8,128)S(1)}, s32[8,128]{1,0:T(8,128)S(1)}, u32[]{:S(2)}, u32[]{:S(2)}) collective-permute-start(s32[8,128]{1,0:T(8,128)S(1)} %copy-done.2), channel_id=1, source_target_pairs={{0,1},{1,0},{2,3},{3,2},{4,5},{5,4},{6,7},{7,6},{8,9},{9,8},{10,11... | collective-permute-start | bytes 12296 | tf_op jit(solution)/shard_map/ppermute | solution.py:346
  10.9 3.1 %collective-permute-start.3 = (s16[1,24,128]{2,1,0:T(8,128)(2,1)S(1)}, s16[1,24,128]{2,1,0:T(8,128)(2,1)S(1)}, u32[]{:S(2)}, u32[]{:S(2)}) collective-permute-start(s16[1,24,128]{2,1,0:T(8,128)(2,1)S(1)} %bitcast.6), channel_id=1, source_target_pairs={{0,3},{1,2},{2,1},{3,0},{4,7},{5,6},{6,5},{7,4},{8,11},{9,10},{10,... | collective-permute-start | bytes 18440 | tf_op jit(solution)/shard_map/ppermute | solution.py:293
  14.0 4.9 %collective-permute-start.4 = (s16[2,24,128]{2,1,0:T(8,128)(2,1)S(1)}, s16[2,24,128]{2,1,0:T(8,128)(2,1)S(1)}, u32[]{:S(2)}, u32[]{:S(2)}) collective-permute-start(s16[2,24,128]{2,1,0:T(8,128)(2,1)S(1)} %pad_add_fusion), channel_id=1, source_target_pairs={{0,13},{1,12},{2,15},{3,14},{4,9},{5,8},{6,11},{7,10},{8,5},{9,4},... | collective-permute-start | bytes 36872 | tf_op jit(solution)/shard_map/ppermute | solution.py:293
  16.5 4.0 %collective-permute-start.5 = (s16[2,24,128]{2,1,0:T(8,128)(2,1)S(1)}, s16[2,24,128]{2,1,0:T(8,128)(2,1)S(1)}, u32[]{:S(2)}, u32[]{:S(2)}) collective-permute-start(s16[2,24,128]{2,1,0:T(8,128)(2,1)S(1)} %pad_add_fusion), channel_id=1, source_target_pairs={{0,9},{1,8},{2,11},{3,10},{4,13},{5,12},{6,15},{7,14},{8,1},{9,0},... | collective-permute-start | bytes 36872 | tf_op jit(solution)/shard_map/ppermute | solution.py:293
  16.9 3.7 %collective-permute-start.6 = (s16[2,24,128]{2,1,0:T(8,128)(2,1)S(1)}, s16[2,24,128]{2,1,0:T(8,128)(2,1)S(1)}, u32[]{:S(2)}, u32[]{:S(2)}) collective-permute-start(s16[2,24,128]{2,1,0:T(8,128)(2,1)S(1)} %pad_add_fusion), channel_id=1, source_target_pairs={{0,5},{1,4},{2,7},{3,6},{4,1},{5,0},{6,3},{7,2},{8,13},{9,12},{10,... | collective-permute-start | bytes 36872 | tf_op jit(solution)/shard_map/ppermute | solution.py:293
  20.6 1.4 %collective-permute-start.7 = (s16[8,24,128]{2,1,0:T(8,128)(2,1)S(1)}, s16[8,24,128]{2,1,0:T(8,128)(2,1)S(1)}, u32[]{:S(2)}, u32[]{:S(2)}) collective-permute-start(s16[8,24,128]{2,1,0:T(8,128)(2,1)S(1)} %constant_dynamic-update-slice_fusion.held), channel_id=1, source_target_pairs={{0,1},{1,0},{2,3},{3,2},{4,5},{5,4},{6,7},{7,6},{8,9},{9,8},{10,11... | collective-permute-start | bytes 147464 | tf_op jit(solution)/shard_map/ppermute | solution.py:300

commit v7 on v6

--- a/solution.py
+++ b/solution.py
@@ -82,7 +82,7 @@
 def spread(samples, part, wide, out):
     blocks, looks = wide.shape[1], out.shape[3]
     for j in range(blocks):
-        wide[part, j] = samples[part, :, j * LANES : (j + 1) * LANES].astype(F32)
+        wide[part, j, : samples.shape[1]] = samples[part, :, j * LANES : (j + 1) * LANES].astype(F32)
         for i in range(LOOK_A):
             out[part, j, i] = wide[part, j, pl.ds(i, looks, stride=LOOK_A), :]
 
@@ -112,7 +112,7 @@
         out_shape=(shape, shape, jax.ShapeDtypeStruct((parts, blocks, LOOK_A, looks, LANES), F32)),
         in_specs=[VMEM] * 3,
         out_specs=(VMEM,) * 3,
-        scratch_shapes=[pltpu.VMEM((parts, blocks, lines, LANES), F32)],
+        scratch_shapes=[pltpu.VMEM((parts, blocks, lines + LOOK_A, LANES), F32)],
         name="first_matching",
         compiler_params=pltpu.CompilerParams(vmem_limit_bytes=4 * 2**20),
         cost_estimate=pl.CostEstimate(flops=2 * 2**20, bytes_accessed=2**18, transcendentals=0),
@@ -125,7 +125,7 @@
     columns = []
     for j in range(blocks):
         for part in range(2):
-            wide[part, j] = other[part, :, j * LANES : (j + 1) * LANES].astype(F32)
+            wide[part, j, : other.shape[1]] = other[part, :, j * LANES : (j + 1) * LANES].astype(F32)
         total = 0.0
         for i in range(LOOK_A):
             their_re, their_im = (wide[part, j, pl.ds(i, looks, stride=LOOK_A), :] for part in range(2))
@@ -147,7 +147,7 @@
         out_shape=jax.ShapeDtypeStruct((3 * rows, cells), jnp.int16),
         in_specs=[VMEM] * 5,
         out_specs=VMEM,
-        scratch_shapes=[pltpu.VMEM((parts, width // LANES, lines, LANES), F32)],
+        scratch_shapes=[pltpu.VMEM((parts, width // LANES, lines + LOOK_A, LANES), F32)],
         name="whole_pair",
         compiler_params=pltpu.CompilerParams(vmem_limit_bytes=4 * 2**20),
         cost_estimate=pl.CostEstimate(flops=2 * 2**20, bytes_accessed=2**18, transcendentals=0),
@@ -249,7 +249,7 @@
     gain = lax.rsqrt(jnp.sqrt(real * real + imag * imag + 0.01))
     filtered = (smooth * gain[:, None]).reshape(planes * lines, 2 * cols)
     for side in range(2):
-        filt[side] = filtered[:, side * cols : (side + 1) * cols]
+        filt[side, : planes * lines] = filtered[:, side * cols : (side + 1) * cols]
     left = []
     for line in range(lines):
         value = [filt[side, pl.ds(line, planes, stride=lines), :] for side in range(2)]
@@ -280,7 +280,7 @@
         scratch_shapes=[
             pltpu.VMEM((BLOCK, 2, rows, cols), F32),
             pltpu.VMEM((ROUNDS * pairs * 2 * lines, 2 * cols), F32),
-            pltpu.VMEM((2, ROUNDS * pairs * 2 * lines, cols), F32),
+            pltpu.VMEM((2, (ROUNDS * pairs * 2 + 1) * lines, cols), F32),
         ],
         name="geocode",
         compiler_params=pltpu.CompilerParams(vmem_limit_bytes=8 * 2**20),

time: 23.4 us -> 23.4 us (level)
  no operation moved by 1% of the time
where the time goes in v7:
time: 23.4 us; the launch traced here: 23.3 us
  starting transfers between devices  9.98 us (43%)
  waiting for transfers between devices  9.29 us (40%)
  Pallas kernels  2.92 us (12%)
  local copies, waits for them, and re-layouts  1.02 us (4%)
    ppermute x4, waiting for transfers between devices, across(): return lax.ppermute(value, ('acq', 'rng'), pairs)  5.75 us
    ppermute x1, starting transfers between devices, per_device(): whole = lax.ppermute(own, 'acq', list(enumerate(quarter)))  4.04 us
    ppermute x4, starting transfers between devices, across(): return lax.ppermute(value, ('acq', 'rng'), pairs)  3.9 us
    ppermute x1, waiting for transfers between devices, per_device(): lax.ppermute(pick(own), 'acq', [(a, a ^ 1) for a in range(acq_count)])  1.57 us
    ppermute x1, starting transfers between devices, per_device(): lax.ppermute(pick(own), 'acq', [(a, a ^ 1) for a in range(acq_count)])  1.56 us
    pallas_call x1, Pallas kernels, geocode(): pl.pallas_call(geocode_kernel, out_shape=jax.ShapeDtypeStruct((ROUNDS, pa...  1.34 us
    ppermute x1, waiting for transfers between devices, per_device(): lax.ppermute(map_cell, 'rng', [(0, 1), (1, 0)])  1.08 us
    unnamed x10, local copies, waits for them, and re-layouts  1.02 us
  transfers between devices with their start and end apart: 8, of which 6 were waited for; matrix products, arithmetic and copies ran while one was open for 0% of the time, Pallas kernels for 5%

profile of v7, /device:TPU:0, one launch (start us, length us, event | category | flops | bytes accessed | tf_op | source)
XLA Modules:
  0.0 23.3 jit_solution(11189005047748618900)
XLA Ops:
  0.0 4.0 %collective-permute-start.2 = (bf16[2,64,1024]{2,1,0:T(8,128)(2,1)}, bf16[2,64,1024]{2,1,0:T(8,128)(2,1)S(1)}, u32[]{:S(2)}, u32[]{:S(2)}) collective-permute-start(bf16[2,64,1024]{2,1,0:T(8,128)(2,1)} %bitcast.3), channel_id=1, source_target_pairs={{0,8},{2,10},{4,0},{6,2},{8,12},{10,14},{12,4},{14,6},{1,9},{3,11}... | collective-permute-start | bytes 786440 | tf_op jit(solution)/shard_map/ppermute | solution.py:340
  4.0 1.0 %copy-done = bf16[2,1,64,1024]{3,2,1,0:T(8,128)(2,1)S(1)} copy-done((bf16[2,1,64,1024]{3,2,1,0:T(8,128)(2,1)S(1)}, bf16[2,1,64,1024]{3,2,1,0:T(8,128)(2,1)}, u32[]{:S(2)}) %copy-start) | copy-done | bytes 262168
  5.0 1.6 %collective-permute-start = (bf16[2,32,1024]{2,1,0:T(8,128)(2,1)S(1)}, bf16[2,32,1024]{2,1,0:T(8,128)(2,1)S(1)}, u32[]{:S(2)}, u32[]{:S(2)}) collective-permute-start(bf16[2,32,1024]{2,1,0:T(8,128)(2,1)S(1)} %pick.1), channel_id=1, source_target_pairs={{0,2},{2,0},{4,6},{6,4},{8,10},{10,8},{12,14},{14,12},{1,3},{3,1},... | collective-permute-start | bytes 393224 | tf_op jit(solution)/shard_map/ppermute | solution.py:341
  6.6 0.0 copy-done.2
  6.6 0.0 collective-permute-start.1
  6.6 0.1 taking.1.take
  6.7 1.1 %collective-permute-done.1.other_cells = s32[8,128]{1,0:T(8,128)S(1)} collective-permute-done((s32[8,128]{1,0:T(8,128)S(1)}, s32[8,128]{1,0:T(8,128)S(1)}, u32[]{:S(2)}, u32[]{:S(2)}) %collective-permute-start.1) | collective-permute-done | bytes 4128 | tf_op jit(solution)/shard_map/ppermute | solution.py:346
  7.8 0.7 %select.1 = (bf16[256,256]{1,0:T(8,128)(2,1)S(1)}, bf16[2048,256]{1,0:T(8,128)(2,1)S(1)}, f32[32,256]{1,0:T(8,128)S(1)}, f32[4,256]{1,0:T(4,128)S(1)}) custom-call(s32[8,128]{1,0:T(8,128)S(1)} %copy-done.2, s32[8,128]{1,0:T(8,128)S(1)} %collective-permute-done.1.other_cells), custom_call_target="tpu_custom_call" | custom-call | flops 2097152 | bytes 1048576 | tf_op jit(solution)/shard_map/select/pallas_call | solution.py:207
  8.5 1.6 %collective-permute-done.other = bf16[2,32,1024]{2,1,0:T(8,128)(2,1)S(1)} collective-permute-done((bf16[2,32,1024]{2,1,0:T(8,128)(2,1)S(1)}, bf16[2,32,1024]{2,1,0:T(8,128)(2,1)S(1)}, u32[]{:S(2)}, u32[]{:S(2)}) %collective-permute-start) | collective-permute-done | bytes 131104 | tf_op jit(solution)/shard_map/ppermute | solution.py:341
  10.1 0.0 copy-done.1
  10.1 0.4 %first_matching.1 = (f32[8,128]{1,0:T(8,128)S(1)}, f32[8,128]{1,0:T(8,128)S(1)}, f32[2,8,8,8,128]{4,3,2,1,0:T(8,128)S(1)}) custom-call(bf16[2,64,1024]{2,1,0:T(8,128)(2,1)S(1)} %bitcast.5, bf16[2,32,1024]{2,1,0:T(8,128)(2,1)S(1)} %collective-permute-done.other, bf16[1024,128]{1,0:T(8,128)(2,1)S(1)} %taking.1.take), custom_call_target="tpu_custom_call" | custom-call | flops 2097152 | bytes 262144 | tf_op jit(solution)/shard_map/first_matching/pallas_call | solution.py:110
  10.5 0.0 collective-permute-done.2.other
  10.5 0.3 %whole_pair.1 = s16[24,128]{1,0:T(8,128)(2,1)S(1)} custom-call(f32[2,8,8,8,128]{4,3,2,1,0:T(8,128)S(1)} %get-tuple-element.22.mine, bf16[2,64,1024]{2,1,0:T(8,128)(2,1)S(1)} %collective-permute-done.2.other, bf16[1024,128]{1,0:T(8,128)(2,1)S(1)} %taking.1.take, f32[8,128]{1,0:T(8,128)S(1)} %get-tuple-element.23.power, f32[8,128]{1,0:T(8,128)S(1)} %get-tuple-element.24.first), custom_call_target="tpu_custom_call" | custom-call | flops 2097152 | bytes 262144 | tf_op jit(solution)/shard_map/whole_pair/pallas_call | solution.py:145
  10.9 0.1 collective-permute-start.3
  11.0 3.0 %collective-permute-done.3 = s16[1,24,128]{2,1,0:T(8,128)(2,1)S(1)} collective-permute-done((s16[1,24,128]{2,1,0:T(8,128)(2,1)S(1)}, s16[1,24,128]{2,1,0:T(8,128)(2,1)S(1)}, u32[]{:S(2)}, u32[]{:S(2)}) %collective-permute-start.3) | collective-permute-done | bytes 6176 | tf_op jit(solution)/shard_map/ppermute | solution.py:293
  14.0 2.5 %collective-permute-start.4 = (s16[2,24,128]{2,1,0:T(8,128)(2,1)S(1)}, s16[2,24,128]{2,1,0:T(8,128)(2,1)S(1)}, u32[]{:S(2)}, u32[]{:S(2)}) collective-permute-start(s16[2,24,128]{2,1,0:T(8,128)(2,1)S(1)} %pad_add_fusion), channel_id=1, source_target_pairs={{0,13},{1,12},{2,15},{3,14},{4,9},{5,8},{6,11},{7,10},{8,5},{9,4},... | collective-permute-start | bytes 36872 | tf_op jit(solution)/shard_map/ppermute | solution.py:293
  16.5 0.4 %collective-permute-start.5 = (s16[2,24,128]{2,1,0:T(8,128)(2,1)S(1)}, s16[2,24,128]{2,1,0:T(8,128)(2,1)S(1)}, u32[]{:S(2)}, u32[]{:S(2)}) collective-permute-start(s16[2,24,128]{2,1,0:T(8,128)(2,1)S(1)} %pad_add_fusion), channel_id=1, source_target_pairs={{0,9},{1,8},{2,11},{3,10},{4,13},{5,12},{6,15},{7,14},{8,1},{9,0},... | collective-permute-start | bytes 36872 | tf_op jit(solution)/shard_map/ppermute | solution.py:293
  16.9 0.9 %collective-permute-start.6 = (s16[2,24,128]{2,1,0:T(8,128)(2,1)S(1)}, s16[2,24,128]{2,1,0:T(8,128)(2,1)S(1)}, u32[]{:S(2)}, u32[]{:S(2)}) collective-permute-start(s16[2,24,128]{2,1,0:T(8,128)(2,1)S(1)} %pad_add_fusion), channel_id=1, source_target_pairs={{0,5},{1,4},{2,7},{3,6},{4,1},{5,0},{6,3},{7,2},{8,13},{9,12},{10,... | collective-permute-start | bytes 36872 | tf_op jit(solution)/shard_map/ppermute | solution.py:293
  17.8 1.1 %collective-permute-done.4 = s16[2,24,128]{2,1,0:T(8,128)(2,1)S(1)} collective-permute-done((s16[2,24,128]{2,1,0:T(8,128)(2,1)S(1)}, s16[2,24,128]{2,1,0:T(8,128)(2,1)S(1)}, u32[]{:S(2)}, u32[]{:S(2)}) %collective-permute-start.4) | collective-permute-done | bytes 12320 | tf_op jit(solution)/shard_map/ppermute | solution.py:293
  18.9 1.6 %collective-permute-done.5 = s16[2,24,128]{2,1,0:T(8,128)(2,1)S(1)} collective-permute-done((s16[2,24,128]{2,1,0:T(8,128)(2,1)S(1)}, s16[2,24,128]{2,1,0:T(8,128)(2,1)S(1)}, u32[]{:S(2)}, u32[]{:S(2)}) %collective-permute-start.5) | collective-permute-done | bytes 12320 | tf_op jit(solution)/shard_map/ppermute | solution.py:293
  20.6 0.0 collective-permute-done.6
  20.6 0.5 %collective-permute-start.7 = (s16[8,24,128]{2,1,0:T(8,128)(2,1)S(1)}, s16[8,24,128]{2,1,0:T(8,128)(2,1)S(1)}, u32[]{:S(2)}, u32[]{:S(2)}) collective-permute-start(s16[8,24,128]{2,1,0:T(8,128)(2,1)S(1)} %constant_dynamic-update-slice_fusion.held), channel_id=1, source_target_pairs={{0,1},{1,0},{2,3},{3,2},{4,5},{5,4},{6,7},{7,6},{8,9},{9,8},{10,11... | collective-permute-start | bytes 147464 | tf_op jit(solution)/shard_map/ppermute | solution.py:300
  21.1 0.9 %collective-permute-done.7.sent = s16[8,24,128]{2,1,0:T(8,128)(2,1)S(1)} collective-permute-done((s16[8,24,128]{2,1,0:T(8,128)(2,1)S(1)}, s16[8,24,128]{2,1,0:T(8,128)(2,1)S(1)}, u32[]{:S(2)}, u32[]{:S(2)}) %collective-permute-start.7) | collective-permute-done | bytes 49184 | tf_op jit(solution)/shard_map/ppermute | solution.py:300
  21.9 1.3 %geocode.1 = f32[3,4,2,1024]{3,2,1,0:T(2,128)} custom-call(s16[8,24,128]{2,1,0:T(8,128)(2,1)S(1)} %constant_dynamic-update-slice_fusion.held, s16[8,24,128]{2,1,0:T(8,128)(2,1)S(1)} %collective-permute-done.7.sent, bf16[256,256]{1,0:T(8,128)(2,1)S(1)} %get-tuple-element.25.band, bf16[2048,256]{1,0:T(8,128)(2,1)S(1)} %get-tuple-element.26.onehot, ...), custom_call_target="tpu_custom_call" | custom-call | flops 268435456 | bytes 2097152 | tf_op jit(solution)/shard_map/geocode/pallas_call | solution.py:275
  (10 shorter events, 0.1 us)
Async XLA Ops:
  0.0 10.5 %collective-permute-start.2 = (bf16[2,64,1024]{2,1,0:T(8,128)(2,1)}, bf16[2,64,1024]{2,1,0:T(8,128)(2,1)S(1)}, u32[]{:S(2)}, u32[]{:S(2)}) collective-permute-start(bf16[2,64,1024]{2,1,0:T(8,128)(2,1)} %bitcast.3), channel_id=1, source_target_pairs={{0,8},{2,10},{4,0},{6,2},{8,12},{10,14},{12,4},{14,6},{1,9},{3,11}... | collective-permute-start | bytes 786440 | tf_op jit(solution)/shard_map/ppermute | solution.py:340
  4.0 1.0 %copy-start = (bf16[2,1,64,1024]{3,2,1,0:T(8,128)(2,1)S(1)}, bf16[2,1,64,1024]{3,2,1,0:T(8,128)(2,1)}, u32[]{:S(2)}) copy-start(bf16[2,1,64,1024]{3,2,1,0:T(8,128)(2,1)} %param.2) | copy-start | bytes 786436
  5.0 1.6 %copy-start.2 = (s32[8,128]{1,0:T(8,128)S(1)}, s32[8,128]{1,0:T(8,128)}, u32[]{:S(2)}) copy-start(s32[8,128]{1,0:T(8,128)} %own_cells.1) | copy-start | bytes 12292
  5.0 5.1 %copy-start.1 = (bf16[2,1,64,1024]{3,2,1,0:T(8,128)(2,1)S(1)}, bf16[2,1,64,1024]{3,2,1,0:T(8,128)(2,1)}, u32[]{:S(2)}) copy-start(bf16[2,1,64,1024]{3,2,1,0:T(8,128)(2,1)} %param.2) | copy-start | bytes 786436
  5.0 5.0 %collective-permute-start = (bf16[2,32,1024]{2,1,0:T(8,128)(2,1)S(1)}, bf16[2,32,1024]{2,1,0:T(8,128)(2,1)S(1)}, u32[]{:S(2)}, u32[]{:S(2)}) collective-permute-start(bf16[2,32,1024]{2,1,0:T(8,128)(2,1)S(1)} %pick.1), channel_id=1, source_target_pairs={{0,2},{2,0},{4,6},{6,4},{8,10},{10,8},{12,14},{14,12},{1,3},{3,1},... | collective-permute-start | bytes 393224 | tf_op jit(solution)/shard_map/ppermute | solution.py:341
  6.6 1.2 %collective-permute-start.1 = (s32[8,128]{1,0:T(8,128)S(1)}, s32[8,128]{1,0:T(8,128)S(1)}, u32[]{:S(2)}, u32[]{:S(2)}) collective-permute-start(s32[8,128]{1,0:T(8,128)S(1)} %copy-done.2), channel_id=1, source_target_pairs={{0,1},{1,0},{2,3},{3,2},{4,5},{5,4},{6,7},{7,6},{8,9},{9,8},{10,11... | collective-permute-start | bytes 12296 | tf_op jit(solution)/shard_map/ppermute | solution.py:346
  10.9 3.1 %collective-permute-start.3 = (s16[1,24,128]{2,1,0:T(8,128)(2,1)S(1)}, s16[1,24,128]{2,1,0:T(8,128)(2,1)S(1)}, u32[]{:S(2)}, u32[]{:S(2)}) collective-permute-start(s16[1,24,128]{2,1,0:T(8,128)(2,1)S(1)} %bitcast.6), channel_id=1, source_target_pairs={{0,3},{1,2},{2,1},{3,0},{4,7},{5,6},{6,5},{7,4},{8,11},{9,10},{10,... | collective-permute-start | bytes 18440 | tf_op jit(solution)/shard_map/ppermute | solution.py:293
  14.0 4.9 %collective-permute-start.4 = (s16[2,24,128]{2,1,0:T(8,128)(2,1)S(1)}, s16[2,24,128]{2,1,0:T(8,128)(2,1)S(1)}, u32[]{:S(2)}, u32[]{:S(2)}) collective-permute-start(s16[2,24,128]{2,1,0:T(8,128)(2,1)S(1)} %pad_add_fusion), channel_id=1, source_target_pairs={{0,13},{1,12},{2,15},{3,14},{4,9},{5,8},{6,11},{7,10},{8,5},{9,4},... | collective-permute-start | bytes 36872 | tf_op jit(solution)/shard_map/ppermute | solution.py:293
  16.5 4.0 %collective-permute-start.5 = (s16[2,24,128]{2,1,0:T(8,128)(2,1)S(1)}, s16[2,24,128]{2,1,0:T(8,128)(2,1)S(1)}, u32[]{:S(2)}, u32[]{:S(2)}) collective-permute-start(s16[2,24,128]{2,1,0:T(8,128)(2,1)S(1)} %pad_add_fusion), channel_id=1, source_target_pairs={{0,9},{1,8},{2,11},{3,10},{4,13},{5,12},{6,15},{7,14},{8,1},{9,0},... | collective-permute-start | bytes 36872 | tf_op jit(solution)/shard_map/ppermute | solution.py:293
  16.9 3.7 %collective-permute-start.6 = (s16[2,24,128]{2,1,0:T(8,128)(2,1)S(1)}, s16[2,24,128]{2,1,0:T(8,128)(2,1)S(1)}, u32[]{:S(2)}, u32[]{:S(2)}) collective-permute-start(s16[2,24,128]{2,1,0:T(8,128)(2,1)S(1)} %pad_add_fusion), channel_id=1, source_target_pairs={{0,5},{1,4},{2,7},{3,6},{4,1},{5,0},{6,3},{7,2},{8,13},{9,12},{10,... | collective-permute-start | bytes 36872 | tf_op jit(solution)/shard_map/ppermute | solution.py:293
  20.6 1.4 %collective-permute-start.7 = (s16[8,24,128]{2,1,0:T(8,128)(2,1)S(1)}, s16[8,24,128]{2,1,0:T(8,128)(2,1)S(1)}, u32[]{:S(2)}, u32[]{:S(2)}) collective-permute-start(s16[8,24,128]{2,1,0:T(8,128)(2,1)S(1)} %constant_dynamic-update-slice_fusion.held), channel_id=1, source_target_pairs={{0,1},{1,0},{2,3},{3,2},{4,5},{5,4},{6,7},{7,6},{8,9},{9,8},{10,11... | collective-permute-start | bytes 147464 | tf_op jit(solution)/shard_map/ppermute | solution.py:300

commit v8 on v7

--- a/solution.py
+++ b/solution.py
@@ -293,11 +293,18 @@
     return lax.ppermute(value, ("acq", "rng"), pairs)
 
 
+def swap(value):
+    return lax.ppermute(value, "rng", [(0, 1), (1, 0)])
+
+
 def gather_small(packed, chosen):
     held = packed[None]
-    for step in STEPS:
+    for step in STEPS[:-1]:
         held = jnp.concatenate([held] + [across(held, mask) for mask in step], axis=0)
-    return geocode(held, lax.ppermute(held, "rng", [(0, 1), (1, 0)]), *chosen)
+    last = [across(held, mask) for mask in STEPS[-1]]
+    early = swap(jnp.concatenate([held] + last[:1], axis=0))
+    late = swap(jnp.concatenate(last[1:], axis=0))
+    return geocode(jnp.concatenate([held] + last, axis=0), jnp.concatenate([early, late], axis=0), *chosen)
 
 
 def gather_large(packed, map_cell):
@@ -343,7 +350,7 @@
     take = taking(own.shape[2])
     if small:
         blocks = MAPC // (acq_count * lax.axis_size("rng")) // WIDE
-        chosen = select(blocks, map_cell, lax.ppermute(map_cell, "rng", [(0, 1), (1, 0)]))
+        chosen = select(blocks, map_cell, swap(map_cell))
         take, chosen = lax.optimization_barrier((take, chosen))
     first, power, mine = first_matching(own, half, take)
     packed = whole_pair(mine, whole, take, power, first)

time: 23.4 us -> 23.3 us (level)
    ppermute x2 -> x3, waiting for transfers between devices: 1.96 us -> 1.9 us  [swap(): return lax.ppermute(value, 'rng', [(0, 1), (1, 0)])]
    ppermute x2 -> x3, starting transfers between devices: 0.49 us -> 0.55 us  [swap(): return lax.ppermute(value, 'rng', [(0, 1), (1, 0)])]
  transfers between devices with their start and end apart: 8 -> 9, of which waited for: 6 -> 6; matrix products, arithmetic and copies ran while one was open for 0% -> 0% of each run, Pallas kernels for 5% -> 5%
where the time goes in v8:
time: 23.3 us; the launch traced here: 23.2 us
  starting transfers between devices  10 us (43%)
  waiting for transfers between devices  9.11 us (39%)
  Pallas kernels  2.92 us (13%)
  local copies, waits for them, and re-layouts  1.02 us (4%)
    ppermute x4, waiting for transfers between devices, across(): return lax.ppermute(value, ('acq', 'rng'), pairs)  5.64 us
    ppermute x1, starting transfers between devices, per_device(): whole = lax.ppermute(own, 'acq', list(enumerate(quarter)))  4.04 us
    ppermute x4, starting transfers between devices, across(): return lax.ppermute(value, ('acq', 'rng'), pairs)  3.9 us
    ppermute x3, waiting for transfers between devices, swap(): return lax.ppermute(value, 'rng', [(0, 1), (1, 0)])  1.9 us
    ppermute x1, waiting for transfers between devices, per_device(): lax.ppermute(pick(own), 'acq', [(a, a ^ 1) for a in range(acq_count)])  1.57 us
    ppermute x1, starting transfers between devices, per_device(): lax.ppermute(pick(own), 'acq', [(a, a ^ 1) for a in range(acq_count)])  1.56 us
    pallas_call x1, Pallas kernels, geocode(): pl.pallas_call(geocode_kernel, out_shape=jax.ShapeDtypeStruct((ROUNDS, pa...  1.34 us
    unnamed x10, local copies, waits for them, and re-layouts  1.02 us
  transfers between devices with their start and end apart: 9, of which 6 were waited for; matrix products, arithmetic and copies ran while one was open for 0% of the time, Pallas kernels for 5%

profile of v8, /device:TPU:0, one launch (start us, length us, event | category | flops | bytes accessed | tf_op | source)
XLA Modules:
  0.0 23.2 jit_solution(13674476785782053451)
XLA Ops:
  0.0 4.0 %collective-permute-start.2 = (bf16[2,64,1024]{2,1,0:T(8,128)(2,1)}, bf16[2,64,1024]{2,1,0:T(8,128)(2,1)S(1)}, u32[]{:S(2)}, u32[]{:S(2)}) collective-permute-start(bf16[2,64,1024]{2,1,0:T(8,128)(2,1)} %bitcast.3), channel_id=1, source_target_pairs={{0,8},{2,10},{4,0},{6,2},{8,12},{10,14},{12,4},{14,6},{1,9},{3,11}... | collective-permute-start | bytes 786440 | tf_op jit(solution)/shard_map/ppermute | solution.py:347
  4.0 1.0 %copy-done = bf16[2,1,64,1024]{3,2,1,0:T(8,128)(2,1)S(1)} copy-done((bf16[2,1,64,1024]{3,2,1,0:T(8,128)(2,1)S(1)}, bf16[2,1,64,1024]{3,2,1,0:T(8,128)(2,1)}, u32[]{:S(2)}) %copy-start) | copy-done | bytes 262168
  5.0 1.6 %collective-permute-start = (bf16[2,32,1024]{2,1,0:T(8,128)(2,1)S(1)}, bf16[2,32,1024]{2,1,0:T(8,128)(2,1)S(1)}, u32[]{:S(2)}, u32[]{:S(2)}) collective-permute-start(bf16[2,32,1024]{2,1,0:T(8,128)(2,1)S(1)} %pick.1), channel_id=1, source_target_pairs={{0,2},{2,0},{4,6},{6,4},{8,10},{10,8},{12,14},{14,12},{1,3},{3,1},... | collective-permute-start | bytes 393224 | tf_op jit(solution)/shard_map/ppermute | solution.py:348
  6.6 0.0 collective-permute-start.1
  6.6 0.1 taking.1.take
  6.7 1.1 %collective-permute-done.1.other_cells = s32[8,128]{1,0:T(8,128)S(1)} collective-permute-done((s32[8,128]{1,0:T(8,128)S(1)}, s32[8,128]{1,0:T(8,128)S(1)}, u32[]{:S(2)}, u32[]{:S(2)}) %collective-permute-start.1) | collective-permute-done | bytes 4128 | tf_op jit(solution)/shard_map/ppermute | solution.py:297
  7.8 0.7 %select.1 = (bf16[256,256]{1,0:T(8,128)(2,1)S(1)}, bf16[2048,256]{1,0:T(8,128)(2,1)S(1)}, f32[32,256]{1,0:T(8,128)S(1)}, f32[4,256]{1,0:T(4,128)S(1)}) custom-call(s32[8,128]{1,0:T(8,128)S(1)} %copy-done.2, s32[8,128]{1,0:T(8,128)S(1)} %collective-permute-done.1.other_cells), custom_call_target="tpu_custom_call" | custom-call | flops 2097152 | bytes 1048576 | tf_op jit(solution)/shard_map/select/pallas_call | solution.py:207
  8.5 1.6 %collective-permute-done.other = bf16[2,32,1024]{2,1,0:T(8,128)(2,1)S(1)} collective-permute-done((bf16[2,32,1024]{2,1,0:T(8,128)(2,1)S(1)}, bf16[2,32,1024]{2,1,0:T(8,128)(2,1)S(1)}, u32[]{:S(2)}, u32[]{:S(2)}) %collective-permute-start) | collective-permute-done | bytes 131104 | tf_op jit(solution)/shard_map/ppermute | solution.py:348
  10.1 0.4 %first_matching.1 = (f32[8,128]{1,0:T(8,128)S(1)}, f32[8,128]{1,0:T(8,128)S(1)}, f32[2,8,8,8,128]{4,3,2,1,0:T(8,128)S(1)}) custom-call(bf16[2,64,1024]{2,1,0:T(8,128)(2,1)S(1)} %bitcast.5, bf16[2,32,1024]{2,1,0:T(8,128)(2,1)S(1)} %collective-permute-done.other, bf16[1024,128]{1,0:T(8,128)(2,1)S(1)} %taking.1.take), custom_call_target="tpu_custom_call" | custom-call | flops 2097152 | bytes 262144 | tf_op jit(solution)/shard_map/first_matching/pallas_call | solution.py:110
  10.5 0.0 collective-permute-done.2.other
  10.5 0.3 %whole_pair.1 = s16[24,128]{1,0:T(8,128)(2,1)S(1)} custom-call(f32[2,8,8,8,128]{4,3,2,1,0:T(8,128)S(1)} %get-tuple-element.22.mine, bf16[2,64,1024]{2,1,0:T(8,128)(2,1)S(1)} %collective-permute-done.2.other, bf16[1024,128]{1,0:T(8,128)(2,1)S(1)} %taking.1.take, f32[8,128]{1,0:T(8,128)S(1)} %get-tuple-element.23.power, f32[8,128]{1,0:T(8,128)S(1)} %get-tuple-element.24.first), custom_call_target="tpu_custom_call" | custom-call | flops 2097152 | bytes 262144 | tf_op jit(solution)/shard_map/whole_pair/pallas_call | solution.py:145
  10.9 0.1 collective-permute-start.3
  11.0 3.0 %collective-permute-done.3 = s16[1,24,128]{2,1,0:T(8,128)(2,1)S(1)} collective-permute-done((s16[1,24,128]{2,1,0:T(8,128)(2,1)S(1)}, s16[1,24,128]{2,1,0:T(8,128)(2,1)S(1)}, u32[]{:S(2)}, u32[]{:S(2)}) %collective-permute-start.3) | collective-permute-done | bytes 6176 | tf_op jit(solution)/shard_map/ppermute | solution.py:293
  14.0 2.5 %collective-permute-start.4 = (s16[2,24,128]{2,1,0:T(8,128)(2,1)S(1)}, s16[2,24,128]{2,1,0:T(8,128)(2,1)S(1)}, u32[]{:S(2)}, u32[]{:S(2)}) collective-permute-start(s16[2,24,128]{2,1,0:T(8,128)(2,1)S(1)} %pad_add_fusion.3), channel_id=1, source_target_pairs={{0,13},{1,12},{2,15},{3,14},{4,9},{5,8},{6,11},{7,10},{8,5},{9,4},... | collective-permute-start | bytes 36872 | tf_op jit(solution)/shard_map/ppermute | solution.py:293
  16.5 0.4 %collective-permute-start.5 = (s16[2,24,128]{2,1,0:T(8,128)(2,1)S(1)}, s16[2,24,128]{2,1,0:T(8,128)(2,1)S(1)}, u32[]{:S(2)}, u32[]{:S(2)}) collective-permute-start(s16[2,24,128]{2,1,0:T(8,128)(2,1)S(1)} %pad_add_fusion.3), channel_id=1, source_target_pairs={{0,9},{1,8},{2,11},{3,10},{4,13},{5,12},{6,15},{7,14},{8,1},{9,0},... | collective-permute-start | bytes 36872 | tf_op jit(solution)/shard_map/ppermute | solution.py:293
  16.9 0.9 %collective-permute-start.6 = (s16[2,24,128]{2,1,0:T(8,128)(2,1)S(1)}, s16[2,24,128]{2,1,0:T(8,128)(2,1)S(1)}, u32[]{:S(2)}, u32[]{:S(2)}) collective-permute-start(s16[2,24,128]{2,1,0:T(8,128)(2,1)S(1)} %pad_add_fusion.3), channel_id=1, source_target_pairs={{0,5},{1,4},{2,7},{3,6},{4,1},{5,0},{6,3},{7,2},{8,13},{9,12},{10,... | collective-permute-start | bytes 36872 | tf_op jit(solution)/shard_map/ppermute | solution.py:293
  17.8 1.1 %collective-permute-done.4 = s16[2,24,128]{2,1,0:T(8,128)(2,1)S(1)} collective-permute-done((s16[2,24,128]{2,1,0:T(8,128)(2,1)S(1)}, s16[2,24,128]{2,1,0:T(8,128)(2,1)S(1)}, u32[]{:S(2)}, u32[]{:S(2)}) %collective-permute-start.4) | collective-permute-done | bytes 12320 | tf_op jit(solution)/shard_map/ppermute | solution.py:293
  18.9 0.1 collective-permute-start.7
  19.0 1.5 %collective-permute-done.5 = s16[2,24,128]{2,1,0:T(8,128)(2,1)S(1)} collective-permute-done((s16[2,24,128]{2,1,0:T(8,128)(2,1)S(1)}, s16[2,24,128]{2,1,0:T(8,128)(2,1)S(1)}, u32[]{:S(2)}, u32[]{:S(2)}) %collective-permute-start.5) | collective-permute-done | bytes 12320 | tf_op jit(solution)/shard_map/ppermute | solution.py:293
  20.6 0.0 collective-permute-done.6
  20.6 0.4 %collective-permute-start.8 = (s16[4,24,128]{2,1,0:T(8,128)(2,1)S(1)}, s16[4,24,128]{2,1,0:T(8,128)(2,1)S(1)}, u32[]{:S(2)}, u32[]{:S(2)}) collective-permute-start(s16[4,24,128]{2,1,0:T(8,128)(2,1)S(1)} %pad_add_fusion.2), channel_id=1, source_target_pairs={{0,1},{1,0},{2,3},{3,2},{4,5},{5,4},{6,7},{7,6},{8,9},{9,8},{10,11... | collective-permute-start | bytes 73736 | tf_op jit(solution)/shard_map/ppermute | solution.py:297
  21.0 0.0 collective-permute-done.7
  21.0 0.8 %collective-permute-done.8 = s16[4,24,128]{2,1,0:T(8,128)(2,1)S(1)} collective-permute-done((s16[4,24,128]{2,1,0:T(8,128)(2,1)S(1)}, s16[4,24,128]{2,1,0:T(8,128)(2,1)S(1)}, u32[]{:S(2)}, u32[]{:S(2)}) %collective-permute-start.8) | collective-permute-done | bytes 24608 | tf_op jit(solution)/shard_map/ppermute | solution.py:297
  21.8 1.3 %geocode.1 = f32[3,4,2,1024]{3,2,1,0:T(2,128)} custom-call(s16[8,24,128]{2,1,0:T(8,128)(2,1)S(1)} %constant_dynamic-update-slice_fusion.held, s16[8,24,128]{2,1,0:T(8,128)(2,1)S(1)} %pad_add_fusion.sent, bf16[256,256]{1,0:T(8,128)(2,1)S(1)} %get-tuple-element.25.band, bf16[2048,256]{1,0:T(8,128)(2,1)S(1)} %get-tuple-element.26.onehot, ...), custom_call_target="tpu_custom_call" | custom-call | flops 268435456 | bytes 2097152 | tf_op jit(solution)/shard_map/geocode/pallas_call | solution.py:275
  (15 shorter events, 0.1 us)
Async XLA Ops:
  0.0 10.5 %collective-permute-start.2 = (bf16[2,64,1024]{2,1,0:T(8,128)(2,1)}, bf16[2,64,1024]{2,1,0:T(8,128)(2,1)S(1)}, u32[]{:S(2)}, u32[]{:S(2)}) collective-permute-start(bf16[2,64,1024]{2,1,0:T(8,128)(2,1)} %bitcast.3), channel_id=1, source_target_pairs={{0,8},{2,10},{4,0},{6,2},{8,12},{10,14},{12,4},{14,6},{1,9},{3,11}... | collective-permute-start | bytes 786440 | tf_op jit(solution)/shard_map/ppermute | solution.py:347
  4.0 1.0 %copy-start = (bf16[2,1,64,1024]{3,2,1,0:T(8,128)(2,1)S(1)}, bf16[2,1,64,1024]{3,2,1,0:T(8,128)(2,1)}, u32[]{:S(2)}) copy-start(bf16[2,1,64,1024]{3,2,1,0:T(8,128)(2,1)} %param.2) | copy-start | bytes 786436
  5.0 1.6 %copy-start.2 = (s32[8,128]{1,0:T(8,128)S(1)}, s32[8,128]{1,0:T(8,128)}, u32[]{:S(2)}) copy-start(s32[8,128]{1,0:T(8,128)} %own_cells.1) | copy-start | bytes 12292
  5.0 5.1 %copy-start.1 = (bf16[2,1,64,1024]{3,2,1,0:T(8,128)(2,1)S(1)}, bf16[2,1,64,1024]{3,2,1,0:T(8,128)(2,1)}, u32[]{:S(2)}) copy-start(bf16[2,1,64,1024]{3,2,1,0:T(8,128)(2,1)} %param.2) | copy-start | bytes 786436
  5.0 5.0 %collective-permute-start = (bf16[2,32,1024]{2,1,0:T(8,128)(2,1)S(1)}, bf16[2,32,1024]{2,1,0:T(8,128)(2,1)S(1)}, u32[]{:S(2)}, u32[]{:S(2)}) collective-permute-start(bf16[2,32,1024]{2,1,0:T(8,128)(2,1)S(1)} %pick.1), channel_id=1, source_target_pairs={{0,2},{2,0},{4,6},{6,4},{8,10},{10,8},{12,14},{14,12},{1,3},{3,1},... | collective-permute-start | bytes 393224 | tf_op jit(solution)/shard_map/ppermute | solution.py:348
  6.6 1.2 %collective-permute-start.1 = (s32[8,128]{1,0:T(8,128)S(1)}, s32[8,128]{1,0:T(8,128)S(1)}, u32[]{:S(2)}, u32[]{:S(2)}) collective-permute-start(s32[8,128]{1,0:T(8,128)S(1)} %copy-done.2), channel_id=1, source_target_pairs={{0,1},{1,0},{2,3},{3,2},{4,5},{5,4},{6,7},{7,6},{8,9},{9,8},{10,11... | collective-permute-start | bytes 12296 | tf_op jit(solution)/shard_map/ppermute | solution.py:297
  10.9 3.1 %collective-permute-start.3 = (s16[1,24,128]{2,1,0:T(8,128)(2,1)S(1)}, s16[1,24,128]{2,1,0:T(8,128)(2,1)S(1)}, u32[]{:S(2)}, u32[]{:S(2)}) collective-permute-start(s16[1,24,128]{2,1,0:T(8,128)(2,1)S(1)} %bitcast.6), channel_id=1, source_target_pairs={{0,3},{1,2},{2,1},{3,0},{4,7},{5,6},{6,5},{7,4},{8,11},{9,10},{10,... | collective-permute-start | bytes 18440 | tf_op jit(solution)/shard_map/ppermute | solution.py:293
  14.0 4.9 %collective-permute-start.4 = (s16[2,24,128]{2,1,0:T(8,128)(2,1)S(1)}, s16[2,24,128]{2,1,0:T(8,128)(2,1)S(1)}, u32[]{:S(2)}, u32[]{:S(2)}) collective-permute-start(s16[2,24,128]{2,1,0:T(8,128)(2,1)S(1)} %pad_add_fusion.3), channel_id=1, source_target_pairs={{0,13},{1,12},{2,15},{3,14},{4,9},{5,8},{6,11},{7,10},{8,5},{9,4},... | collective-permute-start | bytes 36872 | tf_op jit(solution)/shard_map/ppermute | solution.py:293
  16.5 4.0 %collective-permute-start.5 = (s16[2,24,128]{2,1,0:T(8,128)(2,1)S(1)}, s16[2,24,128]{2,1,0:T(8,128)(2,1)S(1)}, u32[]{:S(2)}, u32[]{:S(2)}) collective-permute-start(s16[2,24,128]{2,1,0:T(8,128)(2,1)S(1)} %pad_add_fusion.3), channel_id=1, source_target_pairs={{0,9},{1,8},{2,11},{3,10},{4,13},{5,12},{6,15},{7,14},{8,1},{9,0},... | collective-permute-start | bytes 36872 | tf_op jit(solution)/shard_map/ppermute | solution.py:293
  16.9 3.7 %collective-permute-start.6 = (s16[2,24,128]{2,1,0:T(8,128)(2,1)S(1)}, s16[2,24,128]{2,1,0:T(8,128)(2,1)S(1)}, u32[]{:S(2)}, u32[]{:S(2)}) collective-permute-start(s16[2,24,128]{2,1,0:T(8,128)(2,1)S(1)} %pad_add_fusion.3), channel_id=1, source_target_pairs={{0,5},{1,4},{2,7},{3,6},{4,1},{5,0},{6,3},{7,2},{8,13},{9,12},{10,... | collective-permute-start | bytes 36872 | tf_op jit(solution)/shard_map/ppermute | solution.py:293
  18.9 2.1 %collective-permute-start.7 = (s16[4,24,128]{2,1,0:T(8,128)(2,1)S(1)}, s16[4,24,128]{2,1,0:T(8,128)(2,1)S(1)}, u32[]{:S(2)}, u32[]{:S(2)}) collective-permute-start(s16[4,24,128]{2,1,0:T(8,128)(2,1)S(1)} %pad_add_fusion.1), channel_id=1, source_target_pairs={{0,1},{1,0},{2,3},{3,2},{4,5},{5,4},{6,7},{7,6},{8,9},{9,8},{10,11... | collective-permute-start | bytes 73736 | tf_op jit(solution)/shard_map/ppermute | solution.py:297
  20.6 1.3 %collective-permute-start.8 = (s16[4,24,128]{2,1,0:T(8,128)(2,1)S(1)}, s16[4,24,128]{2,1,0:T(8,128)(2,1)S(1)}, u32[]{:S(2)}, u32[]{:S(2)}) collective-permute-start(s16[4,24,128]{2,1,0:T(8,128)(2,1)S(1)} %pad_add_fusion.2), channel_id=1, source_target_pairs={{0,1},{1,0},{2,3},{3,2},{4,5},{5,4},{6,7},{7,6},{8,9},{9,8},{10,11... | collective-permute-start | bytes 73736 | tf_op jit(solution)/shard_map/ppermute | solution.py:297

commit v9 on v8

--- a/solution.py
+++ b/solution.py
@@ -12,7 +12,7 @@
 HALF_W = 4
 ROUNDS = 3
 BLOCK = 2**ROUNDS
-STEPS = ((1,), (6, 4, 2))
+STEPS = ((6, 4, 2), (1,))
 SEND = (2, 0, 3, 1)
 WHOLE = ((1, 0), (2, 2), (2, 0), (1, 2))
 MAPC = 16384
@@ -220,29 +220,29 @@
     )(own_cells, other_cells)
 
 
-def geocode_kernel(held, sent, band, onehot, masks, scale, out, by_acq, grid, filt):
-    pairs = BLOCK // 2
+def half_sums(held, sent, other_line, band, onehot, masks, by_quarter, grid, filt):
     looks = held.shape[1] // 6
     lines, cols = 2 * looks, held.shape[2]
-    planes = ROUNDS * pairs * 2
-    blocks = scale.shape[0]
+    quarters = BLOCK // 2
+    planes = 4 * quarters
+    blocks = masks.shape[0] // lines
     rank, core = lax.axis_index("acq"), lax.axis_index("rng")
-    origins = [(0, 0)]
-    for step in STEPS:
-        origins = origins + [(bits ^ mask, 1 - other) for mask in step for bits, other in origins]
-    for slot, (bits, other) in enumerate(origins):
-        acq, side = rank ^ bits, core ^ other
-        by_acq[acq, side] = squared(held[slot].astype(jnp.int32))
-        by_acq[acq, 1 - side] = squared(sent[slot].astype(jnp.int32))
+    for slot, bits in enumerate((0,) + STEPS[0]):
+        quarter, side = (rank ^ bits) >> 1, core ^ (bits != 0) ^ other_line
+        by_quarter[quarter, side] = squared(held[slot].astype(jnp.int32))
+        by_quarter[quarter, 1 - side] = squared(sent[slot].astype(jnp.int32))
+    upper = (rank & 1) ^ other_line
+    none = jnp.zeros((looks, cols), F32)
     for side in range(2):
         columns = slice(side * cols, (side + 1) * cols)
-        for acq in range(BLOCK):
+        for quarter in range(quarters):
             for part in range(2):
-                row = (acq // 2 * 2 + part) * lines + (acq & 1) * looks
-                grid[row : row + looks, columns] = by_acq[acq, side, part * looks : (part + 1) * looks, :]
-            r, pair = WHOLE[acq >> 1]
-            row = (r * pairs + pair + (acq & 1)) * 2 * lines
-            grid[row : row + 2 * lines, columns] = by_acq[acq, side, lines:, :]
+                value = by_quarter[quarter, side, part * looks : (part + 1) * looks, :]
+                row = (quarter * 2 + part) * lines
+                grid[row : row + looks, columns] = jnp.where(upper == 0, value, none)
+                grid[row + looks : row + lines, columns] = jnp.where(upper == 0, none, value)
+            row = (planes // 2 + quarter * 2) * lines
+            grid[row : row + 2 * lines, columns] = by_quarter[quarter, side, lines:, :]
     smooth = dot_in_two(grid[...], band[...]) * (1.0 / (UNIT * (HALF_W + 1)) ** 2)
     smooth = smooth.reshape(planes // 2, 2, lines, 2 * cols)
     real, imag = smooth[:, 0], smooth[:, 1]
@@ -259,33 +259,49 @@
         rows = [both * masks[line * blocks + block : line * blocks + block + 1, :] for block in range(blocks)]
         left.append(jnp.concatenate(rows, axis=0).astype(BF16))
     sums = dot(jnp.concatenate(left, axis=1), onehot[...])
-    for block in range(blocks):
-        start = block * 2 * planes
-        total = sums[start : start + planes] + sums[start + planes : start + 2 * planes]
+    starts = [block * 2 * planes for block in range(blocks)]
+    return [sums[start : start + planes] + sums[start + planes : start + 2 * planes] for start in starts]
+
+
+def near_kernel(held, sent, band, onehot, masks, scale, out, by_quarter, grid, filt):
+    for block, total in enumerate(half_sums(held, sent, 0, band, onehot, masks, by_quarter, grid, filt)):
+        out[block] = total * scale[block : block + 1, :]
+
+
+def far_kernel(held, sent, band, onehot, masks, scale, near, out, by_quarter, grid, filt):
+    line = lax.axis_index("acq") & 1
+    half = near.shape[1] // 2
+    for block, total in enumerate(half_sums(held, sent, 1, band, onehot, masks, by_quarter, grid, filt)):
         total = total * scale[block : block + 1, :]
-        for plane in range(0, planes, 2):
-            r, pair = plane // (2 * pairs), plane // 2 % pairs
-            out[r, pair, :, block * WIDE : (block + 1) * WIDE] = total[plane : plane + 2]
-
-
-def geocode(held, sent, band, onehot, masks, scale):
-    pairs, blocks = BLOCK // 2, scale.shape[0]
-    _, rows, cols = held.shape
+        ours = near[block]
+        columns = slice(block * WIDE, (block + 1) * WIDE)
+        for quarter in range(BLOCK // 2):
+            rows = slice(2 * quarter, 2 * quarter + 2)
+            out[0, quarter, :, columns] = ours[rows] + total[rows]
+            r, pair = WHOLE[quarter]
+            rows = slice(half + 2 * quarter, half + 2 * quarter + 2)
+            out[r, pair + line, :, columns] = ours[rows]
+            out[r, pair + 1 - line, :, columns] = total[rows]
+
+
+def geocode_half(kernel, name, shape, held, sent, *rest):
+    slots, rows, cols = held.shape
     lines = rows // 3
-    return pl.pallas_call(
-        geocode_kernel,
-        out_shape=jax.ShapeDtypeStruct((ROUNDS, pairs, 2, blocks * WIDE), F32),
-        in_specs=[VMEM] * 6,
+    planes = 4 * slots
+    return pl.pallas_call(
+        kernel,
+        out_shape=jax.ShapeDtypeStruct(shape, F32),
+        in_specs=[VMEM] * (2 + len(rest)),
         out_specs=VMEM,
         scratch_shapes=[
-            pltpu.VMEM((BLOCK, 2, rows, cols), F32),
-            pltpu.VMEM((ROUNDS * pairs * 2 * lines, 2 * cols), F32),
-            pltpu.VMEM((2, (ROUNDS * pairs * 2 + 1) * lines, cols), F32),
+            pltpu.VMEM((slots, 2, rows, cols), F32),
+            pltpu.VMEM((planes * lines, 2 * cols), F32),
+            pltpu.VMEM((2, (planes + 1) * lines, cols), F32),
         ],
-        name="geocode",
+        name=name,
         compiler_params=pltpu.CompilerParams(vmem_limit_bytes=8 * 2**20),
-        cost_estimate=pl.CostEstimate(flops=2**28, bytes_accessed=2**21, transcendentals=2**16),
-    )(held, sent, band, onehot, masks, scale)
+        cost_estimate=pl.CostEstimate(flops=2**21, bytes_accessed=2**20, transcendentals=2**15),
+    )(held, sent, *rest)
 
 
 def across(value, mask):
@@ -299,12 +315,15 @@
 
 def gather_small(packed, chosen):
     held = packed[None]
-    for step in STEPS[:-1]:
-        held = jnp.concatenate([held] + [across(held, mask) for mask in step], axis=0)
-    last = [across(held, mask) for mask in STEPS[-1]]
-    early = swap(jnp.concatenate([held] + last[:1], axis=0))
-    late = swap(jnp.concatenate(last[1:], axis=0))
-    return geocode(jnp.concatenate([held] + last, axis=0), jnp.concatenate([early, late], axis=0), *chosen)
+    held = jnp.concatenate([held] + [across(held, mask) for mask in STEPS[0]], axis=0)
+    far = across(held, STEPS[1][0])
+    band, onehot, masks, scale = chosen
+    blocks = scale.shape[0]
+    near = geocode_half(
+        near_kernel, "near_line", (blocks, 2 * BLOCK, WIDE), held, swap(held), band, onehot, masks, scale
+    )
+    shape = (ROUNDS, BLOCK // 2, 2, blocks * WIDE)
+    return geocode_half(far_kernel, "far_line", shape, far, swap(far), band, onehot, masks, scale, near)
 
 
 def gather_large(packed, map_cell):

time: 23.3 us -> 23.3 us (level)
  waiting for transfers between devices: 9.11 us -> 7.17 us
  starting transfers between devices: 10 us -> 11.5 us
  Pallas kernels: 2.92 us -> 3.42 us
    ppermute x4, starting transfers between devices: 3.9 us -> 5.29 us  [across(): return lax.ppermute(value, ('acq', 'rng'), pairs)]
    ppermute x4, waiting for transfers between devices: 5.64 us -> 4.26 us  [across(): return lax.ppermute(value, ('acq', 'rng'), pairs)]
    ppermute x3, waiting for transfers between devices: 1.9 us -> 1.33 us  [swap(): return lax.ppermute(value, 'rng', [(0, 1), (1, 0)])]
    pallas_call x1 -> x2, Pallas kernels: 1.34 us -> 1.85 us  [geocode_half(): pl.pallas_call(kernel, out_shape=jax.ShapeDtypeStruct(shape, F32), in_spe...]
    unnamed x10 -> x6, local copies, waits for them, and re-layouts: 1.02 us -> 0.99 us
  transfers between devices with their start and end apart: 9 -> 9, of which waited for: 6 -> 7; matrix products, arithmetic and copies ran while one was open for 0% -> 0% of each run, Pallas kernels for 5% -> 8%
where the time goes in v9:
time: 23.3 us; the launch traced here: 23.2 us
  starting transfers between devices  11.5 us (49%)
  waiting for transfers between devices  7.17 us (31%)
  Pallas kernels  3.42 us (15%)
  local copies, waits for them, and re-layouts  0.99 us (4%)
    ppermute x4, starting transfers between devices, across(): return lax.ppermute(value, ('acq', 'rng'), pairs)  5.29 us
    ppermute x4, waiting for transfers between devices, across(): return lax.ppermute(value, ('acq', 'rng'), pairs)  4.26 us
    ppermute x1, starting transfers between devices, per_device(): whole = lax.ppermute(own, 'acq', list(enumerate(quarter)))  4.04 us
    pallas_call x2, Pallas kernels, geocode_half(): pl.pallas_call(kernel, out_shape=jax.ShapeDtypeStruct(shape, F32), in_spe...  1.85 us
    ppermute x1, waiting for transfers between devices, per_device(): lax.ppermute(pick(own), 'acq', [(a, a ^ 1) for a in range(acq_count)])  1.57 us
    ppermute x1, starting transfers between devices, per_device(): lax.ppermute(pick(own), 'acq', [(a, a ^ 1) for a in range(acq_count)])  1.56 us
    ppermute x3, waiting for transfers between devices, swap(): return lax.ppermute(value, 'rng', [(0, 1), (1, 0)])  1.33 us
    unnamed x6, local copies, waits for them, and re-layouts  0.99 us
  transfers between devices with their start and end apart: 9, of which 7 were waited for; matrix products, arithmetic and copies ran while one was open for 0% of the time, Pallas kernels for 8%

profile of v9, /device:TPU:0, one launch (start us, length us, event | category | flops | bytes accessed | tf_op | source)
XLA Modules:
  0.0 23.2 jit_solution(3141203993200676272)
XLA Ops:
  0.0 4.0 %collective-permute-start.2 = (bf16[2,64,1024]{2,1,0:T(8,128)(2,1)}, bf16[2,64,1024]{2,1,0:T(8,128)(2,1)S(1)}, u32[]{:S(2)}, u32[]{:S(2)}) collective-permute-start(bf16[2,64,1024]{2,1,0:T(8,128)(2,1)} %bitcast.2), channel_id=1, source_target_pairs={{0,8},{2,10},{4,0},{6,2},{8,12},{10,14},{12,4},{14,6},{1,9},{3,11}... | collective-permute-start | bytes 786440 | tf_op jit(solution)/shard_map/ppermute | solution.py:366
  4.0 1.0 %copy-done = bf16[2,1,64,1024]{3,2,1,0:T(8,128)(2,1)S(1)} copy-done((bf16[2,1,64,1024]{3,2,1,0:T(8,128)(2,1)S(1)}, bf16[2,1,64,1024]{3,2,1,0:T(8,128)(2,1)}, u32[]{:S(2)}) %copy-start) | copy-done | bytes 262168
  5.0 1.6 %collective-permute-start = (bf16[2,32,1024]{2,1,0:T(8,128)(2,1)S(1)}, bf16[2,32,1024]{2,1,0:T(8,128)(2,1)S(1)}, u32[]{:S(2)}, u32[]{:S(2)}) collective-permute-start(bf16[2,32,1024]{2,1,0:T(8,128)(2,1)S(1)} %pick.1), channel_id=1, source_target_pairs={{0,2},{2,0},{4,6},{6,4},{8,10},{10,8},{12,14},{14,12},{1,3},{3,1},... | collective-permute-start | bytes 393224 | tf_op jit(solution)/shard_map/ppermute | solution.py:367
  6.6 0.1 taking.1.take
  6.7 1.1 %collective-permute-done.1.other_cells = s32[8,128]{1,0:T(8,128)S(1)} collective-permute-done((s32[8,128]{1,0:T(8,128)S(1)}, s32[8,128]{1,0:T(8,128)S(1)}, u32[]{:S(2)}, u32[]{:S(2)}) %collective-permute-start.1) | collective-permute-done | bytes 4128 | tf_op jit(solution)/shard_map/ppermute | solution.py:313
  7.8 0.7 %select.1 = (bf16[256,256]{1,0:T(8,128)(2,1)S(1)}, bf16[2048,256]{1,0:T(8,128)(2,1)S(1)}, f32[32,256]{1,0:T(8,128)S(1)}, f32[4,256]{1,0:T(4,128)S(1)}) custom-call(s32[8,128]{1,0:T(8,128)S(1)} %copy-done.2, s32[8,128]{1,0:T(8,128)S(1)} %collective-permute-done.1.other_cells), custom_call_target="tpu_custom_call" | custom-call | flops 2097152 | bytes 1048576 | tf_op jit(solution)/shard_map/select/pallas_call | solution.py:207
  8.5 1.6 %collective-permute-done.other = bf16[2,32,1024]{2,1,0:T(8,128)(2,1)S(1)} collective-permute-done((bf16[2,32,1024]{2,1,0:T(8,128)(2,1)S(1)}, bf16[2,32,1024]{2,1,0:T(8,128)(2,1)S(1)}, u32[]{:S(2)}, u32[]{:S(2)}) %collective-permute-start) | collective-permute-done | bytes 131104 | tf_op jit(solution)/shard_map/ppermute | solution.py:367
  10.1 0.4 %first_matching.1 = (f32[8,128]{1,0:T(8,128)S(1)}, f32[8,128]{1,0:T(8,128)S(1)}, f32[2,8,8,8,128]{4,3,2,1,0:T(8,128)S(1)}) custom-call(bf16[2,64,1024]{2,1,0:T(8,128)(2,1)S(1)} %bitcast.4, bf16[2,32,1024]{2,1,0:T(8,128)(2,1)S(1)} %collective-permute-done.other, bf16[1024,128]{1,0:T(8,128)(2,1)S(1)} %taking.1.take), custom_call_target="tpu_custom_call" | custom-call | flops 2097152 | bytes 262144 | tf_op jit(solution)/shard_map/first_matching/pallas_call | solution.py:110
  10.5 0.0 collective-permute-done.2.other
  10.5 0.3 %whole_pair.1 = s16[24,128]{1,0:T(8,128)(2,1)S(1)} custom-call(f32[2,8,8,8,128]{4,3,2,1,0:T(8,128)S(1)} %get-tuple-element.22.mine, bf16[2,64,1024]{2,1,0:T(8,128)(2,1)S(1)} %collective-permute-done.2.other, bf16[1024,128]{1,0:T(8,128)(2,1)S(1)} %taking.1.take, f32[8,128]{1,0:T(8,128)S(1)} %get-tuple-element.23.power, f32[8,128]{1,0:T(8,128)S(1)} %get-tuple-element.24.first), custom_call_target="tpu_custom_call" | custom-call | flops 2097152 | bytes 262144 | tf_op jit(solution)/shard_map/whole_pair/pallas_call | solution.py:145
  10.9 1.4 %collective-permute-start.3 = (s16[1,24,128]{2,1,0:T(8,128)(2,1)S(1)}, s16[1,24,128]{2,1,0:T(8,128)(2,1)S(1)}, u32[]{:S(2)}, u32[]{:S(2)}) collective-permute-start(s16[1,24,128]{2,1,0:T(8,128)(2,1)S(1)} %bitcast.5), channel_id=1, source_target_pairs={{0,13},{1,12},{2,15},{3,14},{4,9},{5,8},{6,11},{7,10},{8,5},{9,4},... | collective-permute-start | bytes 18440 | tf_op jit(solution)/shard_map/ppermute | solution.py:309
  12.3 1.5 %collective-permute-start.4 = (s16[1,24,128]{2,1,0:T(8,128)(2,1)S(1)}, s16[1,24,128]{2,1,0:T(8,128)(2,1)S(1)}, u32[]{:S(2)}, u32[]{:S(2)}) collective-permute-start(s16[1,24,128]{2,1,0:T(8,128)(2,1)S(1)} %bitcast.6), channel_id=1, source_target_pairs={{0,9},{1,8},{2,11},{3,10},{4,13},{5,12},{6,15},{7,14},{8,1},{9,0},... | collective-permute-start | bytes 18440 | tf_op jit(solution)/shard_map/ppermute | solution.py:309
  13.8 0.3 %collective-permute-start.5 = (s16[1,24,128]{2,1,0:T(8,128)(2,1)S(1)}, s16[1,24,128]{2,1,0:T(8,128)(2,1)S(1)}, u32[]{:S(2)}, u32[]{:S(2)}) collective-permute-start(s16[1,24,128]{2,1,0:T(8,128)(2,1)S(1)} %bitcast.7), channel_id=1, source_target_pairs={{0,5},{1,4},{2,7},{3,6},{4,1},{5,0},{6,3},{7,2},{8,13},{9,12},{10,... | collective-permute-start | bytes 18440 | tf_op jit(solution)/shard_map/ppermute | solution.py:309
  14.1 1.7 %collective-permute-done.3 = s16[1,24,128]{2,1,0:T(8,128)(2,1)S(1)} collective-permute-done((s16[1,24,128]{2,1,0:T(8,128)(2,1)S(1)}, s16[1,24,128]{2,1,0:T(8,128)(2,1)S(1)}, u32[]{:S(2)}, u32[]{:S(2)}) %collective-permute-start.3) | collective-permute-done | bytes 6176 | tf_op jit(solution)/shard_map/ppermute | solution.py:309
  15.8 0.5 %collective-permute-done.4 = s16[1,24,128]{2,1,0:T(8,128)(2,1)S(1)} collective-permute-done((s16[1,24,128]{2,1,0:T(8,128)(2,1)S(1)}, s16[1,24,128]{2,1,0:T(8,128)(2,1)S(1)}, u32[]{:S(2)}, u32[]{:S(2)}) %collective-permute-start.4) | collective-permute-done | bytes 6176 | tf_op jit(solution)/shard_map/ppermute | solution.py:309
  16.2 0.6 %collective-permute-done.5 = s16[1,24,128]{2,1,0:T(8,128)(2,1)S(1)} collective-permute-done((s16[1,24,128]{2,1,0:T(8,128)(2,1)S(1)}, s16[1,24,128]{2,1,0:T(8,128)(2,1)S(1)}, u32[]{:S(2)}, u32[]{:S(2)}) %collective-permute-start.5) | collective-permute-done | bytes 6176 | tf_op jit(solution)/shard_map/ppermute | solution.py:309
  16.8 2.1 %collective-permute-start.6 = (s16[4,24,128]{2,1,0:T(8,128)(2,1)S(1)}, s16[4,24,128]{2,1,0:T(8,128)(2,1)S(1)}, u32[]{:S(2)}, u32[]{:S(2)}) collective-permute-start(s16[4,24,128]{2,1,0:T(8,128)(2,1)S(1)} %pad_add_fusion.held), channel_id=1, source_target_pairs={{0,3},{1,2},{2,1},{3,0},{4,7},{5,6},{6,5},{7,4},{8,11},{9,10},{10,... | collective-permute-start | bytes 73736 | tf_op jit(solution)/shard_map/ppermute | solution.py:309
  18.9 0.0 collective-permute-start.8
  18.9 1.5 %collective-permute-done.6.held = s16[4,24,128]{2,1,0:T(8,128)(2,1)S(1)} collective-permute-done((s16[4,24,128]{2,1,0:T(8,128)(2,1)S(1)}, s16[4,24,128]{2,1,0:T(8,128)(2,1)S(1)}, u32[]{:S(2)}, u32[]{:S(2)}) %collective-permute-start.6) | collective-permute-done | bytes 24608 | tf_op jit(solution)/shard_map/ppermute | solution.py:309
  20.4 0.6 %collective-permute-start.7 = (s16[4,24,128]{2,1,0:T(8,128)(2,1)S(1)}, s16[4,24,128]{2,1,0:T(8,128)(2,1)S(1)}, u32[]{:S(2)}, u32[]{:S(2)}) collective-permute-start(s16[4,24,128]{2,1,0:T(8,128)(2,1)S(1)} %collective-permute-done.6.held), channel_id=1, source_target_pairs={{0,1},{1,0},{2,3},{3,2},{4,5},{5,4},{6,7},{7,6},{8,9},{9,8},{10,11... | collective-permute-start | bytes 73736 | tf_op jit(solution)/shard_map/ppermute | solution.py:313
  21.1 0.0 collective-permute-done.8.sent
  21.1 0.6 %near_line.1.near = f32[4,16,256]{2,1,0:T(8,128)S(1)} custom-call(s16[4,24,128]{2,1,0:T(8,128)(2,1)S(1)} %pad_add_fusion.held, s16[4,24,128]{2,1,0:T(8,128)(2,1)S(1)} %collective-permute-done.8.sent, bf16[256,256]{1,0:T(8,128)(2,1)S(1)} %get-tuple-element.25.band, bf16[2048,256]{1,0:T(8,128)(2,1)S(1)} %get-tuple-element.26.onehot, ...), custom_call_target="tpu_custom_call" | custom-call | flops 2097152 | bytes 1048576 | tf_op jit(solution)/shard_map/near_line/pallas_call | solution.py:291
  21.7 0.2 %collective-permute-done.7.sent = s16[4,24,128]{2,1,0:T(8,128)(2,1)S(1)} collective-permute-done((s16[4,24,128]{2,1,0:T(8,128)(2,1)S(1)}, s16[4,24,128]{2,1,0:T(8,128)(2,1)S(1)}, u32[]{:S(2)}, u32[]{:S(2)}) %collective-permute-start.7) | collective-permute-done | bytes 24608 | tf_op jit(solution)/shard_map/ppermute | solution.py:313
  21.9 1.3 %far_line.1 = f32[3,4,2,1024]{3,2,1,0:T(2,128)} custom-call(s16[4,24,128]{2,1,0:T(8,128)(2,1)S(1)} %collective-permute-done.6.held, s16[4,24,128]{2,1,0:T(8,128)(2,1)S(1)} %collective-permute-done.7.sent, bf16[256,256]{1,0:T(8,128)(2,1)S(1)} %get-tuple-element.25.band, bf16[2048,256]{1,0:T(8,128)(2,1)S(1)} %get-tuple-element.26.onehot, ...), custom_call_target="tpu_custom_call" | custom-call | flops 2097152 | bytes 1048576 | tf_op jit(solution)/shard_map/far_line/pallas_call | solution.py:291
  (8 shorter events, 0.0 us)
Async XLA Ops:
  0.0 10.5 %collective-permute-start.2 = (bf16[2,64,1024]{2,1,0:T(8,128)(2,1)}, bf16[2,64,1024]{2,1,0:T(8,128)(2,1)S(1)}, u32[]{:S(2)}, u32[]{:S(2)}) collective-permute-start(bf16[2,64,1024]{2,1,0:T(8,128)(2,1)} %bitcast.2), channel_id=1, source_target_pairs={{0,8},{2,10},{4,0},{6,2},{8,12},{10,14},{12,4},{14,6},{1,9},{3,11}... | collective-permute-start | bytes 786440 | tf_op jit(solution)/shard_map/ppermute | solution.py:366
  4.0 1.0 %copy-start = (bf16[2,1,64,1024]{3,2,1,0:T(8,128)(2,1)S(1)}, bf16[2,1,64,1024]{3,2,1,0:T(8,128)(2,1)}, u32[]{:S(2)}) copy-start(bf16[2,1,64,1024]{3,2,1,0:T(8,128)(2,1)} %param.2) | copy-start | bytes 786436
  5.0 1.6 %copy-start.2 = (s32[8,128]{1,0:T(8,128)S(1)}, s32[8,128]{1,0:T(8,128)}, u32[]{:S(2)}) copy-start(s32[8,128]{1,0:T(8,128)} %own_cells.1) | copy-start | bytes 12292
  5.0 5.1 %copy-start.1 = (bf16[2,1,64,1024]{3,2,1,0:T(8,128)(2,1)S(1)}, bf16[2,1,64,1024]{3,2,1,0:T(8,128)(2,1)}, u32[]{:S(2)}) copy-start(bf16[2,1,64,1024]{3,2,1,0:T(8,128)(2,1)} %param.2) | copy-start | bytes 786436
  5.0 5.0 %collective-permute-start = (bf16[2,32,1024]{2,1,0:T(8,128)(2,1)S(1)}, bf16[2,32,1024]{2,1,0:T(8,128)(2,1)S(1)}, u32[]{:S(2)}, u32[]{:S(2)}) collective-permute-start(bf16[2,32,1024]{2,1,0:T(8,128)(2,1)S(1)} %pick.1), channel_id=1, source_target_pairs={{0,2},{2,0},{4,6},{6,4},{8,10},{10,8},{12,14},{14,12},{1,3},{3,1},... | collective-permute-start | bytes 393224 | tf_op jit(solution)/shard_map/ppermute | solution.py:367
  6.6 1.2 %collective-permute-start.1 = (s32[8,128]{1,0:T(8,128)S(1)}, s32[8,128]{1,0:T(8,128)S(1)}, u32[]{:S(2)}, u32[]{:S(2)}) collective-permute-start(s32[8,128]{1,0:T(8,128)S(1)} %copy-done.2), channel_id=1, source_target_pairs={{0,1},{1,0},{2,3},{3,2},{4,5},{5,4},{6,7},{7,6},{8,9},{9,8},{10,11... | collective-permute-start | bytes 12296 | tf_op jit(solution)/shard_map/ppermute | solution.py:313
  10.9 4.9 %collective-permute-start.3 = (s16[1,24,128]{2,1,0:T(8,128)(2,1)S(1)}, s16[1,24,128]{2,1,0:T(8,128)(2,1)S(1)}, u32[]{:S(2)}, u32[]{:S(2)}) collective-permute-start(s16[1,24,128]{2,1,0:T(8,128)(2,1)S(1)} %bitcast.5), channel_id=1, source_target_pairs={{0,13},{1,12},{2,15},{3,14},{4,9},{5,8},{6,11},{7,10},{8,5},{9,4},... | collective-permute-start | bytes 18440 | tf_op jit(solution)/shard_map/ppermute | solution.py:309
  12.3 4.0 %collective-permute-start.4 = (s16[1,24,128]{2,1,0:T(8,128)(2,1)S(1)}, s16[1,24,128]{2,1,0:T(8,128)(2,1)S(1)}, u32[]{:S(2)}, u32[]{:S(2)}) collective-permute-start(s16[1,24,128]{2,1,0:T(8,128)(2,1)S(1)} %bitcast.6), channel_id=1, source_target_pairs={{0,9},{1,8},{2,11},{3,10},{4,13},{5,12},{6,15},{7,14},{8,1},{9,0},... | collective-permute-start | bytes 18440 | tf_op jit(solution)/shard_map/ppermute | solution.py:309
  13.8 3.1 %collective-permute-start.5 = (s16[1,24,128]{2,1,0:T(8,128)(2,1)S(1)}, s16[1,24,128]{2,1,0:T(8,128)(2,1)S(1)}, u32[]{:S(2)}, u32[]{:S(2)}) collective-permute-start(s16[1,24,128]{2,1,0:T(8,128)(2,1)S(1)} %bitcast.7), channel_id=1, source_target_pairs={{0,5},{1,4},{2,7},{3,6},{4,1},{5,0},{6,3},{7,2},{8,13},{9,12},{10,... | collective-permute-start | bytes 18440 | tf_op jit(solution)/shard_map/ppermute | solution.py:309
  16.8 3.6 %collective-permute-start.6 = (s16[4,24,128]{2,1,0:T(8,128)(2,1)S(1)}, s16[4,24,128]{2,1,0:T(8,128)(2,1)S(1)}, u32[]{:S(2)}, u32[]{:S(2)}) collective-permute-start(s16[4,24,128]{2,1,0:T(8,128)(2,1)S(1)} %pad_add_fusion.held), channel_id=1, source_target_pairs={{0,3},{1,2},{2,1},{3,0},{4,7},{5,6},{6,5},{7,4},{8,11},{9,10},{10,... | collective-permute-start | bytes 73736 | tf_op jit(solution)/shard_map/ppermute | solution.py:309
  18.9 2.2 %collective-permute-start.8 = (s16[4,24,128]{2,1,0:T(8,128)(2,1)S(1)}, s16[4,24,128]{2,1,0:T(8,128)(2,1)S(1)}, u32[]{:S(2)}, u32[]{:S(2)}) collective-permute-start(s16[4,24,128]{2,1,0:T(8,128)(2,1)S(1)} %pad_add_fusion.held), channel_id=1, source_target_pairs={{0,1},{1,0},{2,3},{3,2},{4,5},{5,4},{6,7},{7,6},{8,9},{9,8},{10,11... | collective-permute-start | bytes 73736 | tf_op jit(solution)/shard_map/ppermute | solution.py:313
  20.4 1.5 %collective-permute-start.7 = (s16[4,24,128]{2,1,0:T(8,128)(2,1)S(1)}, s16[4,24,128]{2,1,0:T(8,128)(2,1)S(1)}, u32[]{:S(2)}, u32[]{:S(2)}) collective-permute-start(s16[4,24,128]{2,1,0:T(8,128)(2,1)S(1)} %collective-permute-done.6.held), channel_id=1, source_target_pairs={{0,1},{1,0},{2,3},{3,2},{4,5},{5,4},{6,7},{7,6},{8,9},{9,8},{10,11... | collective-permute-start | bytes 73736 | tf_op jit(solution)/shard_map/ppermute | solution.py:313

commit v10 on v9

--- a/solution.py
+++ b/solution.py
@@ -122,7 +122,7 @@
 def whole_kernel(mine, other, take, power, first, out, wide):
     upper = (lax.axis_index("acq") >> 2) & 1
     blocks, looks = mine.shape[1], mine.shape[3]
-    columns = []
+    sums = 0.0
     for j in range(blocks):
         for part in range(2):
             wide[part, j, : other.shape[1]] = other[part, :, j * LANES : (j + 1) * LANES].astype(F32)
@@ -131,8 +131,7 @@
             their_re, their_im = (wide[part, j, pl.ds(i, looks, stride=LOOK_A), :] for part in range(2))
             terms = products(mine[0, j, i], mine[1, j, i], their_re, their_im)
             total = total + jnp.concatenate(terms, axis=0)
-        columns.append(total)
-    sums = dot_in_two(jnp.concatenate(columns, axis=1), take[...])
+        sums = sums + dot_in_two(total, take[j * LANES : (j + 1) * LANES])
     whole = normalised(sums, power[...], (1 - 2 * upper).astype(F32))
     packed = jnp.concatenate([first[...], whole], axis=0)
     root = jnp.sqrt(jnp.abs(packed)) * UNIT

time: 23.3 us -> 23.3 us (level)
  no operation moved by 1% of the time
where the time goes in v10:
time: 23.3 us; the launch traced here: 23.1 us
  starting transfers between devices  11.5 us (49%)
  waiting for transfers between devices  7.16 us (31%)
  Pallas kernels  3.4 us (15%)
  local copies, waits for them, and re-layouts  0.99 us (4%)
    ppermute x4, starting transfers between devices, across(): return lax.ppermute(value, ('acq', 'rng'), pairs)  5.29 us
    ppermute x4, waiting for transfers between devices, across(): return lax.ppermute(value, ('acq', 'rng'), pairs)  4.26 us
    ppermute x1, starting transfers between devices, per_device(): whole = lax.ppermute(own, 'acq', list(enumerate(quarter)))  4.04 us
    pallas_call x2, Pallas kernels, geocode_half(): pl.pallas_call(kernel, out_shape=jax.ShapeDtypeStruct(shape, F32), in_spe...  1.85 us
    ppermute x1, waiting for transfers between devices, per_device(): lax.ppermute(pick(own), 'acq', [(a, a ^ 1) for a in range(acq_count)])  1.57 us
    ppermute x1, starting transfers between devices, per_device(): lax.ppermute(pick(own), 'acq', [(a, a ^ 1) for a in range(acq_count)])  1.56 us
    ppermute x3, waiting for transfers between devices, swap(): return lax.ppermute(value, 'rng', [(0, 1), (1, 0)])  1.32 us
    unnamed x6, local copies, waits for them, and re-layouts  0.99 us
  transfers between devices with their start and end apart: 9, of which 7 were waited for; matrix products, arithmetic and copies ran while one was open for 0% of the time, Pallas kernels for 8%

profile of v10, /device:TPU:0, one launch (start us, length us, event | category | flops | bytes accessed | tf_op | source)
XLA Modules:
  0.0 23.1 jit_solution(12313914539031742781)
XLA Ops:
  0.0 4.0 %collective-permute-start.2 = (bf16[2,64,1024]{2,1,0:T(8,128)(2,1)}, bf16[2,64,1024]{2,1,0:T(8,128)(2,1)S(1)}, u32[]{:S(2)}, u32[]{:S(2)}) collective-permute-start(bf16[2,64,1024]{2,1,0:T(8,128)(2,1)} %bitcast.2), channel_id=1, source_target_pairs={{0,8},{2,10},{4,0},{6,2},{8,12},{10,14},{12,4},{14,6},{1,9},{3,11}... | collective-permute-start | bytes 786440 | tf_op jit(solution)/shard_map/ppermute | solution.py:365
  4.0 1.0 %copy-done = bf16[2,1,64,1024]{3,2,1,0:T(8,128)(2,1)S(1)} copy-done((bf16[2,1,64,1024]{3,2,1,0:T(8,128)(2,1)S(1)}, bf16[2,1,64,1024]{3,2,1,0:T(8,128)(2,1)}, u32[]{:S(2)}) %copy-start) | copy-done | bytes 262168
  5.0 1.6 %collective-permute-start = (bf16[2,32,1024]{2,1,0:T(8,128)(2,1)S(1)}, bf16[2,32,1024]{2,1,0:T(8,128)(2,1)S(1)}, u32[]{:S(2)}, u32[]{:S(2)}) collective-permute-start(bf16[2,32,1024]{2,1,0:T(8,128)(2,1)S(1)} %pick.1), channel_id=1, source_target_pairs={{0,2},{2,0},{4,6},{6,4},{8,10},{10,8},{12,14},{14,12},{1,3},{3,1},... | collective-permute-start | bytes 393224 | tf_op jit(solution)/shard_map/ppermute | solution.py:366
  6.6 0.0 collective-permute-start.1
  6.6 0.1 taking.1.take
  6.7 1.1 %collective-permute-done.1.other_cells = s32[8,128]{1,0:T(8,128)S(1)} collective-permute-done((s32[8,128]{1,0:T(8,128)S(1)}, s32[8,128]{1,0:T(8,128)S(1)}, u32[]{:S(2)}, u32[]{:S(2)}) %collective-permute-start.1) | collective-permute-done | bytes 4128 | tf_op jit(solution)/shard_map/ppermute | solution.py:312
  7.8 0.7 %select.1 = (bf16[256,256]{1,0:T(8,128)(2,1)S(1)}, bf16[2048,256]{1,0:T(8,128)(2,1)S(1)}, f32[32,256]{1,0:T(8,128)S(1)}, f32[4,256]{1,0:T(4,128)S(1)}) custom-call(s32[8,128]{1,0:T(8,128)S(1)} %copy-done.2, s32[8,128]{1,0:T(8,128)S(1)} %collective-permute-done.1.other_cells), custom_call_target="tpu_custom_call" | custom-call | flops 2097152 | bytes 1048576 | tf_op jit(solution)/shard_map/select/pallas_call | solution.py:206
  8.5 1.6 %collective-permute-done.other = bf16[2,32,1024]{2,1,0:T(8,128)(2,1)S(1)} collective-permute-done((bf16[2,32,1024]{2,1,0:T(8,128)(2,1)S(1)}, bf16[2,32,1024]{2,1,0:T(8,128)(2,1)S(1)}, u32[]{:S(2)}, u32[]{:S(2)}) %collective-permute-start) | collective-permute-done | bytes 131104 | tf_op jit(solution)/shard_map/ppermute | solution.py:366
  10.1 0.4 %first_matching.1 = (f32[8,128]{1,0:T(8,128)S(1)}, f32[8,128]{1,0:T(8,128)S(1)}, f32[2,8,8,8,128]{4,3,2,1,0:T(8,128)S(1)}) custom-call(bf16[2,64,1024]{2,1,0:T(8,128)(2,1)S(1)} %bitcast.4, bf16[2,32,1024]{2,1,0:T(8,128)(2,1)S(1)} %collective-permute-done.other, bf16[1024,128]{1,0:T(8,128)(2,1)S(1)} %taking.1.take), custom_call_target="tpu_custom_call" | custom-call | flops 2097152 | bytes 262144 | tf_op jit(solution)/shard_map/first_matching/pallas_call | solution.py:110
  10.5 0.0 collective-permute-done.2.other
  10.5 0.3 %whole_pair.1 = s16[24,128]{1,0:T(8,128)(2,1)S(1)} custom-call(f32[2,8,8,8,128]{4,3,2,1,0:T(8,128)S(1)} %get-tuple-element.22.mine, bf16[2,64,1024]{2,1,0:T(8,128)(2,1)S(1)} %collective-permute-done.2.other, bf16[1024,128]{1,0:T(8,128)(2,1)S(1)} %taking.1.take, f32[8,128]{1,0:T(8,128)S(1)} %get-tuple-element.23.power, f32[8,128]{1,0:T(8,128)S(1)} %get-tuple-element.24.first), custom_call_target="tpu_custom_call" | custom-call | flops 2097152 | bytes 262144 | tf_op jit(solution)/shard_map/whole_pair/pallas_call | solution.py:144
  10.8 1.4 %collective-permute-start.3 = (s16[1,24,128]{2,1,0:T(8,128)(2,1)S(1)}, s16[1,24,128]{2,1,0:T(8,128)(2,1)S(1)}, u32[]{:S(2)}, u32[]{:S(2)}) collective-permute-start(s16[1,24,128]{2,1,0:T(8,128)(2,1)S(1)} %bitcast.5), channel_id=1, source_target_pairs={{0,13},{1,12},{2,15},{3,14},{4,9},{5,8},{6,11},{7,10},{8,5},{9,4},... | collective-permute-start | bytes 18440 | tf_op jit(solution)/shard_map/ppermute | solution.py:308
  12.3 1.5 %collective-permute-start.4 = (s16[1,24,128]{2,1,0:T(8,128)(2,1)S(1)}, s16[1,24,128]{2,1,0:T(8,128)(2,1)S(1)}, u32[]{:S(2)}, u32[]{:S(2)}) collective-permute-start(s16[1,24,128]{2,1,0:T(8,128)(2,1)S(1)} %bitcast.6), channel_id=1, source_target_pairs={{0,9},{1,8},{2,11},{3,10},{4,13},{5,12},{6,15},{7,14},{8,1},{9,0},... | collective-permute-start | bytes 18440 | tf_op jit(solution)/shard_map/ppermute | solution.py:308
  13.8 0.3 %collective-permute-start.5 = (s16[1,24,128]{2,1,0:T(8,128)(2,1)S(1)}, s16[1,24,128]{2,1,0:T(8,128)(2,1)S(1)}, u32[]{:S(2)}, u32[]{:S(2)}) collective-permute-start(s16[1,24,128]{2,1,0:T(8,128)(2,1)S(1)} %bitcast.7), channel_id=1, source_target_pairs={{0,5},{1,4},{2,7},{3,6},{4,1},{5,0},{6,3},{7,2},{8,13},{9,12},{10,... | collective-permute-start | bytes 18440 | tf_op jit(solution)/shard_map/ppermute | solution.py:308
  14.1 1.7 %collective-permute-done.3 = s16[1,24,128]{2,1,0:T(8,128)(2,1)S(1)} collective-permute-done((s16[1,24,128]{2,1,0:T(8,128)(2,1)S(1)}, s16[1,24,128]{2,1,0:T(8,128)(2,1)S(1)}, u32[]{:S(2)}, u32[]{:S(2)}) %collective-permute-start.3) | collective-permute-done | bytes 6176 | tf_op jit(solution)/shard_map/ppermute | solution.py:308
  15.7 0.5 %collective-permute-done.4 = s16[1,24,128]{2,1,0:T(8,128)(2,1)S(1)} collective-permute-done((s16[1,24,128]{2,1,0:T(8,128)(2,1)S(1)}, s16[1,24,128]{2,1,0:T(8,128)(2,1)S(1)}, u32[]{:S(2)}, u32[]{:S(2)}) %collective-permute-start.4) | collective-permute-done | bytes 6176 | tf_op jit(solution)/shard_map/ppermute | solution.py:308
  16.2 0.6 %collective-permute-done.5 = s16[1,24,128]{2,1,0:T(8,128)(2,1)S(1)} collective-permute-done((s16[1,24,128]{2,1,0:T(8,128)(2,1)S(1)}, s16[1,24,128]{2,1,0:T(8,128)(2,1)S(1)}, u32[]{:S(2)}, u32[]{:S(2)}) %collective-permute-start.5) | collective-permute-done | bytes 6176 | tf_op jit(solution)/shard_map/ppermute | solution.py:308
  16.8 2.1 %collective-permute-start.6 = (s16[4,24,128]{2,1,0:T(8,128)(2,1)S(1)}, s16[4,24,128]{2,1,0:T(8,128)(2,1)S(1)}, u32[]{:S(2)}, u32[]{:S(2)}) collective-permute-start(s16[4,24,128]{2,1,0:T(8,128)(2,1)S(1)} %pad_add_fusion.held), channel_id=1, source_target_pairs={{0,3},{1,2},{2,1},{3,0},{4,7},{5,6},{6,5},{7,4},{8,11},{9,10},{10,... | collective-permute-start | bytes 73736 | tf_op jit(solution)/shard_map/ppermute | solution.py:308
  18.9 0.0 collective-permute-start.8
  18.9 1.5 %collective-permute-done.6.held = s16[4,24,128]{2,1,0:T(8,128)(2,1)S(1)} collective-permute-done((s16[4,24,128]{2,1,0:T(8,128)(2,1)S(1)}, s16[4,24,128]{2,1,0:T(8,128)(2,1)S(1)}, u32[]{:S(2)}, u32[]{:S(2)}) %collective-permute-start.6) | collective-permute-done | bytes 24608 | tf_op jit(solution)/shard_map/ppermute | solution.py:308
  20.4 0.6 %collective-permute-start.7 = (s16[4,24,128]{2,1,0:T(8,128)(2,1)S(1)}, s16[4,24,128]{2,1,0:T(8,128)(2,1)S(1)}, u32[]{:S(2)}, u32[]{:S(2)}) collective-permute-start(s16[4,24,128]{2,1,0:T(8,128)(2,1)S(1)} %collective-permute-done.6.held), channel_id=1, source_target_pairs={{0,1},{1,0},{2,3},{3,2},{4,5},{5,4},{6,7},{7,6},{8,9},{9,8},{10,11... | collective-permute-start | bytes 73736 | tf_op jit(solution)/shard_map/ppermute | solution.py:312
  21.0 0.6 %near_line.1.near = f32[4,16,256]{2,1,0:T(8,128)S(1)} custom-call(s16[4,24,128]{2,1,0:T(8,128)(2,1)S(1)} %pad_add_fusion.held, s16[4,24,128]{2,1,0:T(8,128)(2,1)S(1)} %collective-permute-done.8.sent, bf16[256,256]{1,0:T(8,128)(2,1)S(1)} %get-tuple-element.25.band, bf16[2048,256]{1,0:T(8,128)(2,1)S(1)} %get-tuple-element.26.onehot, ...), custom_call_target="tpu_custom_call" | custom-call | flops 2097152 | bytes 1048576 | tf_op jit(solution)/shard_map/near_line/pallas_call | solution.py:290
  21.6 0.2 %collective-permute-done.7.sent = s16[4,24,128]{2,1,0:T(8,128)(2,1)S(1)} collective-permute-done((s16[4,24,128]{2,1,0:T(8,128)(2,1)S(1)}, s16[4,24,128]{2,1,0:T(8,128)(2,1)S(1)}, u32[]{:S(2)}, u32[]{:S(2)}) %collective-permute-start.7) | collective-permute-done | bytes 24608 | tf_op jit(solution)/shard_map/ppermute | solution.py:312
  21.9 1.3 %far_line.1 = f32[3,4,2,1024]{3,2,1,0:T(2,128)} custom-call(s16[4,24,128]{2,1,0:T(8,128)(2,1)S(1)} %collective-permute-done.6.held, s16[4,24,128]{2,1,0:T(8,128)(2,1)S(1)} %collective-permute-done.7.sent, bf16[256,256]{1,0:T(8,128)(2,1)S(1)} %get-tuple-element.25.band, bf16[2048,256]{1,0:T(8,128)(2,1)S(1)} %get-tuple-element.26.onehot, ...), custom_call_target="tpu_custom_call" | custom-call | flops 2097152 | bytes 1048576 | tf_op jit(solution)/shard_map/far_line/pallas_call | solution.py:290
  (8 shorter events, 0.0 us)
Async XLA Ops:
  0.0 10.5 %collective-permute-start.2 = (bf16[2,64,1024]{2,1,0:T(8,128)(2,1)}, bf16[2,64,1024]{2,1,0:T(8,128)(2,1)S(1)}, u32[]{:S(2)}, u32[]{:S(2)}) collective-permute-start(bf16[2,64,1024]{2,1,0:T(8,128)(2,1)} %bitcast.2), channel_id=1, source_target_pairs={{0,8},{2,10},{4,0},{6,2},{8,12},{10,14},{12,4},{14,6},{1,9},{3,11}... | collective-permute-start | bytes 786440 | tf_op jit(solution)/shard_map/ppermute | solution.py:365
  4.0 1.0 %copy-start = (bf16[2,1,64,1024]{3,2,1,0:T(8,128)(2,1)S(1)}, bf16[2,1,64,1024]{3,2,1,0:T(8,128)(2,1)}, u32[]{:S(2)}) copy-start(bf16[2,1,64,1024]{3,2,1,0:T(8,128)(2,1)} %param.2) | copy-start | bytes 786436
  5.0 1.6 %copy-start.2 = (s32[8,128]{1,0:T(8,128)S(1)}, s32[8,128]{1,0:T(8,128)}, u32[]{:S(2)}) copy-start(s32[8,128]{1,0:T(8,128)} %own_cells.1) | copy-start | bytes 12292
  5.0 5.1 %copy-start.1 = (bf16[2,1,64,1024]{3,2,1,0:T(8,128)(2,1)S(1)}, bf16[2,1,64,1024]{3,2,1,0:T(8,128)(2,1)}, u32[]{:S(2)}) copy-start(bf16[2,1,64,1024]{3,2,1,0:T(8,128)(2,1)} %param.2) | copy-start | bytes 786436
  5.0 5.0 %collective-permute-start = (bf16[2,32,1024]{2,1,0:T(8,128)(2,1)S(1)}, bf16[2,32,1024]{2,1,0:T(8,128)(2,1)S(1)}, u32[]{:S(2)}, u32[]{:S(2)}) collective-permute-start(bf16[2,32,1024]{2,1,0:T(8,128)(2,1)S(1)} %pick.1), channel_id=1, source_target_pairs={{0,2},{2,0},{4,6},{6,4},{8,10},{10,8},{12,14},{14,12},{1,3},{3,1},... | collective-permute-start | bytes 393224 | tf_op jit(solution)/shard_map/ppermute | solution.py:366
  6.6 1.2 %collective-permute-start.1 = (s32[8,128]{1,0:T(8,128)S(1)}, s32[8,128]{1,0:T(8,128)S(1)}, u32[]{:S(2)}, u32[]{:S(2)}) collective-permute-start(s32[8,128]{1,0:T(8,128)S(1)} %copy-done.2), channel_id=1, source_target_pairs={{0,1},{1,0},{2,3},{3,2},{4,5},{5,4},{6,7},{7,6},{8,9},{9,8},{10,11... | collective-permute-start | bytes 12296 | tf_op jit(solution)/shard_map/ppermute | solution.py:312
  10.8 4.9 %collective-permute-start.3 = (s16[1,24,128]{2,1,0:T(8,128)(2,1)S(1)}, s16[1,24,128]{2,1,0:T(8,128)(2,1)S(1)}, u32[]{:S(2)}, u32[]{:S(2)}) collective-permute-start(s16[1,24,128]{2,1,0:T(8,128)(2,1)S(1)} %bitcast.5), channel_id=1, source_target_pairs={{0,13},{1,12},{2,15},{3,14},{4,9},{5,8},{6,11},{7,10},{8,5},{9,4},... | collective-permute-start | bytes 18440 | tf_op jit(solution)/shard_map/ppermute | solution.py:308
  12.3 4.0 %collective-permute-start.4 = (s16[1,24,128]{2,1,0:T(8,128)(2,1)S(1)}, s16[1,24,128]{2,1,0:T(8,128)(2,1)S(1)}, u32[]{:S(2)}, u32[]{:S(2)}) collective-permute-start(s16[1,24,128]{2,1,0:T(8,128)(2,1)S(1)} %bitcast.6), channel_id=1, source_target_pairs={{0,9},{1,8},{2,11},{3,10},{4,13},{5,12},{6,15},{7,14},{8,1},{9,0},... | collective-permute-start | bytes 18440 | tf_op jit(solution)/shard_map/ppermute | solution.py:308
  13.8 3.1 %collective-permute-start.5 = (s16[1,24,128]{2,1,0:T(8,128)(2,1)S(1)}, s16[1,24,128]{2,1,0:T(8,128)(2,1)S(1)}, u32[]{:S(2)}, u32[]{:S(2)}) collective-permute-start(s16[1,24,128]{2,1,0:T(8,128)(2,1)S(1)} %bitcast.7), channel_id=1, source_target_pairs={{0,5},{1,4},{2,7},{3,6},{4,1},{5,0},{6,3},{7,2},{8,13},{9,12},{10,... | collective-permute-start | bytes 18440 | tf_op jit(solution)/shard_map/ppermute | solution.py:308
  16.8 3.6 %collective-permute-start.6 = (s16[4,24,128]{2,1,0:T(8,128)(2,1)S(1)}, s16[4,24,128]{2,1,0:T(8,128)(2,1)S(1)}, u32[]{:S(2)}, u32[]{:S(2)}) collective-permute-start(s16[4,24,128]{2,1,0:T(8,128)(2,1)S(1)} %pad_add_fusion.held), channel_id=1, source_target_pairs={{0,3},{1,2},{2,1},{3,0},{4,7},{5,6},{6,5},{7,4},{8,11},{9,10},{10,... | collective-permute-start | bytes 73736 | tf_op jit(solution)/shard_map/ppermute | solution.py:308
  18.9 2.2 %collective-permute-start.8 = (s16[4,24,128]{2,1,0:T(8,128)(2,1)S(1)}, s16[4,24,128]{2,1,0:T(8,128)(2,1)S(1)}, u32[]{:S(2)}, u32[]{:S(2)}) collective-permute-start(s16[4,24,128]{2,1,0:T(8,128)(2,1)S(1)} %pad_add_fusion.held), channel_id=1, source_target_pairs={{0,1},{1,0},{2,3},{3,2},{4,5},{5,4},{6,7},{7,6},{8,9},{9,8},{10,11... | collective-permute-start | bytes 73736 | tf_op jit(solution)/shard_map/ppermute | solution.py:312
  20.4 1.5 %collective-permute-start.7 = (s16[4,24,128]{2,1,0:T(8,128)(2,1)S(1)}, s16[4,24,128]{2,1,0:T(8,128)(2,1)S(1)}, u32[]{:S(2)}, u32[]{:S(2)}) collective-permute-start(s16[4,24,128]{2,1,0:T(8,128)(2,1)S(1)} %collective-permute-done.6.held), channel_id=1, source_target_pairs={{0,1},{1,0},{2,3},{3,2},{4,5},{5,4},{6,7},{7,6},{8,9},{9,8},{10,11... | collective-permute-start | bytes 73736 | tf_op jit(solution)/shard_map/ppermute | solution.py:312

commit v11 on v10

--- a/solution.py
+++ b/solution.py
@@ -257,7 +257,9 @@
         both = jnp.concatenate([top, value - top], axis=0)
         rows = [both * masks[line * blocks + block : line * blocks + block + 1, :] for block in range(blocks)]
         left.append(jnp.concatenate(rows, axis=0).astype(BF16))
-    sums = dot(jnp.concatenate(left, axis=1), onehot[...])
+    middle = lines // 2
+    sums = dot(jnp.concatenate(left[:middle], axis=1), onehot[: middle * 2 * cols, :])
+    sums = sums + dot(jnp.concatenate(left[middle:], axis=1), onehot[middle * 2 * cols :, :])
     starts = [block * 2 * planes for block in range(blocks)]
     return [sums[start : start + planes] + sums[start + planes : start + 2 * planes] for start in starts]
 

time: 23.3 us -> 23.3 us (level)
  no operation moved by 1% of the time
where the time goes in v11:
time: 23.3 us; the launch traced here: 23.1 us
  starting transfers between devices  11.5 us (49%)
  waiting for transfers between devices  7.16 us (31%)
  Pallas kernels  3.39 us (15%)
  local copies, waits for them, and re-layouts  0.99 us (4%)
    ppermute x4, starting transfers between devices, across(): return lax.ppermute(value, ('acq', 'rng'), pairs)  5.29 us
    ppermute x4, waiting for transfers between devices, across(): return lax.ppermute(value, ('acq', 'rng'), pairs)  4.26 us
    ppermute x1, starting transfers between devices, per_device(): whole = lax.ppermute(own, 'acq', list(enumerate(quarter)))  4.04 us
    pallas_call x2, Pallas kernels, geocode_half(): pl.pallas_call(kernel, out_shape=jax.ShapeDtypeStruct(shape, F32), in_spe...  1.85 us
    ppermute x1, waiting for transfers between devices, per_device(): lax.ppermute(pick(own), 'acq', [(a, a ^ 1) for a in range(acq_count)])  1.57 us
    ppermute x1, starting transfers between devices, per_device(): lax.ppermute(pick(own), 'acq', [(a, a ^ 1) for a in range(acq_count)])  1.56 us
    ppermute x3, waiting for transfers between devices, swap(): return lax.ppermute(value, 'rng', [(0, 1), (1, 0)])  1.32 us
    unnamed x6, local copies, waits for them, and re-layouts  0.99 us
  transfers between devices with their start and end apart: 9, of which 7 were waited for; matrix products, arithmetic and copies ran while one was open for 0% of the time, Pallas kernels for 8%

profile of v11, /device:TPU:0, one launch (start us, length us, event | category | flops | bytes accessed | tf_op | source)
XLA Modules:
  0.0 23.1 jit_solution(15497939625156945150)
XLA Ops:
  0.0 4.0 %collective-permute-start.2 = (bf16[2,64,1024]{2,1,0:T(8,128)(2,1)}, bf16[2,64,1024]{2,1,0:T(8,128)(2,1)S(1)}, u32[]{:S(2)}, u32[]{:S(2)}) collective-permute-start(bf16[2,64,1024]{2,1,0:T(8,128)(2,1)} %bitcast.2), channel_id=1, source_target_pairs={{0,8},{2,10},{4,0},{6,2},{8,12},{10,14},{12,4},{14,6},{1,9},{3,11}... | collective-permute-start | bytes 786440 | tf_op jit(solution)/shard_map/ppermute | solution.py:367
  4.0 1.0 %copy-done = bf16[2,1,64,1024]{3,2,1,0:T(8,128)(2,1)S(1)} copy-done((bf16[2,1,64,1024]{3,2,1,0:T(8,128)(2,1)S(1)}, bf16[2,1,64,1024]{3,2,1,0:T(8,128)(2,1)}, u32[]{:S(2)}) %copy-start) | copy-done | bytes 262168
  5.0 1.6 %collective-permute-start = (bf16[2,32,1024]{2,1,0:T(8,128)(2,1)S(1)}, bf16[2,32,1024]{2,1,0:T(8,128)(2,1)S(1)}, u32[]{:S(2)}, u32[]{:S(2)}) collective-permute-start(bf16[2,32,1024]{2,1,0:T(8,128)(2,1)S(1)} %pick.1), channel_id=1, source_target_pairs={{0,2},{2,0},{4,6},{6,4},{8,10},{10,8},{12,14},{14,12},{1,3},{3,1},... | collective-permute-start | bytes 393224 | tf_op jit(solution)/shard_map/ppermute | solution.py:368
  6.6 0.0 collective-permute-start.1
  6.6 0.1 taking.1.take
  6.7 1.1 %collective-permute-done.1.other_cells = s32[8,128]{1,0:T(8,128)S(1)} collective-permute-done((s32[8,128]{1,0:T(8,128)S(1)}, s32[8,128]{1,0:T(8,128)S(1)}, u32[]{:S(2)}, u32[]{:S(2)}) %collective-permute-start.1) | collective-permute-done | bytes 4128 | tf_op jit(solution)/shard_map/ppermute | solution.py:314
  7.8 0.7 %select.1 = (bf16[256,256]{1,0:T(8,128)(2,1)S(1)}, bf16[2048,256]{1,0:T(8,128)(2,1)S(1)}, f32[32,256]{1,0:T(8,128)S(1)}, f32[4,256]{1,0:T(4,128)S(1)}) custom-call(s32[8,128]{1,0:T(8,128)S(1)} %copy-done.2, s32[8,128]{1,0:T(8,128)S(1)} %collective-permute-done.1.other_cells), custom_call_target="tpu_custom_call" | custom-call | flops 2097152 | bytes 1048576 | tf_op jit(solution)/shard_map/select/pallas_call | solution.py:206
  8.5 1.6 %collective-permute-done.other = bf16[2,32,1024]{2,1,0:T(8,128)(2,1)S(1)} collective-permute-done((bf16[2,32,1024]{2,1,0:T(8,128)(2,1)S(1)}, bf16[2,32,1024]{2,1,0:T(8,128)(2,1)S(1)}, u32[]{:S(2)}, u32[]{:S(2)}) %collective-permute-start) | collective-permute-done | bytes 131104 | tf_op jit(solution)/shard_map/ppermute | solution.py:368
  10.1 0.4 %first_matching.1 = (f32[8,128]{1,0:T(8,128)S(1)}, f32[8,128]{1,0:T(8,128)S(1)}, f32[2,8,8,8,128]{4,3,2,1,0:T(8,128)S(1)}) custom-call(bf16[2,64,1024]{2,1,0:T(8,128)(2,1)S(1)} %bitcast.4, bf16[2,32,1024]{2,1,0:T(8,128)(2,1)S(1)} %collective-permute-done.other, bf16[1024,128]{1,0:T(8,128)(2,1)S(1)} %taking.1.take), custom_call_target="tpu_custom_call" | custom-call | flops 2097152 | bytes 262144 | tf_op jit(solution)/shard_map/first_matching/pallas_call | solution.py:110
  10.5 0.0 collective-permute-done.2.other
  10.5 0.3 %whole_pair.1 = s16[24,128]{1,0:T(8,128)(2,1)S(1)} custom-call(f32[2,8,8,8,128]{4,3,2,1,0:T(8,128)S(1)} %get-tuple-element.22.mine, bf16[2,64,1024]{2,1,0:T(8,128)(2,1)S(1)} %collective-permute-done.2.other, bf16[1024,128]{1,0:T(8,128)(2,1)S(1)} %taking.1.take, f32[8,128]{1,0:T(8,128)S(1)} %get-tuple-element.23.power, f32[8,128]{1,0:T(8,128)S(1)} %get-tuple-element.24.first), custom_call_target="tpu_custom_call" | custom-call | flops 2097152 | bytes 262144 | tf_op jit(solution)/shard_map/whole_pair/pallas_call | solution.py:144
  10.8 1.4 %collective-permute-start.3 = (s16[1,24,128]{2,1,0:T(8,128)(2,1)S(1)}, s16[1,24,128]{2,1,0:T(8,128)(2,1)S(1)}, u32[]{:S(2)}, u32[]{:S(2)}) collective-permute-start(s16[1,24,128]{2,1,0:T(8,128)(2,1)S(1)} %bitcast.5), channel_id=1, source_target_pairs={{0,13},{1,12},{2,15},{3,14},{4,9},{5,8},{6,11},{7,10},{8,5},{9,4},... | collective-permute-start | bytes 18440 | tf_op jit(solution)/shard_map/ppermute | solution.py:310
  12.3 1.5 %collective-permute-start.4 = (s16[1,24,128]{2,1,0:T(8,128)(2,1)S(1)}, s16[1,24,128]{2,1,0:T(8,128)(2,1)S(1)}, u32[]{:S(2)}, u32[]{:S(2)}) collective-permute-start(s16[1,24,128]{2,1,0:T(8,128)(2,1)S(1)} %bitcast.6), channel_id=1, source_target_pairs={{0,9},{1,8},{2,11},{3,10},{4,13},{5,12},{6,15},{7,14},{8,1},{9,0},... | collective-permute-start | bytes 18440 | tf_op jit(solution)/shard_map/ppermute | solution.py:310
  13.8 0.3 %collective-permute-start.5 = (s16[1,24,128]{2,1,0:T(8,128)(2,1)S(1)}, s16[1,24,128]{2,1,0:T(8,128)(2,1)S(1)}, u32[]{:S(2)}, u32[]{:S(2)}) collective-permute-start(s16[1,24,128]{2,1,0:T(8,128)(2,1)S(1)} %bitcast.7), channel_id=1, source_target_pairs={{0,5},{1,4},{2,7},{3,6},{4,1},{5,0},{6,3},{7,2},{8,13},{9,12},{10,... | collective-permute-start | bytes 18440 | tf_op jit(solution)/shard_map/ppermute | solution.py:310
  14.1 1.7 %collective-permute-done.3 = s16[1,24,128]{2,1,0:T(8,128)(2,1)S(1)} collective-permute-done((s16[1,24,128]{2,1,0:T(8,128)(2,1)S(1)}, s16[1,24,128]{2,1,0:T(8,128)(2,1)S(1)}, u32[]{:S(2)}, u32[]{:S(2)}) %collective-permute-start.3) | collective-permute-done | bytes 6176 | tf_op jit(solution)/shard_map/ppermute | solution.py:310
  15.7 0.5 %collective-permute-done.4 = s16[1,24,128]{2,1,0:T(8,128)(2,1)S(1)} collective-permute-done((s16[1,24,128]{2,1,0:T(8,128)(2,1)S(1)}, s16[1,24,128]{2,1,0:T(8,128)(2,1)S(1)}, u32[]{:S(2)}, u32[]{:S(2)}) %collective-permute-start.4) | collective-permute-done | bytes 6176 | tf_op jit(solution)/shard_map/ppermute | solution.py:310
  16.2 0.6 %collective-permute-done.5 = s16[1,24,128]{2,1,0:T(8,128)(2,1)S(1)} collective-permute-done((s16[1,24,128]{2,1,0:T(8,128)(2,1)S(1)}, s16[1,24,128]{2,1,0:T(8,128)(2,1)S(1)}, u32[]{:S(2)}, u32[]{:S(2)}) %collective-permute-start.5) | collective-permute-done | bytes 6176 | tf_op jit(solution)/shard_map/ppermute | solution.py:310
  16.8 2.1 %collective-permute-start.6 = (s16[4,24,128]{2,1,0:T(8,128)(2,1)S(1)}, s16[4,24,128]{2,1,0:T(8,128)(2,1)S(1)}, u32[]{:S(2)}, u32[]{:S(2)}) collective-permute-start(s16[4,24,128]{2,1,0:T(8,128)(2,1)S(1)} %pad_add_fusion.held), channel_id=1, source_target_pairs={{0,3},{1,2},{2,1},{3,0},{4,7},{5,6},{6,5},{7,4},{8,11},{9,10},{10,... | collective-permute-start | bytes 73736 | tf_op jit(solution)/shard_map/ppermute | solution.py:310
  18.9 0.0 collective-permute-start.8
  18.9 1.5 %collective-permute-done.6.held = s16[4,24,128]{2,1,0:T(8,128)(2,1)S(1)} collective-permute-done((s16[4,24,128]{2,1,0:T(8,128)(2,1)S(1)}, s16[4,24,128]{2,1,0:T(8,128)(2,1)S(1)}, u32[]{:S(2)}, u32[]{:S(2)}) %collective-permute-start.6) | collective-permute-done | bytes 24608 | tf_op jit(solution)/shard_map/ppermute | solution.py:310
  20.4 0.6 %collective-permute-start.7 = (s16[4,24,128]{2,1,0:T(8,128)(2,1)S(1)}, s16[4,24,128]{2,1,0:T(8,128)(2,1)S(1)}, u32[]{:S(2)}, u32[]{:S(2)}) collective-permute-start(s16[4,24,128]{2,1,0:T(8,128)(2,1)S(1)} %collective-permute-done.6.held), channel_id=1, source_target_pairs={{0,1},{1,0},{2,3},{3,2},{4,5},{5,4},{6,7},{7,6},{8,9},{9,8},{10,11... | collective-permute-start | bytes 73736 | tf_op jit(solution)/shard_map/ppermute | solution.py:314
  21.0 0.6 %near_line.1.near = f32[4,16,256]{2,1,0:T(8,128)S(1)} custom-call(s16[4,24,128]{2,1,0:T(8,128)(2,1)S(1)} %pad_add_fusion.held, s16[4,24,128]{2,1,0:T(8,128)(2,1)S(1)} %collective-permute-done.8.sent, bf16[256,256]{1,0:T(8,128)(2,1)S(1)} %get-tuple-element.25.band, bf16[2048,256]{1,0:T(8,128)(2,1)S(1)} %get-tuple-element.26.onehot, ...), custom_call_target="tpu_custom_call" | custom-call | flops 2097152 | bytes 1048576 | tf_op jit(solution)/shard_map/near_line/pallas_call | solution.py:292
  21.6 0.2 %collective-permute-done.7.sent = s16[4,24,128]{2,1,0:T(8,128)(2,1)S(1)} collective-permute-done((s16[4,24,128]{2,1,0:T(8,128)(2,1)S(1)}, s16[4,24,128]{2,1,0:T(8,128)(2,1)S(1)}, u32[]{:S(2)}, u32[]{:S(2)}) %collective-permute-start.7) | collective-permute-done | bytes 24608 | tf_op jit(solution)/shard_map/ppermute | solution.py:314
  21.9 1.3 %far_line.1 = f32[3,4,2,1024]{3,2,1,0:T(2,128)} custom-call(s16[4,24,128]{2,1,0:T(8,128)(2,1)S(1)} %collective-permute-done.6.held, s16[4,24,128]{2,1,0:T(8,128)(2,1)S(1)} %collective-permute-done.7.sent, bf16[256,256]{1,0:T(8,128)(2,1)S(1)} %get-tuple-element.25.band, bf16[2048,256]{1,0:T(8,128)(2,1)S(1)} %get-tuple-element.26.onehot, ...), custom_call_target="tpu_custom_call" | custom-call | flops 2097152 | bytes 1048576 | tf_op jit(solution)/shard_map/far_line/pallas_call | solution.py:292
  (8 shorter events, 0.0 us)
Async XLA Ops:
  0.0 10.5 %collective-permute-start.2 = (bf16[2,64,1024]{2,1,0:T(8,128)(2,1)}, bf16[2,64,1024]{2,1,0:T(8,128)(2,1)S(1)}, u32[]{:S(2)}, u32[]{:S(2)}) collective-permute-start(bf16[2,64,1024]{2,1,0:T(8,128)(2,1)} %bitcast.2), channel_id=1, source_target_pairs={{0,8},{2,10},{4,0},{6,2},{8,12},{10,14},{12,4},{14,6},{1,9},{3,11}... | collective-permute-start | bytes 786440 | tf_op jit(solution)/shard_map/ppermute | solution.py:367
  4.0 1.0 %copy-start = (bf16[2,1,64,1024]{3,2,1,0:T(8,128)(2,1)S(1)}, bf16[2,1,64,1024]{3,2,1,0:T(8,128)(2,1)}, u32[]{:S(2)}) copy-start(bf16[2,1,64,1024]{3,2,1,0:T(8,128)(2,1)} %param.2) | copy-start | bytes 786436
  5.0 1.6 %copy-start.2 = (s32[8,128]{1,0:T(8,128)S(1)}, s32[8,128]{1,0:T(8,128)}, u32[]{:S(2)}) copy-start(s32[8,128]{1,0:T(8,128)} %own_cells.1) | copy-start | bytes 12292
  5.0 5.1 %copy-start.1 = (bf16[2,1,64,1024]{3,2,1,0:T(8,128)(2,1)S(1)}, bf16[2,1,64,1024]{3,2,1,0:T(8,128)(2,1)}, u32[]{:S(2)}) copy-start(bf16[2,1,64,1024]{3,2,1,0:T(8,128)(2,1)} %param.2) | copy-start | bytes 786436
  5.0 5.0 %collective-permute-start = (bf16[2,32,1024]{2,1,0:T(8,128)(2,1)S(1)}, bf16[2,32,1024]{2,1,0:T(8,128)(2,1)S(1)}, u32[]{:S(2)}, u32[]{:S(2)}) collective-permute-start(bf16[2,32,1024]{2,1,0:T(8,128)(2,1)S(1)} %pick.1), channel_id=1, source_target_pairs={{0,2},{2,0},{4,6},{6,4},{8,10},{10,8},{12,14},{14,12},{1,3},{3,1},... | collective-permute-start | bytes 393224 | tf_op jit(solution)/shard_map/ppermute | solution.py:368
  6.6 1.2 %collective-permute-start.1 = (s32[8,128]{1,0:T(8,128)S(1)}, s32[8,128]{1,0:T(8,128)S(1)}, u32[]{:S(2)}, u32[]{:S(2)}) collective-permute-start(s32[8,128]{1,0:T(8,128)S(1)} %copy-done.2), channel_id=1, source_target_pairs={{0,1},{1,0},{2,3},{3,2},{4,5},{5,4},{6,7},{7,6},{8,9},{9,8},{10,11... | collective-permute-start | bytes 12296 | tf_op jit(solution)/shard_map/ppermute | solution.py:314
  10.8 4.9 %collective-permute-start.3 = (s16[1,24,128]{2,1,0:T(8,128)(2,1)S(1)}, s16[1,24,128]{2,1,0:T(8,128)(2,1)S(1)}, u32[]{:S(2)}, u32[]{:S(2)}) collective-permute-start(s16[1,24,128]{2,1,0:T(8,128)(2,1)S(1)} %bitcast.5), channel_id=1, source_target_pairs={{0,13},{1,12},{2,15},{3,14},{4,9},{5,8},{6,11},{7,10},{8,5},{9,4},... | collective-permute-start | bytes 18440 | tf_op jit(solution)/shard_map/ppermute | solution.py:310
  12.3 4.0 %collective-permute-start.4 = (s16[1,24,128]{2,1,0:T(8,128)(2,1)S(1)}, s16[1,24,128]{2,1,0:T(8,128)(2,1)S(1)}, u32[]{:S(2)}, u32[]{:S(2)}) collective-permute-start(s16[1,24,128]{2,1,0:T(8,128)(2,1)S(1)} %bitcast.6), channel_id=1, source_target_pairs={{0,9},{1,8},{2,11},{3,10},{4,13},{5,12},{6,15},{7,14},{8,1},{9,0},... | collective-permute-start | bytes 18440 | tf_op jit(solution)/shard_map/ppermute | solution.py:310
  13.8 3.1 %collective-permute-start.5 = (s16[1,24,128]{2,1,0:T(8,128)(2,1)S(1)}, s16[1,24,128]{2,1,0:T(8,128)(2,1)S(1)}, u32[]{:S(2)}, u32[]{:S(2)}) collective-permute-start(s16[1,24,128]{2,1,0:T(8,128)(2,1)S(1)} %bitcast.7), channel_id=1, source_target_pairs={{0,5},{1,4},{2,7},{3,6},{4,1},{5,0},{6,3},{7,2},{8,13},{9,12},{10,... | collective-permute-start | bytes 18440 | tf_op jit(solution)/shard_map/ppermute | solution.py:310
  16.8 3.6 %collective-permute-start.6 = (s16[4,24,128]{2,1,0:T(8,128)(2,1)S(1)}, s16[4,24,128]{2,1,0:T(8,128)(2,1)S(1)}, u32[]{:S(2)}, u32[]{:S(2)}) collective-permute-start(s16[4,24,128]{2,1,0:T(8,128)(2,1)S(1)} %pad_add_fusion.held), channel_id=1, source_target_pairs={{0,3},{1,2},{2,1},{3,0},{4,7},{5,6},{6,5},{7,4},{8,11},{9,10},{10,... | collective-permute-start | bytes 73736 | tf_op jit(solution)/shard_map/ppermute | solution.py:310
  18.9 2.2 %collective-permute-start.8 = (s16[4,24,128]{2,1,0:T(8,128)(2,1)S(1)}, s16[4,24,128]{2,1,0:T(8,128)(2,1)S(1)}, u32[]{:S(2)}, u32[]{:S(2)}) collective-permute-start(s16[4,24,128]{2,1,0:T(8,128)(2,1)S(1)} %pad_add_fusion.held), channel_id=1, source_target_pairs={{0,1},{1,0},{2,3},{3,2},{4,5},{5,4},{6,7},{7,6},{8,9},{9,8},{10,11... | collective-permute-start | bytes 73736 | tf_op jit(solution)/shard_map/ppermute | solution.py:314
  20.4 1.5 %collective-permute-start.7 = (s16[4,24,128]{2,1,0:T(8,128)(2,1)S(1)}, s16[4,24,128]{2,1,0:T(8,128)(2,1)S(1)}, u32[]{:S(2)}, u32[]{:S(2)}) collective-permute-start(s16[4,24,128]{2,1,0:T(8,128)(2,1)S(1)} %collective-permute-done.6.held), channel_id=1, source_target_pairs={{0,1},{1,0},{2,3},{3,2},{4,5},{5,4},{6,7},{7,6},{8,9},{9,8},{10,11... | collective-permute-start | bytes 73736 | tf_op jit(solution)/shard_map/ppermute | solution.py:314

commit v12 on v8

--- a/solution.py
+++ b/solution.py
@@ -122,7 +122,7 @@
 def whole_kernel(mine, other, take, power, first, out, wide):
     upper = (lax.axis_index("acq") >> 2) & 1
     blocks, looks = mine.shape[1], mine.shape[3]
-    columns = []
+    sums = 0.0
     for j in range(blocks):
         for part in range(2):
             wide[part, j, : other.shape[1]] = other[part, :, j * LANES : (j + 1) * LANES].astype(F32)
@@ -131,8 +131,7 @@
             their_re, their_im = (wide[part, j, pl.ds(i, looks, stride=LOOK_A), :] for part in range(2))
             terms = products(mine[0, j, i], mine[1, j, i], their_re, their_im)
             total = total + jnp.concatenate(terms, axis=0)
-        columns.append(total)
-    sums = dot_in_two(jnp.concatenate(columns, axis=1), take[...])
+        sums = sums + dot_in_two(total, take[j * LANES : (j + 1) * LANES])
     whole = normalised(sums, power[...], (1 - 2 * upper).astype(F32))
     packed = jnp.concatenate([first[...], whole], axis=0)
     root = jnp.sqrt(jnp.abs(packed)) * UNIT

time: 23.3 us -> 23.3 us (level)
  no operation moved by 1% of the time
where the time goes in v12:
time: 23.3 us; the launch traced here: 23.2 us
  starting transfers between devices  10 us (43%)
  waiting for transfers between devices  9.11 us (39%)
  Pallas kernels  2.9 us (12%)
  local copies, waits for them, and re-layouts  1.02 us (4%)
    ppermute x4, waiting for transfers between devices, across(): return lax.ppermute(value, ('acq', 'rng'), pairs)  5.64 us
    ppermute x1, starting transfers between devices, per_device(): whole = lax.ppermute(own, 'acq', list(enumerate(quarter)))  4.04 us
    ppermute x4, starting transfers between devices, across(): return lax.ppermute(value, ('acq', 'rng'), pairs)  3.9 us
    ppermute x3, waiting for transfers between devices, swap(): return lax.ppermute(value, 'rng', [(0, 1), (1, 0)])  1.9 us
    ppermute x1, waiting for transfers between devices, per_device(): lax.ppermute(pick(own), 'acq', [(a, a ^ 1) for a in range(acq_count)])  1.57 us
    ppermute x1, starting transfers between devices, per_device(): lax.ppermute(pick(own), 'acq', [(a, a ^ 1) for a in range(acq_count)])  1.56 us
    pallas_call x1, Pallas kernels, geocode(): pl.pallas_call(geocode_kernel, out_shape=jax.ShapeDtypeStruct((ROUNDS, pa...  1.34 us
    unnamed x10, local copies, waits for them, and re-layouts  1.02 us
  transfers between devices with their start and end apart: 9, of which 6 were waited for; matrix products, arithmetic and copies ran while one was open for 0% of the time, Pallas kernels for 5%

profile of v12, /device:TPU:0, one launch (start us, length us, event | category | flops | bytes accessed | tf_op | source)
XLA Modules:
  0.0 23.2 jit_solution(17202163750852874590)
XLA Ops:
  0.0 4.0 %collective-permute-start.2 = (bf16[2,64,1024]{2,1,0:T(8,128)(2,1)}, bf16[2,64,1024]{2,1,0:T(8,128)(2,1)S(1)}, u32[]{:S(2)}, u32[]{:S(2)}) collective-permute-start(bf16[2,64,1024]{2,1,0:T(8,128)(2,1)} %bitcast.3), channel_id=1, source_target_pairs={{0,8},{2,10},{4,0},{6,2},{8,12},{10,14},{12,4},{14,6},{1,9},{3,11}... | collective-permute-start | bytes 786440 | tf_op jit(solution)/shard_map/ppermute | solution.py:346
  4.0 1.0 %copy-done = bf16[2,1,64,1024]{3,2,1,0:T(8,128)(2,1)S(1)} copy-done((bf16[2,1,64,1024]{3,2,1,0:T(8,128)(2,1)S(1)}, bf16[2,1,64,1024]{3,2,1,0:T(8,128)(2,1)}, u32[]{:S(2)}) %copy-start) | copy-done | bytes 262168
  5.0 1.6 %collective-permute-start = (bf16[2,32,1024]{2,1,0:T(8,128)(2,1)S(1)}, bf16[2,32,1024]{2,1,0:T(8,128)(2,1)S(1)}, u32[]{:S(2)}, u32[]{:S(2)}) collective-permute-start(bf16[2,32,1024]{2,1,0:T(8,128)(2,1)S(1)} %pick.1), channel_id=1, source_target_pairs={{0,2},{2,0},{4,6},{6,4},{8,10},{10,8},{12,14},{14,12},{1,3},{3,1},... | collective-permute-start | bytes 393224 | tf_op jit(solution)/shard_map/ppermute | solution.py:347
  6.6 0.0 collective-permute-start.1
  6.6 0.1 taking.1.take
  6.7 1.1 %collective-permute-done.1.other_cells = s32[8,128]{1,0:T(8,128)S(1)} collective-permute-done((s32[8,128]{1,0:T(8,128)S(1)}, s32[8,128]{1,0:T(8,128)S(1)}, u32[]{:S(2)}, u32[]{:S(2)}) %collective-permute-start.1) | collective-permute-done | bytes 4128 | tf_op jit(solution)/shard_map/ppermute | solution.py:296
  7.8 0.7 %select.1 = (bf16[256,256]{1,0:T(8,128)(2,1)S(1)}, bf16[2048,256]{1,0:T(8,128)(2,1)S(1)}, f32[32,256]{1,0:T(8,128)S(1)}, f32[4,256]{1,0:T(4,128)S(1)}) custom-call(s32[8,128]{1,0:T(8,128)S(1)} %copy-done.2, s32[8,128]{1,0:T(8,128)S(1)} %collective-permute-done.1.other_cells), custom_call_target="tpu_custom_call" | custom-call | flops 2097152 | bytes 1048576 | tf_op jit(solution)/shard_map/select/pallas_call | solution.py:206
  8.5 1.6 %collective-permute-done.other = bf16[2,32,1024]{2,1,0:T(8,128)(2,1)S(1)} collective-permute-done((bf16[2,32,1024]{2,1,0:T(8,128)(2,1)S(1)}, bf16[2,32,1024]{2,1,0:T(8,128)(2,1)S(1)}, u32[]{:S(2)}, u32[]{:S(2)}) %collective-permute-start) | collective-permute-done | bytes 131104 | tf_op jit(solution)/shard_map/ppermute | solution.py:347
  10.1 0.4 %first_matching.1 = (f32[8,128]{1,0:T(8,128)S(1)}, f32[8,128]{1,0:T(8,128)S(1)}, f32[2,8,8,8,128]{4,3,2,1,0:T(8,128)S(1)}) custom-call(bf16[2,64,1024]{2,1,0:T(8,128)(2,1)S(1)} %bitcast.5, bf16[2,32,1024]{2,1,0:T(8,128)(2,1)S(1)} %collective-permute-done.other, bf16[1024,128]{1,0:T(8,128)(2,1)S(1)} %taking.1.take), custom_call_target="tpu_custom_call" | custom-call | flops 2097152 | bytes 262144 | tf_op jit(solution)/shard_map/first_matching/pallas_call | solution.py:110
  10.5 0.0 collective-permute-done.2.other
  10.5 0.3 %whole_pair.1 = s16[24,128]{1,0:T(8,128)(2,1)S(1)} custom-call(f32[2,8,8,8,128]{4,3,2,1,0:T(8,128)S(1)} %get-tuple-element.22.mine, bf16[2,64,1024]{2,1,0:T(8,128)(2,1)S(1)} %collective-permute-done.2.other, bf16[1024,128]{1,0:T(8,128)(2,1)S(1)} %taking.1.take, f32[8,128]{1,0:T(8,128)S(1)} %get-tuple-element.23.power, f32[8,128]{1,0:T(8,128)S(1)} %get-tuple-element.24.first), custom_call_target="tpu_custom_call" | custom-call | flops 2097152 | bytes 262144 | tf_op jit(solution)/shard_map/whole_pair/pallas_call | solution.py:144
  10.8 0.1 collective-permute-start.3
  10.9 3.0 %collective-permute-done.3 = s16[1,24,128]{2,1,0:T(8,128)(2,1)S(1)} collective-permute-done((s16[1,24,128]{2,1,0:T(8,128)(2,1)S(1)}, s16[1,24,128]{2,1,0:T(8,128)(2,1)S(1)}, u32[]{:S(2)}, u32[]{:S(2)}) %collective-permute-start.3) | collective-permute-done | bytes 6176 | tf_op jit(solution)/shard_map/ppermute | solution.py:292
  14.0 2.5 %collective-permute-start.4 = (s16[2,24,128]{2,1,0:T(8,128)(2,1)S(1)}, s16[2,24,128]{2,1,0:T(8,128)(2,1)S(1)}, u32[]{:S(2)}, u32[]{:S(2)}) collective-permute-start(s16[2,24,128]{2,1,0:T(8,128)(2,1)S(1)} %pad_add_fusion.3), channel_id=1, source_target_pairs={{0,13},{1,12},{2,15},{3,14},{4,9},{5,8},{6,11},{7,10},{8,5},{9,4},... | collective-permute-start | bytes 36872 | tf_op jit(solution)/shard_map/ppermute | solution.py:292
  16.5 0.4 %collective-permute-start.5 = (s16[2,24,128]{2,1,0:T(8,128)(2,1)S(1)}, s16[2,24,128]{2,1,0:T(8,128)(2,1)S(1)}, u32[]{:S(2)}, u32[]{:S(2)}) collective-permute-start(s16[2,24,128]{2,1,0:T(8,128)(2,1)S(1)} %pad_add_fusion.3), channel_id=1, source_target_pairs={{0,9},{1,8},{2,11},{3,10},{4,13},{5,12},{6,15},{7,14},{8,1},{9,0},... | collective-permute-start | bytes 36872 | tf_op jit(solution)/shard_map/ppermute | solution.py:292
  16.9 0.9 %collective-permute-start.6 = (s16[2,24,128]{2,1,0:T(8,128)(2,1)S(1)}, s16[2,24,128]{2,1,0:T(8,128)(2,1)S(1)}, u32[]{:S(2)}, u32[]{:S(2)}) collective-permute-start(s16[2,24,128]{2,1,0:T(8,128)(2,1)S(1)} %pad_add_fusion.3), channel_id=1, source_target_pairs={{0,5},{1,4},{2,7},{3,6},{4,1},{5,0},{6,3},{7,2},{8,13},{9,12},{10,... | collective-permute-start | bytes 36872 | tf_op jit(solution)/shard_map/ppermute | solution.py:292
  17.8 1.1 %collective-permute-done.4 = s16[2,24,128]{2,1,0:T(8,128)(2,1)S(1)} collective-permute-done((s16[2,24,128]{2,1,0:T(8,128)(2,1)S(1)}, s16[2,24,128]{2,1,0:T(8,128)(2,1)S(1)}, u32[]{:S(2)}, u32[]{:S(2)}) %collective-permute-start.4) | collective-permute-done | bytes 12320 | tf_op jit(solution)/shard_map/ppermute | solution.py:292
  18.9 0.1 collective-permute-start.7
  19.0 1.5 %collective-permute-done.5 = s16[2,24,128]{2,1,0:T(8,128)(2,1)S(1)} collective-permute-done((s16[2,24,128]{2,1,0:T(8,128)(2,1)S(1)}, s16[2,24,128]{2,1,0:T(8,128)(2,1)S(1)}, u32[]{:S(2)}, u32[]{:S(2)}) %collective-permute-start.5) | collective-permute-done | bytes 12320 | tf_op jit(solution)/shard_map/ppermute | solution.py:292
  20.5 0.0 collective-permute-done.6
  20.5 0.4 %collective-permute-start.8 = (s16[4,24,128]{2,1,0:T(8,128)(2,1)S(1)}, s16[4,24,128]{2,1,0:T(8,128)(2,1)S(1)}, u32[]{:S(2)}, u32[]{:S(2)}) collective-permute-start(s16[4,24,128]{2,1,0:T(8,128)(2,1)S(1)} %pad_add_fusion.2), channel_id=1, source_target_pairs={{0,1},{1,0},{2,3},{3,2},{4,5},{5,4},{6,7},{7,6},{8,9},{9,8},{10,11... | collective-permute-start | bytes 73736 | tf_op jit(solution)/shard_map/ppermute | solution.py:296
  21.0 0.0 collective-permute-done.7
  21.0 0.8 %collective-permute-done.8 = s16[4,24,128]{2,1,0:T(8,128)(2,1)S(1)} collective-permute-done((s16[4,24,128]{2,1,0:T(8,128)(2,1)S(1)}, s16[4,24,128]{2,1,0:T(8,128)(2,1)S(1)}, u32[]{:S(2)}, u32[]{:S(2)}) %collective-permute-start.8) | collective-permute-done | bytes 24608 | tf_op jit(solution)/shard_map/ppermute | solution.py:296
  21.8 1.3 %geocode.1 = f32[3,4,2,1024]{3,2,1,0:T(2,128)} custom-call(s16[8,24,128]{2,1,0:T(8,128)(2,1)S(1)} %constant_dynamic-update-slice_fusion.held, s16[8,24,128]{2,1,0:T(8,128)(2,1)S(1)} %pad_add_fusion.sent, bf16[256,256]{1,0:T(8,128)(2,1)S(1)} %get-tuple-element.25.band, bf16[2048,256]{1,0:T(8,128)(2,1)S(1)} %get-tuple-element.26.onehot, ...), custom_call_target="tpu_custom_call" | custom-call | flops 268435456 | bytes 2097152 | tf_op jit(solution)/shard_map/geocode/pallas_call | solution.py:274
  (15 shorter events, 0.1 us)
Async XLA Ops:
  0.0 10.5 %collective-permute-start.2 = (bf16[2,64,1024]{2,1,0:T(8,128)(2,1)}, bf16[2,64,1024]{2,1,0:T(8,128)(2,1)S(1)}, u32[]{:S(2)}, u32[]{:S(2)}) collective-permute-start(bf16[2,64,1024]{2,1,0:T(8,128)(2,1)} %bitcast.3), channel_id=1, source_target_pairs={{0,8},{2,10},{4,0},{6,2},{8,12},{10,14},{12,4},{14,6},{1,9},{3,11}... | collective-permute-start | bytes 786440 | tf_op jit(solution)/shard_map/ppermute | solution.py:346
  4.0 1.0 %copy-start = (bf16[2,1,64,1024]{3,2,1,0:T(8,128)(2,1)S(1)}, bf16[2,1,64,1024]{3,2,1,0:T(8,128)(2,1)}, u32[]{:S(2)}) copy-start(bf16[2,1,64,1024]{3,2,1,0:T(8,128)(2,1)} %param.2) | copy-start | bytes 786436
  5.0 1.6 %copy-start.2 = (s32[8,128]{1,0:T(8,128)S(1)}, s32[8,128]{1,0:T(8,128)}, u32[]{:S(2)}) copy-start(s32[8,128]{1,0:T(8,128)} %own_cells.1) | copy-start | bytes 12292
  5.0 5.1 %copy-start.1 = (bf16[2,1,64,1024]{3,2,1,0:T(8,128)(2,1)S(1)}, bf16[2,1,64,1024]{3,2,1,0:T(8,128)(2,1)}, u32[]{:S(2)}) copy-start(bf16[2,1,64,1024]{3,2,1,0:T(8,128)(2,1)} %param.2) | copy-start | bytes 786436
  5.0 5.0 %collective-permute-start = (bf16[2,32,1024]{2,1,0:T(8,128)(2,1)S(1)}, bf16[2,32,1024]{2,1,0:T(8,128)(2,1)S(1)}, u32[]{:S(2)}, u32[]{:S(2)}) collective-permute-start(bf16[2,32,1024]{2,1,0:T(8,128)(2,1)S(1)} %pick.1), channel_id=1, source_target_pairs={{0,2},{2,0},{4,6},{6,4},{8,10},{10,8},{12,14},{14,12},{1,3},{3,1},... | collective-permute-start | bytes 393224 | tf_op jit(solution)/shard_map/ppermute | solution.py:347
  6.6 1.2 %collective-permute-start.1 = (s32[8,128]{1,0:T(8,128)S(1)}, s32[8,128]{1,0:T(8,128)S(1)}, u32[]{:S(2)}, u32[]{:S(2)}) collective-permute-start(s32[8,128]{1,0:T(8,128)S(1)} %copy-done.2), channel_id=1, source_target_pairs={{0,1},{1,0},{2,3},{3,2},{4,5},{5,4},{6,7},{7,6},{8,9},{9,8},{10,11... | collective-permute-start | bytes 12296 | tf_op jit(solution)/shard_map/ppermute | solution.py:296
  10.8 3.1 %collective-permute-start.3 = (s16[1,24,128]{2,1,0:T(8,128)(2,1)S(1)}, s16[1,24,128]{2,1,0:T(8,128)(2,1)S(1)}, u32[]{:S(2)}, u32[]{:S(2)}) collective-permute-start(s16[1,24,128]{2,1,0:T(8,128)(2,1)S(1)} %bitcast.6), channel_id=1, source_target_pairs={{0,3},{1,2},{2,1},{3,0},{4,7},{5,6},{6,5},{7,4},{8,11},{9,10},{10,... | collective-permute-start | bytes 18440 | tf_op jit(solution)/shard_map/ppermute | solution.py:292
  14.0 4.9 %collective-permute-start.4 = (s16[2,24,128]{2,1,0:T(8,128)(2,1)S(1)}, s16[2,24,128]{2,1,0:T(8,128)(2,1)S(1)}, u32[]{:S(2)}, u32[]{:S(2)}) collective-permute-start(s16[2,24,128]{2,1,0:T(8,128)(2,1)S(1)} %pad_add_fusion.3), channel_id=1, source_target_pairs={{0,13},{1,12},{2,15},{3,14},{4,9},{5,8},{6,11},{7,10},{8,5},{9,4},... | collective-permute-start | bytes 36872 | tf_op jit(solution)/shard_map/ppermute | solution.py:292
  16.5 4.0 %collective-permute-start.5 = (s16[2,24,128]{2,1,0:T(8,128)(2,1)S(1)}, s16[2,24,128]{2,1,0:T(8,128)(2,1)S(1)}, u32[]{:S(2)}, u32[]{:S(2)}) collective-permute-start(s16[2,24,128]{2,1,0:T(8,128)(2,1)S(1)} %pad_add_fusion.3), channel_id=1, source_target_pairs={{0,9},{1,8},{2,11},{3,10},{4,13},{5,12},{6,15},{7,14},{8,1},{9,0},... | collective-permute-start | bytes 36872 | tf_op jit(solution)/shard_map/ppermute | solution.py:292
  16.9 3.7 %collective-permute-start.6 = (s16[2,24,128]{2,1,0:T(8,128)(2,1)S(1)}, s16[2,24,128]{2,1,0:T(8,128)(2,1)S(1)}, u32[]{:S(2)}, u32[]{:S(2)}) collective-permute-start(s16[2,24,128]{2,1,0:T(8,128)(2,1)S(1)} %pad_add_fusion.3), channel_id=1, source_target_pairs={{0,5},{1,4},{2,7},{3,6},{4,1},{5,0},{6,3},{7,2},{8,13},{9,12},{10,... | collective-permute-start | bytes 36872 | tf_op jit(solution)/shard_map/ppermute | solution.py:292
  18.9 2.1 %collective-permute-start.7 = (s16[4,24,128]{2,1,0:T(8,128)(2,1)S(1)}, s16[4,24,128]{2,1,0:T(8,128)(2,1)S(1)}, u32[]{:S(2)}, u32[]{:S(2)}) collective-permute-start(s16[4,24,128]{2,1,0:T(8,128)(2,1)S(1)} %pad_add_fusion.1), channel_id=1, source_target_pairs={{0,1},{1,0},{2,3},{3,2},{4,5},{5,4},{6,7},{7,6},{8,9},{9,8},{10,11... | collective-permute-start | bytes 73736 | tf_op jit(solution)/shard_map/ppermute | solution.py:296
  20.5 1.3 %collective-permute-start.8 = (s16[4,24,128]{2,1,0:T(8,128)(2,1)S(1)}, s16[4,24,128]{2,1,0:T(8,128)(2,1)S(1)}, u32[]{:S(2)}, u32[]{:S(2)}) collective-permute-start(s16[4,24,128]{2,1,0:T(8,128)(2,1)S(1)} %pad_add_fusion.2), channel_id=1, source_target_pairs={{0,1},{1,0},{2,3},{3,2},{4,5},{5,4},{6,7},{7,6},{8,9},{9,8},{10,11... | collective-permute-start | bytes 73736 | tf_op jit(solution)/shard_map/ppermute | solution.py:296

commit v13 on v12

--- a/solution.py
+++ b/solution.py
@@ -257,7 +257,9 @@
         both = jnp.concatenate([top, value - top], axis=0)
         rows = [both * masks[line * blocks + block : line * blocks + block + 1, :] for block in range(blocks)]
         left.append(jnp.concatenate(rows, axis=0).astype(BF16))
-    sums = dot(jnp.concatenate(left, axis=1), onehot[...])
+    middle = lines // 2
+    sums = dot(jnp.concatenate(left[:middle], axis=1), onehot[: middle * 2 * cols, :])
+    sums = sums + dot(jnp.concatenate(left[middle:], axis=1), onehot[middle * 2 * cols :, :])
     for block in range(blocks):
         start = block * 2 * planes
         total = sums[start : start + planes] + sums[start + planes : start + 2 * planes]

time: 23.3 us -> 23.3 us (level)
  no operation moved by 1% of the time
where the time goes in v13:
time: 23.3 us; the launch traced here: 23.2 us
  starting transfers between devices  10 us (43%)
  waiting for transfers between devices  9.11 us (39%)
  Pallas kernels  2.9 us (12%)
  local copies, waits for them, and re-layouts  1.02 us (4%)
    ppermute x4, waiting for transfers between devices, across(): return lax.ppermute(value, ('acq', 'rng'), pairs)  5.64 us
    ppermute x1, starting transfers between devices, per_device(): whole = lax.ppermute(own, 'acq', list(enumerate(quarter)))  4.04 us
    ppermute x4, starting transfers between devices, across(): return lax.ppermute(value, ('acq', 'rng'), pairs)  3.9 us
    ppermute x3, waiting for transfers between devices, swap(): return lax.ppermute(value, 'rng', [(0, 1), (1, 0)])  1.9 us
    ppermute x1, waiting for transfers between devices, per_device(): lax.ppermute(pick(own), 'acq', [(a, a ^ 1) for a in range(acq_count)])  1.57 us
    ppermute x1, starting transfers between devices, per_device(): lax.ppermute(pick(own), 'acq', [(a, a ^ 1) for a in range(acq_count)])  1.56 us
    pallas_call x1, Pallas kernels, geocode(): pl.pallas_call(geocode_kernel, out_shape=jax.ShapeDtypeStruct((ROUNDS, pa...  1.34 us
    unnamed x10, local copies, waits for them, and re-layouts  1.02 us
  transfers between devices with their start and end apart: 9, of which 6 were waited for; matrix products, arithmetic and copies ran while one was open for 0% of the time, Pallas kernels for 5%

profile of v13, /device:TPU:0, one launch (start us, length us, event | category | flops | bytes accessed | tf_op | source)
XLA Modules:
  0.0 23.2 jit_solution(3957322952330154038)
XLA Ops:
  0.0 4.0 %collective-permute-start.2 = (bf16[2,64,1024]{2,1,0:T(8,128)(2,1)}, bf16[2,64,1024]{2,1,0:T(8,128)(2,1)S(1)}, u32[]{:S(2)}, u32[]{:S(2)}) collective-permute-start(bf16[2,64,1024]{2,1,0:T(8,128)(2,1)} %bitcast.3), channel_id=1, source_target_pairs={{0,8},{2,10},{4,0},{6,2},{8,12},{10,14},{12,4},{14,6},{1,9},{3,11}... | collective-permute-start | bytes 786440 | tf_op jit(solution)/shard_map/ppermute | solution.py:348
  4.0 1.0 %copy-done = bf16[2,1,64,1024]{3,2,1,0:T(8,128)(2,1)S(1)} copy-done((bf16[2,1,64,1024]{3,2,1,0:T(8,128)(2,1)S(1)}, bf16[2,1,64,1024]{3,2,1,0:T(8,128)(2,1)}, u32[]{:S(2)}) %copy-start) | copy-done | bytes 262168
  5.0 1.6 %collective-permute-start = (bf16[2,32,1024]{2,1,0:T(8,128)(2,1)S(1)}, bf16[2,32,1024]{2,1,0:T(8,128)(2,1)S(1)}, u32[]{:S(2)}, u32[]{:S(2)}) collective-permute-start(bf16[2,32,1024]{2,1,0:T(8,128)(2,1)S(1)} %pick.1), channel_id=1, source_target_pairs={{0,2},{2,0},{4,6},{6,4},{8,10},{10,8},{12,14},{14,12},{1,3},{3,1},... | collective-permute-start | bytes 393224 | tf_op jit(solution)/shard_map/ppermute | solution.py:349
  6.6 0.0 collective-permute-start.1
  6.6 0.1 taking.1.take
  6.7 1.1 %collective-permute-done.1.other_cells = s32[8,128]{1,0:T(8,128)S(1)} collective-permute-done((s32[8,128]{1,0:T(8,128)S(1)}, s32[8,128]{1,0:T(8,128)S(1)}, u32[]{:S(2)}, u32[]{:S(2)}) %collective-permute-start.1) | collective-permute-done | bytes 4128 | tf_op jit(solution)/shard_map/ppermute | solution.py:298
  7.8 0.7 %select.1 = (bf16[256,256]{1,0:T(8,128)(2,1)S(1)}, bf16[2048,256]{1,0:T(8,128)(2,1)S(1)}, f32[32,256]{1,0:T(8,128)S(1)}, f32[4,256]{1,0:T(4,128)S(1)}) custom-call(s32[8,128]{1,0:T(8,128)S(1)} %copy-done.2, s32[8,128]{1,0:T(8,128)S(1)} %collective-permute-done.1.other_cells), custom_call_target="tpu_custom_call" | custom-call | flops 2097152 | bytes 1048576 | tf_op jit(solution)/shard_map/select/pallas_call | solution.py:206
  8.5 1.6 %collective-permute-done.other = bf16[2,32,1024]{2,1,0:T(8,128)(2,1)S(1)} collective-permute-done((bf16[2,32,1024]{2,1,0:T(8,128)(2,1)S(1)}, bf16[2,32,1024]{2,1,0:T(8,128)(2,1)S(1)}, u32[]{:S(2)}, u32[]{:S(2)}) %collective-permute-start) | collective-permute-done | bytes 131104 | tf_op jit(solution)/shard_map/ppermute | solution.py:349
  10.1 0.4 %first_matching.1 = (f32[8,128]{1,0:T(8,128)S(1)}, f32[8,128]{1,0:T(8,128)S(1)}, f32[2,8,8,8,128]{4,3,2,1,0:T(8,128)S(1)}) custom-call(bf16[2,64,1024]{2,1,0:T(8,128)(2,1)S(1)} %bitcast.5, bf16[2,32,1024]{2,1,0:T(8,128)(2,1)S(1)} %collective-permute-done.other, bf16[1024,128]{1,0:T(8,128)(2,1)S(1)} %taking.1.take), custom_call_target="tpu_custom_call" | custom-call | flops 2097152 | bytes 262144 | tf_op jit(solution)/shard_map/first_matching/pallas_call | solution.py:110
  10.5 0.0 collective-permute-done.2.other
  10.5 0.3 %whole_pair.1 = s16[24,128]{1,0:T(8,128)(2,1)S(1)} custom-call(f32[2,8,8,8,128]{4,3,2,1,0:T(8,128)S(1)} %get-tuple-element.22.mine, bf16[2,64,1024]{2,1,0:T(8,128)(2,1)S(1)} %collective-permute-done.2.other, bf16[1024,128]{1,0:T(8,128)(2,1)S(1)} %taking.1.take, f32[8,128]{1,0:T(8,128)S(1)} %get-tuple-element.23.power, f32[8,128]{1,0:T(8,128)S(1)} %get-tuple-element.24.first), custom_call_target="tpu_custom_call" | custom-call | flops 2097152 | bytes 262144 | tf_op jit(solution)/shard_map/whole_pair/pallas_call | solution.py:144
  10.8 0.1 collective-permute-start.3
  10.9 3.0 %collective-permute-done.3 = s16[1,24,128]{2,1,0:T(8,128)(2,1)S(1)} collective-permute-done((s16[1,24,128]{2,1,0:T(8,128)(2,1)S(1)}, s16[1,24,128]{2,1,0:T(8,128)(2,1)S(1)}, u32[]{:S(2)}, u32[]{:S(2)}) %collective-permute-start.3) | collective-permute-done | bytes 6176 | tf_op jit(solution)/shard_map/ppermute | solution.py:294
  14.0 2.5 %collective-permute-start.4 = (s16[2,24,128]{2,1,0:T(8,128)(2,1)S(1)}, s16[2,24,128]{2,1,0:T(8,128)(2,1)S(1)}, u32[]{:S(2)}, u32[]{:S(2)}) collective-permute-start(s16[2,24,128]{2,1,0:T(8,128)(2,1)S(1)} %pad_add_fusion.3), channel_id=1, source_target_pairs={{0,13},{1,12},{2,15},{3,14},{4,9},{5,8},{6,11},{7,10},{8,5},{9,4},... | collective-permute-start | bytes 36872 | tf_op jit(solution)/shard_map/ppermute | solution.py:294
  16.5 0.4 %collective-permute-start.5 = (s16[2,24,128]{2,1,0:T(8,128)(2,1)S(1)}, s16[2,24,128]{2,1,0:T(8,128)(2,1)S(1)}, u32[]{:S(2)}, u32[]{:S(2)}) collective-permute-start(s16[2,24,128]{2,1,0:T(8,128)(2,1)S(1)} %pad_add_fusion.3), channel_id=1, source_target_pairs={{0,9},{1,8},{2,11},{3,10},{4,13},{5,12},{6,15},{7,14},{8,1},{9,0},... | collective-permute-start | bytes 36872 | tf_op jit(solution)/shard_map/ppermute | solution.py:294
  16.9 0.9 %collective-permute-start.6 = (s16[2,24,128]{2,1,0:T(8,128)(2,1)S(1)}, s16[2,24,128]{2,1,0:T(8,128)(2,1)S(1)}, u32[]{:S(2)}, u32[]{:S(2)}) collective-permute-start(s16[2,24,128]{2,1,0:T(8,128)(2,1)S(1)} %pad_add_fusion.3), channel_id=1, source_target_pairs={{0,5},{1,4},{2,7},{3,6},{4,1},{5,0},{6,3},{7,2},{8,13},{9,12},{10,... | collective-permute-start | bytes 36872 | tf_op jit(solution)/shard_map/ppermute | solution.py:294
  17.8 1.1 %collective-permute-done.4 = s16[2,24,128]{2,1,0:T(8,128)(2,1)S(1)} collective-permute-done((s16[2,24,128]{2,1,0:T(8,128)(2,1)S(1)}, s16[2,24,128]{2,1,0:T(8,128)(2,1)S(1)}, u32[]{:S(2)}, u32[]{:S(2)}) %collective-permute-start.4) | collective-permute-done | bytes 12320 | tf_op jit(solution)/shard_map/ppermute | solution.py:294
  18.9 0.1 collective-permute-start.7
  19.0 1.5 %collective-permute-done.5 = s16[2,24,128]{2,1,0:T(8,128)(2,1)S(1)} collective-permute-done((s16[2,24,128]{2,1,0:T(8,128)(2,1)S(1)}, s16[2,24,128]{2,1,0:T(8,128)(2,1)S(1)}, u32[]{:S(2)}, u32[]{:S(2)}) %collective-permute-start.5) | collective-permute-done | bytes 12320 | tf_op jit(solution)/shard_map/ppermute | solution.py:294
  20.5 0.0 collective-permute-done.6
  20.5 0.4 %collective-permute-start.8 = (s16[4,24,128]{2,1,0:T(8,128)(2,1)S(1)}, s16[4,24,128]{2,1,0:T(8,128)(2,1)S(1)}, u32[]{:S(2)}, u32[]{:S(2)}) collective-permute-start(s16[4,24,128]{2,1,0:T(8,128)(2,1)S(1)} %pad_add_fusion.2), channel_id=1, source_target_pairs={{0,1},{1,0},{2,3},{3,2},{4,5},{5,4},{6,7},{7,6},{8,9},{9,8},{10,11... | collective-permute-start | bytes 73736 | tf_op jit(solution)/shard_map/ppermute | solution.py:298
  21.0 0.0 collective-permute-done.7
  21.0 0.8 %collective-permute-done.8 = s16[4,24,128]{2,1,0:T(8,128)(2,1)S(1)} collective-permute-done((s16[4,24,128]{2,1,0:T(8,128)(2,1)S(1)}, s16[4,24,128]{2,1,0:T(8,128)(2,1)S(1)}, u32[]{:S(2)}, u32[]{:S(2)}) %collective-permute-start.8) | collective-permute-done | bytes 24608 | tf_op jit(solution)/shard_map/ppermute | solution.py:298
  21.8 1.3 %geocode.1 = f32[3,4,2,1024]{3,2,1,0:T(2,128)} custom-call(s16[8,24,128]{2,1,0:T(8,128)(2,1)S(1)} %constant_dynamic-update-slice_fusion.held, s16[8,24,128]{2,1,0:T(8,128)(2,1)S(1)} %pad_add_fusion.sent, bf16[256,256]{1,0:T(8,128)(2,1)S(1)} %get-tuple-element.25.band, bf16[2048,256]{1,0:T(8,128)(2,1)S(1)} %get-tuple-element.26.onehot, ...), custom_call_target="tpu_custom_call" | custom-call | flops 268435456 | bytes 2097152 | tf_op jit(solution)/shard_map/geocode/pallas_call | solution.py:276
  (15 shorter events, 0.1 us)
Async XLA Ops:
  0.0 10.5 %collective-permute-start.2 = (bf16[2,64,1024]{2,1,0:T(8,128)(2,1)}, bf16[2,64,1024]{2,1,0:T(8,128)(2,1)S(1)}, u32[]{:S(2)}, u32[]{:S(2)}) collective-permute-start(bf16[2,64,1024]{2,1,0:T(8,128)(2,1)} %bitcast.3), channel_id=1, source_target_pairs={{0,8},{2,10},{4,0},{6,2},{8,12},{10,14},{12,4},{14,6},{1,9},{3,11}... | collective-permute-start | bytes 786440 | tf_op jit(solution)/shard_map/ppermute | solution.py:348
  4.0 1.0 %copy-start = (bf16[2,1,64,1024]{3,2,1,0:T(8,128)(2,1)S(1)}, bf16[2,1,64,1024]{3,2,1,0:T(8,128)(2,1)}, u32[]{:S(2)}) copy-start(bf16[2,1,64,1024]{3,2,1,0:T(8,128)(2,1)} %param.2) | copy-start | bytes 786436
  5.0 1.6 %copy-start.2 = (s32[8,128]{1,0:T(8,128)S(1)}, s32[8,128]{1,0:T(8,128)}, u32[]{:S(2)}) copy-start(s32[8,128]{1,0:T(8,128)} %own_cells.1) | copy-start | bytes 12292
  5.0 5.1 %copy-start.1 = (bf16[2,1,64,1024]{3,2,1,0:T(8,128)(2,1)S(1)}, bf16[2,1,64,1024]{3,2,1,0:T(8,128)(2,1)}, u32[]{:S(2)}) copy-start(bf16[2,1,64,1024]{3,2,1,0:T(8,128)(2,1)} %param.2) | copy-start | bytes 786436
  5.0 5.0 %collective-permute-start = (bf16[2,32,1024]{2,1,0:T(8,128)(2,1)S(1)}, bf16[2,32,1024]{2,1,0:T(8,128)(2,1)S(1)}, u32[]{:S(2)}, u32[]{:S(2)}) collective-permute-start(bf16[2,32,1024]{2,1,0:T(8,128)(2,1)S(1)} %pick.1), channel_id=1, source_target_pairs={{0,2},{2,0},{4,6},{6,4},{8,10},{10,8},{12,14},{14,12},{1,3},{3,1},... | collective-permute-start | bytes 393224 | tf_op jit(solution)/shard_map/ppermute | solution.py:349
  6.6 1.2 %collective-permute-start.1 = (s32[8,128]{1,0:T(8,128)S(1)}, s32[8,128]{1,0:T(8,128)S(1)}, u32[]{:S(2)}, u32[]{:S(2)}) collective-permute-start(s32[8,128]{1,0:T(8,128)S(1)} %copy-done.2), channel_id=1, source_target_pairs={{0,1},{1,0},{2,3},{3,2},{4,5},{5,4},{6,7},{7,6},{8,9},{9,8},{10,11... | collective-permute-start | bytes 12296 | tf_op jit(solution)/shard_map/ppermute | solution.py:298
  10.8 3.1 %collective-permute-start.3 = (s16[1,24,128]{2,1,0:T(8,128)(2,1)S(1)}, s16[1,24,128]{2,1,0:T(8,128)(2,1)S(1)}, u32[]{:S(2)}, u32[]{:S(2)}) collective-permute-start(s16[1,24,128]{2,1,0:T(8,128)(2,1)S(1)} %bitcast.6), channel_id=1, source_target_pairs={{0,3},{1,2},{2,1},{3,0},{4,7},{5,6},{6,5},{7,4},{8,11},{9,10},{10,... | collective-permute-start | bytes 18440 | tf_op jit(solution)/shard_map/ppermute | solution.py:294
  14.0 4.9 %collective-permute-start.4 = (s16[2,24,128]{2,1,0:T(8,128)(2,1)S(1)}, s16[2,24,128]{2,1,0:T(8,128)(2,1)S(1)}, u32[]{:S(2)}, u32[]{:S(2)}) collective-permute-start(s16[2,24,128]{2,1,0:T(8,128)(2,1)S(1)} %pad_add_fusion.3), channel_id=1, source_target_pairs={{0,13},{1,12},{2,15},{3,14},{4,9},{5,8},{6,11},{7,10},{8,5},{9,4},... | collective-permute-start | bytes 36872 | tf_op jit(solution)/shard_map/ppermute | solution.py:294
  16.5 4.0 %collective-permute-start.5 = (s16[2,24,128]{2,1,0:T(8,128)(2,1)S(1)}, s16[2,24,128]{2,1,0:T(8,128)(2,1)S(1)}, u32[]{:S(2)}, u32[]{:S(2)}) collective-permute-start(s16[2,24,128]{2,1,0:T(8,128)(2,1)S(1)} %pad_add_fusion.3), channel_id=1, source_target_pairs={{0,9},{1,8},{2,11},{3,10},{4,13},{5,12},{6,15},{7,14},{8,1},{9,0},... | collective-permute-start | bytes 36872 | tf_op jit(solution)/shard_map/ppermute | solution.py:294
  16.9 3.7 %collective-permute-start.6 = (s16[2,24,128]{2,1,0:T(8,128)(2,1)S(1)}, s16[2,24,128]{2,1,0:T(8,128)(2,1)S(1)}, u32[]{:S(2)}, u32[]{:S(2)}) collective-permute-start(s16[2,24,128]{2,1,0:T(8,128)(2,1)S(1)} %pad_add_fusion.3), channel_id=1, source_target_pairs={{0,5},{1,4},{2,7},{3,6},{4,1},{5,0},{6,3},{7,2},{8,13},{9,12},{10,... | collective-permute-start | bytes 36872 | tf_op jit(solution)/shard_map/ppermute | solution.py:294
  18.9 2.1 %collective-permute-start.7 = (s16[4,24,128]{2,1,0:T(8,128)(2,1)S(1)}, s16[4,24,128]{2,1,0:T(8,128)(2,1)S(1)}, u32[]{:S(2)}, u32[]{:S(2)}) collective-permute-start(s16[4,24,128]{2,1,0:T(8,128)(2,1)S(1)} %pad_add_fusion.1), channel_id=1, source_target_pairs={{0,1},{1,0},{2,3},{3,2},{4,5},{5,4},{6,7},{7,6},{8,9},{9,8},{10,11... | collective-permute-start | bytes 73736 | tf_op jit(solution)/shard_map/ppermute | solution.py:298
  20.5 1.3 %collective-permute-start.8 = (s16[4,24,128]{2,1,0:T(8,128)(2,1)S(1)}, s16[4,24,128]{2,1,0:T(8,128)(2,1)S(1)}, u32[]{:S(2)}, u32[]{:S(2)}) collective-permute-start(s16[4,24,128]{2,1,0:T(8,128)(2,1)S(1)} %pad_add_fusion.2), channel_id=1, source_target_pairs={{0,1},{1,0},{2,3},{3,2},{4,5},{5,4},{6,7},{7,6},{8,9},{9,8},{10,11... | collective-permute-start | bytes 73736 | tf_op jit(solution)/shard_map/ppermute | solution.py:298

commit v14 on v12

--- a/solution.py
+++ b/solution.py
@@ -12,7 +12,7 @@
 HALF_W = 4
 ROUNDS = 3
 BLOCK = 2**ROUNDS
-STEPS = ((1,), (6, 4, 2))
+STEPS = ((4,), (3, 2, 1))
 SEND = (2, 0, 3, 1)
 WHOLE = ((1, 0), (2, 2), (2, 0), (1, 2))
 MAPC = 16384

time: 23.3 us -> 23.4 us (level)
    ppermute x4, starting transfers between devices: 3.9 us -> 4.28 us  [across(): return lax.ppermute(value, ('acq', 'rng'), pairs)]
    ppermute x4, waiting for transfers between devices: 5.64 us -> 5.33 us  [across(): return lax.ppermute(value, ('acq', 'rng'), pairs)]
  transfers between devices with their start and end apart: 9 -> 9, of which waited for: 6 -> 7; matrix products, arithmetic and copies ran while one was open for 0% -> 0% of each run, Pallas kernels for 5% -> 5%
where the time goes in v14:
time: 23.4 us; the launch traced here: 23.2 us
  starting transfers between devices  10.2 us (44%)
  waiting for transfers between devices  9 us (38%)
  Pallas kernels  2.9 us (12%)
  local copies, waits for them, and re-layouts  1.02 us (4%)
    ppermute x4, waiting for transfers between devices, across(): return lax.ppermute(value, ('acq', 'rng'), pairs)  5.33 us
    ppermute x4, starting transfers between devices, across(): return lax.ppermute(value, ('acq', 'rng'), pairs)  4.28 us
    ppermute x1, starting transfers between devices, per_device(): whole = lax.ppermute(own, 'acq', list(enumerate(quarter)))  4.04 us
    ppermute x3, waiting for transfers between devices, swap(): return lax.ppermute(value, 'rng', [(0, 1), (1, 0)])  2.09 us
    ppermute x1, waiting for transfers between devices, per_device(): lax.ppermute(pick(own), 'acq', [(a, a ^ 1) for a in range(acq_count)])  1.57 us
    ppermute x1, starting transfers between devices, per_device(): lax.ppermute(pick(own), 'acq', [(a, a ^ 1) for a in range(acq_count)])  1.56 us
    pallas_call x1, Pallas kernels, geocode(): pl.pallas_call(geocode_kernel, out_shape=jax.ShapeDtypeStruct((ROUNDS, pa...  1.34 us
    unnamed x10, local copies, waits for them, and re-layouts  1.02 us
  transfers between devices with their start and end apart: 9, of which 7 were waited for; matrix products, arithmetic and copies ran while one was open for 0% of the time, Pallas kernels for 5%

profile of v14, /device:TPU:0, one launch (start us, length us, event | category | flops | bytes accessed | tf_op | source)
XLA Modules:
  0.0 23.2 jit_solution(2718618029126779127)
XLA Ops:
  0.0 4.0 %collective-permute-start.2 = (bf16[2,64,1024]{2,1,0:T(8,128)(2,1)}, bf16[2,64,1024]{2,1,0:T(8,128)(2,1)S(1)}, u32[]{:S(2)}, u32[]{:S(2)}) collective-permute-start(bf16[2,64,1024]{2,1,0:T(8,128)(2,1)} %bitcast.3), channel_id=1, source_target_pairs={{0,8},{2,10},{4,0},{6,2},{8,12},{10,14},{12,4},{14,6},{1,9},{3,11}... | collective-permute-start | bytes 786440 | tf_op jit(solution)/shard_map/ppermute | solution.py:346
  4.0 1.0 %copy-done = bf16[2,1,64,1024]{3,2,1,0:T(8,128)(2,1)S(1)} copy-done((bf16[2,1,64,1024]{3,2,1,0:T(8,128)(2,1)S(1)}, bf16[2,1,64,1024]{3,2,1,0:T(8,128)(2,1)}, u32[]{:S(2)}) %copy-start) | copy-done | bytes 262168
  5.0 1.6 %collective-permute-start = (bf16[2,32,1024]{2,1,0:T(8,128)(2,1)S(1)}, bf16[2,32,1024]{2,1,0:T(8,128)(2,1)S(1)}, u32[]{:S(2)}, u32[]{:S(2)}) collective-permute-start(bf16[2,32,1024]{2,1,0:T(8,128)(2,1)S(1)} %pick.1), channel_id=1, source_target_pairs={{0,2},{2,0},{4,6},{6,4},{8,10},{10,8},{12,14},{14,12},{1,3},{3,1},... | collective-permute-start | bytes 393224 | tf_op jit(solution)/shard_map/ppermute | solution.py:347
  6.6 0.0 collective-permute-start.1
  6.6 0.1 taking.1.take
  6.7 1.1 %collective-permute-done.1.other_cells = s32[8,128]{1,0:T(8,128)S(1)} collective-permute-done((s32[8,128]{1,0:T(8,128)S(1)}, s32[8,128]{1,0:T(8,128)S(1)}, u32[]{:S(2)}, u32[]{:S(2)}) %collective-permute-start.1) | collective-permute-done | bytes 4128 | tf_op jit(solution)/shard_map/ppermute | solution.py:296
  7.8 0.7 %select.1 = (bf16[256,256]{1,0:T(8,128)(2,1)S(1)}, bf16[2048,256]{1,0:T(8,128)(2,1)S(1)}, f32[32,256]{1,0:T(8,128)S(1)}, f32[4,256]{1,0:T(4,128)S(1)}) custom-call(s32[8,128]{1,0:T(8,128)S(1)} %copy-done.2, s32[8,128]{1,0:T(8,128)S(1)} %collective-permute-done.1.other_cells), custom_call_target="tpu_custom_call" | custom-call | flops 2097152 | bytes 1048576 | tf_op jit(solution)/shard_map/select/pallas_call | solution.py:206
  8.5 1.6 %collective-permute-done.other = bf16[2,32,1024]{2,1,0:T(8,128)(2,1)S(1)} collective-permute-done((bf16[2,32,1024]{2,1,0:T(8,128)(2,1)S(1)}, bf16[2,32,1024]{2,1,0:T(8,128)(2,1)S(1)}, u32[]{:S(2)}, u32[]{:S(2)}) %collective-permute-start) | collective-permute-done | bytes 131104 | tf_op jit(solution)/shard_map/ppermute | solution.py:347
  10.1 0.4 %first_matching.1 = (f32[8,128]{1,0:T(8,128)S(1)}, f32[8,128]{1,0:T(8,128)S(1)}, f32[2,8,8,8,128]{4,3,2,1,0:T(8,128)S(1)}) custom-call(bf16[2,64,1024]{2,1,0:T(8,128)(2,1)S(1)} %bitcast.5, bf16[2,32,1024]{2,1,0:T(8,128)(2,1)S(1)} %collective-permute-done.other, bf16[1024,128]{1,0:T(8,128)(2,1)S(1)} %taking.1.take), custom_call_target="tpu_custom_call" | custom-call | flops 2097152 | bytes 262144 | tf_op jit(solution)/shard_map/first_matching/pallas_call | solution.py:110
  10.5 0.0 collective-permute-done.2.other
  10.5 0.3 %whole_pair.1 = s16[24,128]{1,0:T(8,128)(2,1)S(1)} custom-call(f32[2,8,8,8,128]{4,3,2,1,0:T(8,128)S(1)} %get-tuple-element.22.mine, bf16[2,64,1024]{2,1,0:T(8,128)(2,1)S(1)} %collective-permute-done.2.other, bf16[1024,128]{1,0:T(8,128)(2,1)S(1)} %taking.1.take, f32[8,128]{1,0:T(8,128)S(1)} %get-tuple-element.23.power, f32[8,128]{1,0:T(8,128)S(1)} %get-tuple-element.24.first), custom_call_target="tpu_custom_call" | custom-call | flops 2097152 | bytes 262144 | tf_op jit(solution)/shard_map/whole_pair/pallas_call | solution.py:144
  10.8 1.3 %collective-permute-start.3 = (s16[1,24,128]{2,1,0:T(8,128)(2,1)S(1)}, s16[1,24,128]{2,1,0:T(8,128)(2,1)S(1)}, u32[]{:S(2)}, u32[]{:S(2)}) collective-permute-start(s16[1,24,128]{2,1,0:T(8,128)(2,1)S(1)} %bitcast.6), channel_id=1, source_target_pairs={{0,9},{1,8},{2,11},{3,10},{4,13},{5,12},{6,15},{7,14},{8,1},{9,0},... | collective-permute-start | bytes 18440 | tf_op jit(solution)/shard_map/ppermute | solution.py:292
  12.2 2.7 %collective-permute-done.3 = s16[1,24,128]{2,1,0:T(8,128)(2,1)S(1)} collective-permute-done((s16[1,24,128]{2,1,0:T(8,128)(2,1)S(1)}, s16[1,24,128]{2,1,0:T(8,128)(2,1)S(1)}, u32[]{:S(2)}, u32[]{:S(2)}) %collective-permute-start.3) | collective-permute-done | bytes 6176 | tf_op jit(solution)/shard_map/ppermute | solution.py:292
  14.9 1.4 %collective-permute-start.4 = (s16[2,24,128]{2,1,0:T(8,128)(2,1)S(1)}, s16[2,24,128]{2,1,0:T(8,128)(2,1)S(1)}, u32[]{:S(2)}, u32[]{:S(2)}) collective-permute-start(s16[2,24,128]{2,1,0:T(8,128)(2,1)S(1)} %pad_add_fusion.3), channel_id=1, source_target_pairs={{0,7},{1,6},{2,5},{3,4},{4,3},{5,2},{6,1},{7,0},{8,15},{9,14},{10,... | collective-permute-start | bytes 36872 | tf_op jit(solution)/shard_map/ppermute | solution.py:292
  16.2 1.3 %collective-permute-start.5 = (s16[2,24,128]{2,1,0:T(8,128)(2,1)S(1)}, s16[2,24,128]{2,1,0:T(8,128)(2,1)S(1)}, u32[]{:S(2)}, u32[]{:S(2)}) collective-permute-start(s16[2,24,128]{2,1,0:T(8,128)(2,1)S(1)} %pad_add_fusion.3), channel_id=1, source_target_pairs={{0,5},{1,4},{2,7},{3,6},{4,1},{5,0},{6,3},{7,2},{8,13},{9,12},{10,... | collective-permute-start | bytes 36872 | tf_op jit(solution)/shard_map/ppermute | solution.py:292
  17.5 0.3 %collective-permute-start.6 = (s16[2,24,128]{2,1,0:T(8,128)(2,1)S(1)}, s16[2,24,128]{2,1,0:T(8,128)(2,1)S(1)}, u32[]{:S(2)}, u32[]{:S(2)}) collective-permute-start(s16[2,24,128]{2,1,0:T(8,128)(2,1)S(1)} %pad_add_fusion.3), channel_id=1, source_target_pairs={{0,3},{1,2},{2,1},{3,0},{4,7},{5,6},{6,5},{7,4},{8,11},{9,10},{10,... | collective-permute-start | bytes 36872 | tf_op jit(solution)/shard_map/ppermute | solution.py:292
  17.8 1.0 %collective-permute-done.4 = s16[2,24,128]{2,1,0:T(8,128)(2,1)S(1)} collective-permute-done((s16[2,24,128]{2,1,0:T(8,128)(2,1)S(1)}, s16[2,24,128]{2,1,0:T(8,128)(2,1)S(1)}, u32[]{:S(2)}, u32[]{:S(2)}) %collective-permute-start.4) | collective-permute-done | bytes 12320 | tf_op jit(solution)/shard_map/ppermute | solution.py:292
  18.9 0.2 collective-permute-start.7
  19.1 0.3 %collective-permute-done.5 = s16[2,24,128]{2,1,0:T(8,128)(2,1)S(1)} collective-permute-done((s16[2,24,128]{2,1,0:T(8,128)(2,1)S(1)}, s16[2,24,128]{2,1,0:T(8,128)(2,1)S(1)}, u32[]{:S(2)}, u32[]{:S(2)}) %collective-permute-start.5) | collective-permute-done | bytes 12320 | tf_op jit(solution)/shard_map/ppermute | solution.py:292
  19.4 1.3 %collective-permute-done.6 = s16[2,24,128]{2,1,0:T(8,128)(2,1)S(1)} collective-permute-done((s16[2,24,128]{2,1,0:T(8,128)(2,1)S(1)}, s16[2,24,128]{2,1,0:T(8,128)(2,1)S(1)}, u32[]{:S(2)}, u32[]{:S(2)}) %collective-permute-start.6) | collective-permute-done | bytes 12320 | tf_op jit(solution)/shard_map/ppermute | solution.py:292
  20.7 0.2 collective-permute-start.8
  20.8 0.0 collective-permute-done.7
  20.9 1.0 %collective-permute-done.8 = s16[4,24,128]{2,1,0:T(8,128)(2,1)S(1)} collective-permute-done((s16[4,24,128]{2,1,0:T(8,128)(2,1)S(1)}, s16[4,24,128]{2,1,0:T(8,128)(2,1)S(1)}, u32[]{:S(2)}, u32[]{:S(2)}) %collective-permute-start.8) | collective-permute-done | bytes 24608 | tf_op jit(solution)/shard_map/ppermute | solution.py:296
  21.9 1.3 %geocode.1 = f32[3,4,2,1024]{3,2,1,0:T(2,128)} custom-call(s16[8,24,128]{2,1,0:T(8,128)(2,1)S(1)} %constant_dynamic-update-slice_fusion.held, s16[8,24,128]{2,1,0:T(8,128)(2,1)S(1)} %pad_add_fusion.sent, bf16[256,256]{1,0:T(8,128)(2,1)S(1)} %get-tuple-element.25.band, bf16[2048,256]{1,0:T(8,128)(2,1)S(1)} %get-tuple-element.26.onehot, ...), custom_call_target="tpu_custom_call" | custom-call | flops 268435456 | bytes 2097152 | tf_op jit(solution)/shard_map/geocode/pallas_call | solution.py:274
  (15 shorter events, 0.1 us)
Async XLA Ops:
  0.0 10.5 %collective-permute-start.2 = (bf16[2,64,1024]{2,1,0:T(8,128)(2,1)}, bf16[2,64,1024]{2,1,0:T(8,128)(2,1)S(1)}, u32[]{:S(2)}, u32[]{:S(2)}) collective-permute-start(bf16[2,64,1024]{2,1,0:T(8,128)(2,1)} %bitcast.3), channel_id=1, source_target_pairs={{0,8},{2,10},{4,0},{6,2},{8,12},{10,14},{12,4},{14,6},{1,9},{3,11}... | collective-permute-start | bytes 786440 | tf_op jit(solution)/shard_map/ppermute | solution.py:346
  4.0 1.0 %copy-start = (bf16[2,1,64,1024]{3,2,1,0:T(8,128)(2,1)S(1)}, bf16[2,1,64,1024]{3,2,1,0:T(8,128)(2,1)}, u32[]{:S(2)}) copy-start(bf16[2,1,64,1024]{3,2,1,0:T(8,128)(2,1)} %param.2) | copy-start | bytes 786436
  5.0 1.6 %copy-start.2 = (s32[8,128]{1,0:T(8,128)S(1)}, s32[8,128]{1,0:T(8,128)}, u32[]{:S(2)}) copy-start(s32[8,128]{1,0:T(8,128)} %own_cells.1) | copy-start | bytes 12292
  5.0 5.1 %copy-start.1 = (bf16[2,1,64,1024]{3,2,1,0:T(8,128)(2,1)S(1)}, bf16[2,1,64,1024]{3,2,1,0:T(8,128)(2,1)}, u32[]{:S(2)}) copy-start(bf16[2,1,64,1024]{3,2,1,0:T(8,128)(2,1)} %param.2) | copy-start | bytes 786436
  5.0 5.0 %collective-permute-start = (bf16[2,32,1024]{2,1,0:T(8,128)(2,1)S(1)}, bf16[2,32,1024]{2,1,0:T(8,128)(2,1)S(1)}, u32[]{:S(2)}, u32[]{:S(2)}) collective-permute-start(bf16[2,32,1024]{2,1,0:T(8,128)(2,1)S(1)} %pick.1), channel_id=1, source_target_pairs={{0,2},{2,0},{4,6},{6,4},{8,10},{10,8},{12,14},{14,12},{1,3},{3,1},... | collective-permute-start | bytes 393224 | tf_op jit(solution)/shard_map/ppermute | solution.py:347
  6.6 1.2 %collective-permute-start.1 = (s32[8,128]{1,0:T(8,128)S(1)}, s32[8,128]{1,0:T(8,128)S(1)}, u32[]{:S(2)}, u32[]{:S(2)}) collective-permute-start(s32[8,128]{1,0:T(8,128)S(1)} %copy-done.2), channel_id=1, source_target_pairs={{0,1},{1,0},{2,3},{3,2},{4,5},{5,4},{6,7},{7,6},{8,9},{9,8},{10,11... | collective-permute-start | bytes 12296 | tf_op jit(solution)/shard_map/ppermute | solution.py:296
  10.8 4.0 %collective-permute-start.3 = (s16[1,24,128]{2,1,0:T(8,128)(2,1)S(1)}, s16[1,24,128]{2,1,0:T(8,128)(2,1)S(1)}, u32[]{:S(2)}, u32[]{:S(2)}) collective-permute-start(s16[1,24,128]{2,1,0:T(8,128)(2,1)S(1)} %bitcast.6), channel_id=1, source_target_pairs={{0,9},{1,8},{2,11},{3,10},{4,13},{5,12},{6,15},{7,14},{8,1},{9,0},... | collective-permute-start | bytes 18440 | tf_op jit(solution)/shard_map/ppermute | solution.py:292
  14.9 4.0 %collective-permute-start.4 = (s16[2,24,128]{2,1,0:T(8,128)(2,1)S(1)}, s16[2,24,128]{2,1,0:T(8,128)(2,1)S(1)}, u32[]{:S(2)}, u32[]{:S(2)}) collective-permute-start(s16[2,24,128]{2,1,0:T(8,128)(2,1)S(1)} %pad_add_fusion.3), channel_id=1, source_target_pairs={{0,7},{1,6},{2,5},{3,4},{4,3},{5,2},{6,1},{7,0},{8,15},{9,14},{10,... | collective-permute-start | bytes 36872 | tf_op jit(solution)/shard_map/ppermute | solution.py:292
  16.2 3.1 %collective-permute-start.5 = (s16[2,24,128]{2,1,0:T(8,128)(2,1)S(1)}, s16[2,24,128]{2,1,0:T(8,128)(2,1)S(1)}, u32[]{:S(2)}, u32[]{:S(2)}) collective-permute-start(s16[2,24,128]{2,1,0:T(8,128)(2,1)S(1)} %pad_add_fusion.3), channel_id=1, source_target_pairs={{0,5},{1,4},{2,7},{3,6},{4,1},{5,0},{6,3},{7,2},{8,13},{9,12},{10,... | collective-permute-start | bytes 36872 | tf_op jit(solution)/shard_map/ppermute | solution.py:292
  17.5 3.1 %collective-permute-start.6 = (s16[2,24,128]{2,1,0:T(8,128)(2,1)S(1)}, s16[2,24,128]{2,1,0:T(8,128)(2,1)S(1)}, u32[]{:S(2)}, u32[]{:S(2)}) collective-permute-start(s16[2,24,128]{2,1,0:T(8,128)(2,1)S(1)} %pad_add_fusion.3), channel_id=1, source_target_pairs={{0,3},{1,2},{2,1},{3,0},{4,7},{5,6},{6,5},{7,4},{8,11},{9,10},{10,... | collective-permute-start | bytes 36872 | tf_op jit(solution)/shard_map/ppermute | solution.py:292
  18.9 2.0 %collective-permute-start.7 = (s16[4,24,128]{2,1,0:T(8,128)(2,1)S(1)}, s16[4,24,128]{2,1,0:T(8,128)(2,1)S(1)}, u32[]{:S(2)}, u32[]{:S(2)}) collective-permute-start(s16[4,24,128]{2,1,0:T(8,128)(2,1)S(1)} %pad_add_fusion.1), channel_id=1, source_target_pairs={{0,1},{1,0},{2,3},{3,2},{4,5},{5,4},{6,7},{7,6},{8,9},{9,8},{10,11... | collective-permute-start | bytes 73736 | tf_op jit(solution)/shard_map/ppermute | solution.py:296
  20.7 1.2 %collective-permute-start.8 = (s16[4,24,128]{2,1,0:T(8,128)(2,1)S(1)}, s16[4,24,128]{2,1,0:T(8,128)(2,1)S(1)}, u32[]{:S(2)}, u32[]{:S(2)}) collective-permute-start(s16[4,24,128]{2,1,0:T(8,128)(2,1)S(1)} %pad_add_fusion.2), channel_id=1, source_target_pairs={{0,1},{1,0},{2,3},{3,2},{4,5},{5,4},{6,7},{7,6},{8,9},{9,8},{10,11... | collective-permute-start | bytes 73736 | tf_op jit(solution)/shard_map/ppermute | solution.py:296
